TPU v7x, 256 devices: a whole 4x4x8 slice. The times are simulated.
256 devices in a mesh: pair: 16 (over z, x_lo), side: 2 (over core), tp: 8 (over x_hi, y).
Axes of the slice: x: 4 (x_hi: 2, x_lo: 2; x = x_hi * 2 + x_lo), y: 4, z: 8, core: 2. Of those that a mesh axis runs over, the one named last changes fastest.
Arguments:
- token_ids: int32 [768], P(('side', 'tp')), may hold values from 0 to 76031
- embed_table: bfloat16 [76032, 8192], P(('side', 'tp'), 'pair'), may hold values from -6 to 6
- norm_gain: float32 [2, 8192], P(None, 'pair'), may hold values from 0.25 to 1.75
- w_gate: bfloat16 [2, 8192, 16384], P(None, 'pair', ('side', 'tp')), may hold values from -0.0625 to 0.0625
- w_up: bfloat16 [2, 8192, 16384], P(None, 'pair', ('side', 'tp')), may hold values from -0.0625 to 0.0625
- gate_scale: float32 [2, 16384], P(None, ('side', 'tp')), may hold values from 0.5 to 2
- up_scale: float32 [2, 16384], P(None, ('side', 'tp')), may hold values from 0.5 to 2
- w_down: bfloat16 [2, 16384, 8192], P(None, ('side', 'tp'), 'pair'), may hold values from -0.046875 to 0.046875
- down_scale: float32 [2, 8192], P(None, 'pair'), may hold values from 0.5 to 2
Outputs:
- hidden: bfloat16 [768, 8192], P(('side', 'tp'), 'pair')
All inputs are finite; a program needn't handle non-finite values.
Results may differ from a plain program's by a relative error of at most 0.039.
Values may be sent and summed in bfloat16 or wider, within the bound.
No kernel may reach another device: no remote copies, remote signals or barrier semaphores. Data moves between devices by JAX's collectives and lax.ppermute only.
A program may use at most 64 MiB of HBM per device.

v0:
```python
import jax
import jax.numpy as jnp
from jax import lax
from jax.sharding import PartitionSpec as P

LAYERS = 2


def per_device(
    token_ids, embed_table, norm_gain, w_gate, w_up, gate_scale, up_scale, w_down, down_scale
):
    all_ids = lax.all_gather(token_ids, ("side", "tp"), axis=0, tiled=True)
    vocab_rows = embed_table.shape[0]
    local_ids = all_ids - lax.axis_index(("side", "tp")) * vocab_rows
    inside = (local_ids >= 0) & (local_ids < vocab_rows)
    picked = jnp.take(embed_table, jnp.clip(local_ids, 0, vocab_rows - 1), axis=0)
    picked = jnp.where(inside[:, None], picked.astype(jnp.float32), 0.0)
    x = lax.psum_scatter(
        picked.astype(jnp.bfloat16), ("side", "tp"), scatter_dimension=0, tiled=True
    )
    width_total = x.shape[1] * lax.axis_size("pair")
    hidden_width = w_gate.shape[2]
    for layer in range(LAYERS):
        xf = x.astype(jnp.float32)
        squares = lax.psum(jnp.sum(xf * xf, axis=1), "pair")
        inverse = lax.rsqrt(squares / width_total + 1e-05)
        normed = (xf * inverse[:, None] * norm_gain[layer][None, :]).astype(jnp.bfloat16)
        all_rows = lax.all_gather(normed, ("side", "tp"), axis=0, tiled=True)
        gate_w = w_gate[layer]
        up_w = w_up[layer]
        down_w = w_down[layer]
        summed = lax.psum_scatter(
            jnp.concatenate(
                [
                    jnp.dot(all_rows, gate_w, preferred_element_type=jnp.float32),
                    jnp.dot(all_rows, up_w, preferred_element_type=jnp.float32),
                ],
                axis=1,
            ).astype(jnp.bfloat16),
            "pair",
            scatter_dimension=0,
            tiled=True,
        ).astype(jnp.float32)
        gate = summed[:, :hidden_width] * gate_scale[layer][None, :]
        up = summed[:, hidden_width:] * up_scale[layer][None, :]
        act = (jax.nn.silu(gate) * up).astype(jnp.bfloat16)
        terms = jnp.dot(
            lax.all_gather(act, "pair", axis=0, tiled=True),
            down_w,
            preferred_element_type=jnp.float32,
        )
        update = lax.psum_scatter(
            terms.astype(jnp.bfloat16), ("side", "tp"), scatter_dimension=0, tiled=True
        ).astype(jnp.float32)
        x = (xf + update * down_scale[layer][None, :]).astype(jnp.bfloat16)
    return x


def solution(mesh):
    in_specs = (
        P(("side", "tp")),
        P(("side", "tp"), "pair"),
        P(None, "pair"),
        P(None, "pair", ("side", "tp")),
        P(None, "pair", ("side", "tp")),
        P(None, ("side", "tp")),
        P(None, ("side", "tp")),
        P(None, ("side", "tp"), "pair"),
        P(None, "pair"),
    )
    out_specs = P(("side", "tp"), "pair")
    return jax.shard_map(
        per_device, mesh=mesh, in_specs=in_specs, out_specs=out_specs, check_vma=False
    )
```

profile of v0, /device:TPU:2, one launch (start us, length us, event | category | flops | bytes accessed | tf_op | source)
XLA Modules:
  0.0 731.7 jit_solution(10152894789927466124)
XLA Ops:
  6.5 1.3 dynamic-slice
  8.5 0.9 dynamic-update-slice
  9.3 13.6 %all-reduce = s32[768]{0:T(1024)S(1)} all-reduce(s32[768]{0:T(1024)S(1)} %dynamic-update-slice), channel_id=1, replica_groups=mesh['pair'=16,'side'=2,'tp'=8] {'side','tp'}, use_global_device_ids=true, to_apply=%add | all-reduce | flops 768 | bytes 6144
  22.9 5.7 gather_fusion
  28.7 1.2 select_convert_fusion
  29.9 0.0 reduce-scatter.6.cloned.1.call-update
  29.9 0.0 reduce-scatter.8.cloned.1.call-start
  30.0 72.9 %reduce-scatter.6.cloned.1.call-done = bf16[48,512]{1,0:T(8,128)(2,1)} async-done(((bf16[768,512]{1,0:T(8,128)(2,1)}), bf16[48,512]{1,0:T(8,128)(2,1)}) %reduce-scatter.6.cloned.1.call-update) | async-done | bytes 49168 | tf_op jit(solution)/shard_map/reduce_scatter | solution.py:18
  102.9 0.9 fusion.16
  103.8 32.5 %psum.14 = f32[48]{0:T(128)S(1)} all-reduce(f32[48]{0:T(128)S(1)} %fusion.16), channel_id=1, replica_groups=mesh['pair'=16,'side'=2,'tp'=8] {'pair'}, use_global_device_ids=true, to_apply=%region_2.3 | all-reduce | flops 48 | bytes 384 | tf_op jit(solution)/shard_map/psum | solution.py:25
  136.2 0.9 fusion.18
  137.1 39.2 %all_gather.16 = bf16[768,512]{1,0:T(8,128)(2,1)S(1)} all-gather(bf16[48,512]{1,0:T(8,128)(2,1)S(1)} %fusion.18), channel_id=1, replica_groups=mesh['pair'=16,'side'=2,'tp'=8] {'side','tp'}, dimensions={0}, use_global_device_ids=true | all-gather | bytes 835584 | tf_op jit(solution)/shard_map/all_gather | solution.py:28
  176.3 1.0 convolution_convert_fusion.2
  177.3 0.6 copy-done.6
  177.9 1.0 convolution_convert_fusion.3
  178.9 1.9 pad_maximum_fusion
  180.9 0.0 all-gather.3.cloned.1.call-start
  180.9 0.6 copy-done.1
  181.6 82.3 %reduce-scatter.8.cloned.1.call-done = bf16[48,2048]{1,0:T(8,128)(2,1)} async-done(((bf16[768,2048]{1,0:T(8,128)(2,1)}), bf16[48,2048]{1,0:T(8,128)(2,1)}) %reduce-scatter.8.cloned.1.call-update) | async-done | bytes 196624 | tf_op jit(solution)/shard_map/reduce_scatter | solution.py:32
  263.9 1.0 convert_element_type.54
  264.8 0.7 fusion.15
  265.5 0.0 all-gather.3.cloned.1.call-update
  265.6 0.0 reduce-scatter.10.cloned.1.call-start
  265.6 70.0 %all-gather.3.cloned.1.call-done = bf16[768,1024]{1,0:T(8,128)(2,1)} async-done(((bf16[48,1024]{1,0:T(8,128)(2,1)}), bf16[768,1024]{1,0:T(8,128)(2,1)}) %all-gather.3.cloned.1.call-update) | async-done | bytes 1572880 | tf_op jit(solution)/shard_map/all_gather | solution.py:48
  335.6 3.6 convolution_convert_fusion.5
  339.2 0.0 reduce-scatter.10.cloned.1.call-update
  339.2 0.0 reduce-scatter.12.cloned.1.call-start
  339.3 74.4 %reduce-scatter.10.cloned.1.call-done = bf16[48,512]{1,0:T(8,128)(2,1)} async-done(((bf16[768,512]{1,0:T(8,128)(2,1)}), bf16[48,512]{1,0:T(8,128)(2,1)}) %reduce-scatter.10.cloned.1.call-update) | async-done | bytes 49168 | tf_op jit(solution)/shard_map/reduce_scatter | solution.py:52
  413.7 0.9 fusion.20
  414.6 32.5 %psum.15 = f32[48]{0:T(128)S(1)} all-reduce(f32[48]{0:T(128)S(1)} %get-tuple-element.5), channel_id=1, replica_groups=mesh['pair'=16,'side'=2,'tp'=8] {'pair'}, use_global_device_ids=true, to_apply=%region_6.7 | all-reduce | flops 48 | bytes 384 | tf_op jit(solution)/shard_map/psum | solution.py:25
  447.1 0.1 fusion.22
  447.2 39.2 %all_gather.18 = bf16[768,512]{1,0:T(8,128)(2,1)S(1)} all-gather(bf16[48,512]{1,0:T(8,128)(2,1)S(1)} %fusion.22), channel_id=1, replica_groups=mesh['pair'=16,'side'=2,'tp'=8] {'side','tp'}, dimensions={0}, use_global_device_ids=true | all-gather | bytes 835584 | tf_op jit(solution)/shard_map/all_gather | solution.py:28
  486.3 1.0 convolution_convert_fusion
  487.3 0.6 copy-done.7
  487.9 1.0 convolution_convert_fusion.1
  488.9 1.9 pad_maximum_fusion.1
  490.9 0.0 reduce-scatter.12.cloned.1.call-update
  490.9 0.0 all-gather.5.cloned.1.call-start
  490.9 83.3 %reduce-scatter.12.cloned.1.call-done = bf16[48,2048]{1,0:T(8,128)(2,1)} async-done(((bf16[768,2048]{1,0:T(8,128)(2,1)}), bf16[48,2048]{1,0:T(8,128)(2,1)}) %reduce-scatter.12.cloned.1.call-update) | async-done | bytes 196624 | tf_op jit(solution)/shard_map/reduce_scatter | solution.py:32
  574.2 1.0 convert_element_type.61
  575.2 0.7 fusion.13
  575.9 0.0 all-gather.5.cloned.1.call-update
  575.9 0.0 reduce-scatter.14.cloned.1.call-start
  576.0 69.8 %all-gather.5.cloned.1.call-done = bf16[768,1024]{1,0:T(8,128)(2,1)} async-done(((bf16[48,1024]{1,0:T(8,128)(2,1)}), bf16[768,1024]{1,0:T(8,128)(2,1)}) %all-gather.5.cloned.1.call-update) | async-done | bytes 1572880 | tf_op jit(solution)/shard_map/all_gather | solution.py:48
  645.8 3.3 convolution_convert_fusion.4
  649.1 0.0 reduce-scatter.14.cloned.1.call-update
  649.1 74.3 %reduce-scatter.14.cloned.1.call-done = bf16[48,512]{1,0:T(8,128)(2,1)} async-done(((bf16[768,512]{1,0:T(8,128)(2,1)}), bf16[48,512]{1,0:T(8,128)(2,1)}) %reduce-scatter.14.cloned.1.call-update) | async-done | bytes 49168 | tf_op jit(solution)/shard_map/reduce_scatter | solution.py:52
  723.4 1.4 fusion.23
  (26 shorter events, 0.1 us)
Async XLA Ops:
  6.5 96.3 %reduce-scatter.6.cloned.1.call-start = ((), (), s32[]{:S(2)}) async-start(), calls=%async_computation.5 | async-start | bytes 835584 | tf_op jit(solution)/shard_map/reduce_scatter | solution.py:18
  28.7 1.3 copy-start.3
  28.7 147.6 %copy-start.5 = (bf16[2,512,1024]{2,1,0:T(8,128)(2,1)S(1)}, bf16[2,512,1024]{2,1,0:T(8,128)(2,1)}, u32[]{:S(2)}) copy-start(bf16[2,512,1024]{2,1,0:T(8,128)(2,1)} %param.13) | copy-start | bytes 6291460
  29.9 234.0 %reduce-scatter.8.cloned.1.call-start = ((), (), s32[]{:S(2)}) async-start(), calls=%async_computation.6 | async-start | bytes 3342336 | tf_op jit(solution)/shard_map/reduce_scatter | solution.py:32
  176.3 1.6 copy-start.6
  180.8 0.7 copy-start.1
  180.8 0.7 copy-start.2
  180.9 154.8 %all-gather.3.cloned.1.call-start = ((), (), s32[]{:S(2)}) async-start(), calls=%async_computation.7 | async-start | bytes 1671168 | tf_op jit(solution)/shard_map/all_gather | solution.py:48
  265.6 73.7 %copy-start.4 = (f32[2,512]{1,0:T(2,128)S(1)}, f32[2,512]{1,0:T(2,128)}, u32[]{:S(2)}) copy-start(f32[2,512]{1,0:T(2,128)} %param.17) | copy-start | bytes 12292
  265.6 148.1 %copy-start = (bf16[48,512]{1,0:T(8,128)(2,1)S(1)}, bf16[48,512]{1,0:T(8,128)(2,1)}, u32[]{:S(2)}) copy-start(bf16[48,512]{1,0:T(8,128)(2,1)} %reduce-scatter.6.cloned.1.call-done) | copy-start | bytes 147460
  265.6 148.1 %reduce-scatter.10.cloned.1.call-start = ((), (), s32[]{:S(2)}) async-start(), calls=%async_computation.8 | async-start | bytes 835584 | tf_op jit(solution)/shard_map/reduce_scatter | solution.py:52
  339.2 235.0 %reduce-scatter.12.cloned.1.call-start = ((), (), s32[]{:S(2)}) async-start(), calls=%async_computation.9 | async-start | bytes 3342336 | tf_op jit(solution)/shard_map/reduce_scatter | solution.py:32
  486.3 1.6 copy-start.7
  490.9 154.9 %copy-start.8 = (bf16[2,1024,512]{2,1,0:T(8,128)(2,1)S(1)}, bf16[2,1024,512]{2,1,0:T(8,128)(2,1)}, u32[]{:S(2)}) copy-start(bf16[2,1024,512]{2,1,0:T(8,128)(2,1)} %param.16) | copy-start | bytes 6291460
  490.9 154.9 %all-gather.5.cloned.1.call-start = ((), (), s32[]{:S(2)}) async-start(), calls=%async_computation.10 | async-start | bytes 1671168 | tf_op jit(solution)/shard_map/all_gather | solution.py:48
  575.9 147.5 %reduce-scatter.14.cloned.1.call-start = ((), (), s32[]{:S(2)}) async-start(), calls=%async_computation.11 | async-start | bytes 835584 | tf_op jit(solution)/shard_map/reduce_scatter | solution.py:52
Sparse Core Ops, SparseCore 0:
  30.0 72.8 reduce-scatter.5
  181.0 82.8 reduce-scatter.7
  265.8 69.8 all-gather.2
  340.1 73.4 reduce-scatter.9
  491.0 83.1 reduce-scatter.11
  576.1 69.6 all-gather.4
  649.9 73.4 reduce-scatter.13
where the time goes:
time: 733 us; the launch traced here: 732 us
  waiting for transfers between devices  527 us (72%)
  blocking collectives  157 us (21%)
  between operations  14.3 us (2%)
  other arithmetic  12.7 us (2%)
  matrix products  10.8 us (1%)
  local copies, waits for them, and re-layouts  9.7 us (1%)
    reduce_scatter x2, waiting for transfers between devices, per_device(): lax.psum_scatter(jnp.concatenate([jnp.dot(all_rows, gate_w, preferred_ele...  166 us
    reduce_scatter x2, waiting for transfers between devices, per_device(): lax.psum_scatter(terms.astype(jnp.bfloat16), ('side', 'tp'), scatter_dime...  149 us
    all_gather x2, waiting for transfers between devices, per_device(): lax.all_gather(act, 'pair', axis=0, tiled=True)  140 us
    all_gather x2, blocking collectives, per_device(): all_rows = lax.all_gather(normed, ('side', 'tp'), axis=0, tiled=True)  78.4 us
    reduce_scatter x1, waiting for transfers between devices, per_device(): lax.psum_scatter(picked.astype(jnp.bfloat16), ('side', 'tp'), scatter_dim...  72.9 us
    psum x2, blocking collectives, per_device(): squares = lax.psum(jnp.sum(xf * xf, axis=1), 'pair')  64.9 us
  transfers between devices with their start and end apart: 7, of which 7 were waited for; matrix products, arithmetic and copies ran while one was open for 0% of the time, Pallas kernels for 0%

commit v1 on v0

v1 whole, which is shorter than its diff:
```python
import jax
import jax.numpy as jnp
from jax import lax
from jax.sharding import Mesh, PartitionSpec as P

LAYERS = 2
BF, F32 = jnp.bfloat16, jnp.float32
AXES = ("z", "xl", "c", "xh", "y")
SIZES = (8, 2, 2, 2, 4)
Z = SIZES[0]
PLANE = ("xl", "xh", "y")
OWNERS = ("c", "xh", "y")


def turn(n, by):
    return [(i, (i + by) % n) for i in range(n)]


def swap(value, axis):
    return lax.ppermute(value, axis, turn(2, 1))


def add(*terms):
    return sum(t.astype(F32) for t in terms)


def scatter_sum_z(parts):
    z = lax.axis_index("z")

    def block(offset):
        return lax.dynamic_index_in_dim(parts, lax.rem(z + offset + Z, Z), 0, keepdims=False)

    down = lax.ppermute(block(-4), "z", turn(Z, -1))
    up = None
    for far in (3, 2, 1):
        down = add(down, block(-far)).astype(BF)
        up = block(far) if up is None else add(up, block(far)).astype(BF)
        down = lax.ppermute(down, "z", turn(Z, -1))
        up = lax.ppermute(up, "z", turn(Z, 1))
    return add(down, up, block(0))


def gather_plane(x):
    n = SIZES[1] * SIZES[3] * SIZES[4]
    sent = jnp.broadcast_to(x[None], (n, *x.shape))
    got = lax.all_to_all(sent, PLANE, 0, 0, tiled=True)
    return got.reshape(SIZES[1], -1, x.shape[1])


def two_halves(value, axis, mine):
    half = value.shape[axis] // 2
    return (
        lax.dynamic_slice_in_dim(value, mine * half, half, axis),
        lax.dynamic_slice_in_dim(value, (1 - mine) * half, half, axis),
    )


def spread_weights(gate, up, down, xl):
    g_mine, g_other = two_halves(gate, 1, xl)
    u_mine, u_other = two_halves(up, 1, xl)
    gu_mine = jnp.concatenate([g_mine, u_mine], axis=1)
    gu_got = swap(jnp.concatenate([g_other, u_other], axis=1), "xl")
    first = xl == 0
    gu = jnp.concatenate([jnp.where(first, gu_mine, gu_got), jnp.where(first, gu_got, gu_mine)], axis=0)
    d_mine, d_other = two_halves(down, 0, xl)
    d_got = swap(d_other, "xl")
    d = jnp.concatenate([jnp.where(first, d_mine, d_got), jnp.where(first, d_got, d_mine)], axis=1)
    gu_sib = swap(gu, "c")
    d_sib = swap(d, "c")
    return (gu, gu_sib), (d, d_sib)


def per_device(
    token_ids, embed_table, norm_gain, w_gate, w_up, gate_scale, up_scale, w_down, down_scale
):
    xl = lax.axis_index("xl")
    owner = lax.axis_index(OWNERS)
    width = norm_gain.shape[1]
    width_total = width * SIZES[0] * SIZES[1]
    rows = token_ids.shape[0]
    own_tokens = rows * SIZES[3] * SIZES[4]

    n_owners = SIZES[2] * SIZES[3] * SIZES[4]
    all_ids = lax.all_to_all(
        jnp.broadcast_to(token_ids[None], (n_owners, rows)), OWNERS, 0, 0, tiled=True
    ).reshape(-1)
    vocab_rows = embed_table.shape[0]
    local_ids = all_ids - owner * vocab_rows
    inside = (local_ids >= 0) & (local_ids < vocab_rows)
    picked = jnp.take(embed_table, jnp.clip(local_ids, 0, vocab_rows - 1), axis=0)
    picked = jnp.where(inside[:, None], picked, jnp.zeros((), BF))

    spread = [None] * LAYERS
    spread[0] = spread_weights(w_gate[0], w_up[0], w_down[0], xl)
    gain_got = swap(norm_gain, "xl")
    gains = jnp.where(
        xl == 0, jnp.stack([norm_gain, gain_got], 1), jnp.stack([gain_got, norm_gain], 1)
    )
    scales = jnp.stack([two_halves(gate_scale, 1, xl)[0], two_halves(up_scale, 1, xl)[0]], 1)
    scales = jnp.stack([scales, swap(scales, "c")], 1)

    pieces = lax.all_to_all(picked, OWNERS, 0, 0, tiled=True).reshape(n_owners, rows, width)
    x = jnp.sum(pieces.astype(F32), axis=0).astype(BF)

    for layer in range(LAYERS):
        everyone = gather_plane(x)
        if layer + 1 < LAYERS:
            later = (w_gate[layer + 1], w_up[layer + 1], w_down[layer + 1], everyone)
            *later, everyone = lax.optimization_barrier(later)
            spread[layer + 1] = spread_weights(*later, xl)
        (gu, gu_sib), (d, d_sib) = spread[layer]
        ef = everyone.astype(F32)
        normed = (ef * gains[layer][:, None, :]).astype(BF)
        normed = jnp.concatenate([normed[0], normed[1]], axis=1)
        squares = jnp.sum((ef * ef).reshape(2, own_tokens, -1, 128), axis=(0, 2))
        parts = jnp.concatenate(
            [
                jnp.dot(normed, gu, preferred_element_type=F32).astype(BF),
                jnp.dot(normed, gu_sib, preferred_element_type=F32).astype(BF),
                squares.astype(BF),
            ],
            axis=1,
        )
        summed = scatter_sum_z(parts.reshape(Z, own_tokens // Z, -1))
        units = gu.shape[1] // 2
        inverse = lax.rsqrt(
            jnp.sum(summed[:, 4 * units :], axis=1, keepdims=True) / width_total + 1e-05
        )
        act = []
        for core in range(2):
            at = 2 * core * units
            gate = summed[:, at : at + units] * inverse * scales[layer, core, 0][None, :]
            up = summed[:, at + units : at + 2 * units] * inverse * scales[layer, core, 1][None, :]
            act.append((jax.nn.silu(gate) * up).astype(BF))
        act = lax.all_gather(jnp.concatenate(act, axis=1), "z", axis=0, tiled=True)
        weights = jnp.concatenate([d, d_sib], axis=0)
        terms = jnp.dot(act, weights, preferred_element_type=F32).astype(BF)
        terms = jnp.concatenate([terms[:, :width], terms[:, width:]], axis=0)
        got = lax.all_to_all(terms, PLANE, 0, 0, tiled=True).reshape(-1, rows, width)
        update = jnp.sum(got.astype(F32), axis=0)
        x = (x.astype(F32) + update * down_scale[layer][None, :]).astype(BF)
    return x


def solution(mesh):
    cut = Mesh(mesh.devices.reshape(SIZES), AXES)
    pair, owners = ("z", "xl"), OWNERS
    in_specs = (
        P(owners),
        P(owners, pair),
        P(None, pair),
        P(None, pair, owners),
        P(None, pair, owners),
        P(None, owners),
        P(None, owners),
        P(None, owners, pair),
        P(None, pair),
    )
    return jax.shard_map(
        per_device, mesh=cut, in_specs=in_specs, out_specs=P(owners, pair), check_vma=False
    )
```

time: 733 us -> 279 us (0.38)
  waiting for transfers between devices: 527 us -> 88.7 us
  blocking collectives: 157 us -> 66.5 us
  starting transfers between devices: 0.25 us -> 59.2 us
  local copies, waits for them, and re-layouts: 9.7 us -> 28.4 us
  between operations: 14.3 us -> 0.57 us
  other arithmetic: 12.7 us -> 24.6 us
    reduce_scatter x5 -> x0, waiting for transfers between devices: 387 us -> none  [the longest x2 166 us: per_device(): lax.psum_scatter(jnp.concatenate([jnp.dot(all_rows, gate_w, preferred_ele...]
    all_gather x2 -> x0, waiting for transfers between devices: 140 us -> none  [per_device(): lax.all_gather(act, 'pair', axis=0, tiled=True)]
    psum x2 -> x0, blocking collectives: 64.9 us -> none  [per_device(): squares = lax.psum(jnp.sum(xf * xf, axis=1), 'pair')]
    all_to_all x0 -> x5, waiting for transfers between devices: none -> 53.5 us  [the longest x1 21.1 us: per_device(): lax.all_to_all(jnp.broadcast_to(token_ids[None], (n_owners, rows)), OWNER...]
    ppermute x0 -> x24, waiting for transfers between devices: none -> 35.2 us  [the longest x6 16.5 us: scatter_sum_z(): down = lax.ppermute(down, 'z', turn(Z, -1))]
    ppermute x0 -> x24, starting transfers between devices: none -> 33.6 us  [the longest x6 13.4 us: scatter_sum_z(): down = lax.ppermute(down, 'z', turn(Z, -1))]
    all_gather x2, blocking collectives: 78.4 us -> 52.1 us  [per_device(): act = lax.all_gather(jnp.concatenate(act, axis=1), 'z', axis=0, tiled=True)]
    all_to_all x0 -> x5, starting transfers between devices: none -> 25.5 us  [the longest x2 10.8 us: gather_plane(): got = lax.all_to_all(sent, PLANE, 0, 0, tiled=True)]
  transfers between devices with their start and end apart: 7 -> 29, of which waited for: 7 -> 16; matrix products, arithmetic and copies ran while one was open for 0% -> 17% of each run, Pallas kernels for 0% -> 0%
where the time goes in v1:
time: 279 us; the launch traced here: 278 us
  waiting for transfers between devices  88.7 us (32%)
  blocking collectives  66.5 us (24%)
  starting transfers between devices  59.2 us (21%)
  local copies, waits for them, and re-layouts  28.4 us (10%)
  other arithmetic  24.6 us (9%)
  matrix products  10.3 us (4%)
    all_gather x2, blocking collectives, per_device(): act = lax.all_gather(jnp.concatenate(act, axis=1), 'z', axis=0, tiled=True)  52.1 us
    all_to_all x1, waiting for transfers between devices, per_device(): lax.all_to_all(jnp.broadcast_to(token_ids[None], (n_owners, rows)), OWNER...  21.1 us
    all_to_all x2, waiting for transfers between devices, gather_plane(): got = lax.all_to_all(sent, PLANE, 0, 0, tiled=True)  18.9 us
    ppermute x6, waiting for transfers between devices, scatter_sum_z(): down = lax.ppermute(down, 'z', turn(Z, -1))  16.5 us
    all_to_all x1, blocking collectives, per_device(): lax.all_to_all(terms, PLANE, 0, 0, tiled=True).reshape(-1, rows, width)  14.3 us
    ppermute x6, starting transfers between devices, scatter_sum_z(): down = lax.ppermute(down, 'z', turn(Z, -1))  13.4 us
    all_to_all x2, starting transfers between devices, gather_plane(): got = lax.all_to_all(sent, PLANE, 0, 0, tiled=True)  10.8 us
    ppermute x6, waiting for transfers between devices, scatter_sum_z(): up = lax.ppermute(up, 'z', turn(Z, 1))  9.78 us
  transfers between devices with their start and end apart: 29, of which 16 were waited for; matrix products, arithmetic and copies ran while one was open for 17% of the time, Pallas kernels for 0%

profile of v1, /device:TPU:2, one launch (start us, length us, event | category | flops | bytes accessed | tf_op | source)
XLA Modules:
  0.0 278.3 jit_solution(11521356591764416514)
XLA Ops:
  0.0 1.9 fusion.58
  3.4 2.4 dynamic-slice_bitcast_fusion.3
  6.9 2.3 collective-permute-start.1
  9.8 4.7 %all-to-all-start = ((s32[16,1,48]{2,1,0:T(1,128)}), s32[16,1,48]{2,1,0:T(1,128)S(1)}, u32[]{:S(2)}, u32[]{:S(2)}) async-start(s32[16,1,48]{2,1,0:T(1,128)} %broadcast_in_dim.28), calls=%async_computation | async-start | bytes 16384 | tf_op jit(solution)/shard_map/all_to_all | solution.py:84
  14.5 21.1 %all-to-all-done = s32[16,1,48]{2,1,0:T(1,128)S(1)} async-done(((s32[16,1,48]{2,1,0:T(1,128)}), s32[16,1,48]{2,1,0:T(1,128)S(1)}, u32[]{:S(2)}, u32[]{:S(2)}) %all-to-all-start) | async-done | bytes 3104 | tf_op jit(solution)/shard_map/all_to_all | solution.py:84
  35.7 5.7 %gather_fusion = bf16[768,512]{1,0:T(8,128)(2,1)S(1)} fusion(bf16[4752,512]{1,0:T(8,128)(2,1)} %param.10, s32[1024]{0:T(1024)S(1)} %pad_clamp_fusion), kind=kCustom, calls=%fused_computation | custom fusion | bytes 1575936 | tf_op jit(solution)/shard_map/jit(_take)/gather | solution.py:90
  42.6 4.3 %all-to-all-start.1 = ((bf16[16,48,512]{2,1,0:T(8,128)(2,1)}), bf16[16,48,512]{2,1,0:T(8,128)(2,1)}, u32[]{:S(2)}, u32[]{:S(2)}) async-start(bf16[16,48,512]{2,1,0:T(8,128)(2,1)} %select_select_fusion), calls=%async_computation.1 | async-start | bytes 1572864 | tf_op jit(solution)/shard_map/all_to_all | solution.py:102
  46.9 1.9 broadcast_select_fusion.3
  49.9 1.6 pad_maximum_fusion
  51.8 1.8 collective-permute-start
  53.7 8.2 %all-to-all-done.1 = bf16[16,48,512]{2,1,0:T(8,128)(2,1)} async-done(((bf16[16,48,512]{2,1,0:T(8,128)(2,1)}), bf16[16,48,512]{2,1,0:T(8,128)(2,1)}, u32[]{:S(2)}, u32[]{:S(2)}) %all-to-all-start.1) | async-done | bytes 786464 | tf_op jit(solution)/shard_map/all_to_all | solution.py:102
  64.1 5.9 %all-to-all-start.2 = ((bf16[16,48,512]{2,1,0:T(8,128)(2,1)}), bf16[16,48,512]{2,1,0:T(8,128)(2,1)}, u32[]{:S(2)}, u32[]{:S(2)}) async-start(bf16[16,48,512]{2,1,0:T(8,128)(2,1)} %broadcast_in_dim.48), calls=%async_computation.2 | async-start | bytes 1572864 | tf_op jit(solution)/shard_map/all_to_all | solution.py:46
  70.0 2.7 fusion.57
  74.8 8.6 %all-to-all-done.2 = bf16[16,48,512]{2,1,0:T(8,128)(2,1)} async-done(((bf16[16,48,512]{2,1,0:T(8,128)(2,1)}), bf16[16,48,512]{2,1,0:T(8,128)(2,1)}, u32[]{:S(2)}, u32[]{:S(2)}) %all-to-all-start.2) | async-done | bytes 786464 | tf_op jit(solution)/shard_map/all_to_all | solution.py:46
  83.3 3.2 %fusion.12 = (bf16[2,384,512]{2,1,0:T(8,128)(2,1)}, f32[384,512]{1,0:T(8,128)}) fusion(bf16[2,384,512]{2,1,0:T(8,128)(2,1)} %bitcast.7, f32[2,512]{1,0:T(2,128)S(1)} %bitcast.136), kind=kLoop, calls=%fused_computation.19 | loop fusion | flops 1769472 | bytes 2363392 | tf_op jit(solution)/shard_map/convert_element_type | solution.py:113
  86.5 2.4 reduce_sum.75
  88.9 1.6 reduce_sum.76
  91.7 2.2 convolution_convert_fusion.3
  93.9 2.6 convolution_convert_fusion.2
  96.6 5.9 %collective-permute-start.3 = (bf16[48,2176]{1,0:T(8,128)(2,1)S(1)}, bf16[48,2176]{1,0:T(8,128)(2,1)S(1)}, u32[]{:S(2)}, u32[]{:S(2)}) collective-permute-start(bf16[48,2176]{1,0:T(8,128)(2,1)S(1)} %get-tuple-element.35), channel_id=1, source_target_pairs={{0,224},{32,0},{64,32},{96,64},{128,96},{160,128},{192,160},{224,1... | collective-permute-start | bytes 626696 | tf_op jit(solution)/shard_map/ppermute | solution.py:33
  102.7 3.2 %collective-permute-done.3 = bf16[48,2176]{1,0:T(8,128)(2,1)S(1)} collective-permute-done((bf16[48,2176]{1,0:T(8,128)(2,1)S(1)}, bf16[48,2176]{1,0:T(8,128)(2,1)S(1)}, u32[]{:S(2)}, u32[]{:S(2)}) %collective-permute-start.3) | collective-permute-done | bytes 208928 | tf_op jit(solution)/shard_map/ppermute | solution.py:33
  106.0 4.0 %collective-permute-start.4 = (bf16[48,2176]{1,0:T(8,128)(2,1)S(1)}, bf16[48,2176]{1,0:T(8,128)(2,1)S(1)}, u32[]{:S(2)}, u32[]{:S(2)}) collective-permute-start(bf16[48,2176]{1,0:T(8,128)(2,1)S(1)} %fusion.30), channel_id=1, source_target_pairs={{0,224},{32,0},{64,32},{96,64},{128,96},{160,128},{192,160},{224,1... | collective-permute-start | bytes 626696 | tf_op jit(solution)/shard_map/ppermute | solution.py:38
  109.9 3.3 %collective-permute-done.4 = bf16[48,2176]{1,0:T(8,128)(2,1)S(1)} collective-permute-done((bf16[48,2176]{1,0:T(8,128)(2,1)S(1)}, bf16[48,2176]{1,0:T(8,128)(2,1)S(1)}, u32[]{:S(2)}, u32[]{:S(2)}) %collective-permute-start.4) | collective-permute-done | bytes 208928 | tf_op jit(solution)/shard_map/ppermute | solution.py:38
  113.3 3.8 %collective-permute-start.5 = (bf16[48,2176]{1,0:T(8,128)(2,1)S(1)}, bf16[48,2176]{1,0:T(8,128)(2,1)S(1)}, u32[]{:S(2)}, u32[]{:S(2)}) collective-permute-start(bf16[48,2176]{1,0:T(8,128)(2,1)S(1)} %get-tuple-element.33), channel_id=1, source_target_pairs={{0,224},{32,0},{64,32},{96,64},{128,96},{160,128},{192,160},{224,1... | collective-permute-start | bytes 626696 | tf_op jit(solution)/shard_map/ppermute | solution.py:38
  118.6 1.8 collective-permute-done.5
  120.4 3.7 %collective-permute-done.8 = bf16[48,2176]{1,0:T(8,128)(2,1)S(1)} collective-permute-done((bf16[48,2176]{1,0:T(8,128)(2,1)S(1)}, bf16[48,2176]{1,0:T(8,128)(2,1)S(1)}, u32[]{:S(2)}, u32[]{:S(2)}) %collective-permute-start.8) | collective-permute-done | bytes 208928 | tf_op jit(solution)/shard_map/ppermute | solution.py:39
  124.3 2.0 collective-permute-start.9
  128.7 1.5 collective-permute-start.13
  131.8 26.2 %all_gather.6 = bf16[384,1024]{1,0:T(8,128)(2,1)S(1)} all-gather(bf16[48,1024]{1,0:T(8,128)(2,1)S(1)} %pad_maximum_fusion.18), channel_id=1, replica_groups=mesh['z'=8,'xl'=2,'c'=2,'xh'=2,'y'=4] {'z'}, dimensions={0}, use_global_device_ids=true | all-gather | bytes 884736 | tf_op jit(solution)/shard_map/all_gather | solution.py:135
  160.0 5.8 %all-to-all-start.3 = ((bf16[16,48,512]{2,1,0:T(8,128)(2,1)}), bf16[16,48,512]{2,1,0:T(8,128)(2,1)S(1)}, u32[]{:S(2)}, u32[]{:S(2)}) async-start(bf16[16,48,512]{2,1,0:T(8,128)(2,1)} %bitcast.35), calls=%async_computation.3 | async-start | bytes 1572864 | tf_op jit(solution)/shard_map/all_to_all | solution.py:139
  166.9 1.6 broadcast_select_fusion.1
  168.5 1.7 pad_maximum_fusion.1
  170.2 5.3 %all-to-all-done.3 = bf16[16,48,512]{2,1,0:T(8,128)(2,1)S(1)} async-done(((bf16[16,48,512]{2,1,0:T(8,128)(2,1)}), bf16[16,48,512]{2,1,0:T(8,128)(2,1)S(1)}, u32[]{:S(2)}, u32[]{:S(2)}) %all-to-all-start.3) | async-done | bytes 786464 | tf_op jit(solution)/shard_map/all_to_all | solution.py:139
  176.6 4.9 %all-to-all-start.4 = ((bf16[16,48,512]{2,1,0:T(8,128)(2,1)}), bf16[16,48,512]{2,1,0:T(8,128)(2,1)S(1)}, u32[]{:S(2)}, u32[]{:S(2)}) async-start(bf16[16,48,512]{2,1,0:T(8,128)(2,1)} %broadcast_in_dim.49), calls=%async_computation.4 | async-start | bytes 1572864 | tf_op jit(solution)/shard_map/all_to_all | solution.py:46
  181.5 10.3 %all-to-all-done.4 = bf16[16,48,512]{2,1,0:T(8,128)(2,1)S(1)} async-done(((bf16[16,48,512]{2,1,0:T(8,128)(2,1)}), bf16[16,48,512]{2,1,0:T(8,128)(2,1)S(1)}, u32[]{:S(2)}, u32[]{:S(2)}) %all-to-all-start.4) | async-done | bytes 786464 | tf_op jit(solution)/shard_map/all_to_all | solution.py:46
  193.3 1.8 mul.275
  198.9 2.6 convolution_convert_fusion
  204.0 5.6 %collective-permute-done.15 = bf16[48,2176]{1,0:T(8,128)(2,1)S(1)} collective-permute-done((bf16[48,2176]{1,0:T(8,128)(2,1)S(1)}, bf16[48,2176]{1,0:T(8,128)(2,1)S(1)}, u32[]{:S(2)}, u32[]{:S(2)}) %collective-permute-start.15) | collective-permute-done | bytes 208928 | tf_op jit(solution)/shard_map/ppermute | solution.py:33
  209.7 1.6 collective-permute-start.16
  211.3 5.4 %collective-permute-done.16 = bf16[48,2176]{1,0:T(8,128)(2,1)S(1)} collective-permute-done((bf16[48,2176]{1,0:T(8,128)(2,1)S(1)}, bf16[48,2176]{1,0:T(8,128)(2,1)S(1)}, u32[]{:S(2)}, u32[]{:S(2)}) %collective-permute-start.16) | collective-permute-done | bytes 208928 | tf_op jit(solution)/shard_map/ppermute | solution.py:38
  216.8 3.6 %collective-permute-start.17 = (bf16[48,2176]{1,0:T(8,128)(2,1)S(1)}, bf16[48,2176]{1,0:T(8,128)(2,1)S(1)}, u32[]{:S(2)}, u32[]{:S(2)}) collective-permute-start(bf16[48,2176]{1,0:T(8,128)(2,1)S(1)} %get-tuple-element.27), channel_id=1, source_target_pairs={{0,224},{32,0},{64,32},{96,64},{128,96},{160,128},{192,160},{224,1... | collective-permute-start | bytes 626696 | tf_op jit(solution)/shard_map/ppermute | solution.py:38
  220.5 1.7 collective-permute-start.22
  222.2 2.7 collective-permute-done.17
  224.9 3.4 %collective-permute-done.20 = bf16[48,2176]{1,0:T(8,128)(2,1)S(1)} collective-permute-done((bf16[48,2176]{1,0:T(8,128)(2,1)S(1)}, bf16[48,2176]{1,0:T(8,128)(2,1)S(1)}, u32[]{:S(2)}, u32[]{:S(2)}) %collective-permute-start.20) | collective-permute-done | bytes 208928 | tf_op jit(solution)/shard_map/ppermute | solution.py:39
  228.8 1.7 collective-permute-start.21
  231.0 3.3 %collective-permute-done.18 = bf16[48,2176]{1,0:T(8,128)(2,1)S(1)} collective-permute-done((bf16[48,2176]{1,0:T(8,128)(2,1)S(1)}, bf16[48,2176]{1,0:T(8,128)(2,1)S(1)}, u32[]{:S(2)}, u32[]{:S(2)}) %collective-permute-start.18) | collective-permute-done | bytes 208928 | tf_op jit(solution)/shard_map/ppermute | solution.py:38
  236.1 25.9 %all_gather.7 = bf16[384,1024]{1,0:T(8,128)(2,1)S(1)} all-gather(bf16[48,1024]{1,0:T(8,128)(2,1)S(1)} %pad_maximum_fusion.19), channel_id=1, replica_groups=mesh['z'=8,'xl'=2,'c'=2,'xh'=2,'y'=4] {'z'}, dimensions={0}, use_global_device_ids=true | all-gather | bytes 884736 | tf_op jit(solution)/shard_map/all_gather | solution.py:135
  263.2 14.3 %all_to_all.40 = bf16[16,48,512]{2,1,0:T(8,128)(2,1)S(1)} all-to-all(bf16[16,48,512]{2,1,0:T(8,128)(2,1)S(1)} %bitcast.132), channel_id=1, replica_groups=mesh['z'=8,'xl'=2,'c'=2,'xh'=2,'y'=4] {'xl','xh','y'}, dimensions={0} | all-to-all | bytes 1572864 | tf_op jit(solution)/shard_map/all_to_all | solution.py:139
  (126 shorter events, 34.0 us)
Async XLA Ops:
  0.0 2.2 copy-start.8
  5.8 3.4 %copy-start.15 = (s32[48]{0:T(128)S(1)}, s32[48]{0:T(128)}, u32[]{:S(2)}) copy-start(s32[48]{0:T(128)} %param.9) | copy-start | bytes 580
  6.9 40.0 %collective-permute-start.1 = (bf16[512,1024]{1,0:T(8,128)(2,1)}, bf16[512,1024]{1,0:T(8,128)(2,1)}, u32[]{:S(2)}, u32[]{:S(2)}) collective-permute-start(bf16[512,1024]{1,0:T(8,128)(2,1)} %pad_maximum_fusion.5), channel_id=1, source_target_pairs={{0,16},{16,0},{1,17},{17,1},{2,18},{18,2},{3,19},{19,3},{4,20},{20... | collective-permute-start | bytes 3145736 | tf_op jit(solution)/shard_map/ppermute | solution.py:20
  9.8 25.8 %all-to-all-start = ((s32[16,1,48]{2,1,0:T(1,128)}), s32[16,1,48]{2,1,0:T(1,128)S(1)}, u32[]{:S(2)}, u32[]{:S(2)}) async-start(s32[16,1,48]{2,1,0:T(1,128)} %broadcast_in_dim.28), calls=%async_computation | async-start | bytes 16384 | tf_op jit(solution)/shard_map/all_to_all | solution.py:84
  42.6 19.3 %all-to-all-start.1 = ((bf16[16,48,512]{2,1,0:T(8,128)(2,1)}), bf16[16,48,512]{2,1,0:T(8,128)(2,1)}, u32[]{:S(2)}, u32[]{:S(2)}) async-start(bf16[16,48,512]{2,1,0:T(8,128)(2,1)} %select_select_fusion), calls=%async_computation.1 | async-start | bytes 1572864 | tf_op jit(solution)/shard_map/all_to_all | solution.py:102
  48.9 1.0 copy-start
  49.9 1.9 copy-start.12
  49.9 3.7 %copy-start.13 = (f32[2,1024]{1,0:T(2,128)S(1)}, f32[2,1024]{1,0:T(2,128)}, u32[]{:S(2)}) copy-start(f32[2,1024]{1,0:T(2,128)} %param.14) | copy-start | bytes 24580
  49.9 3.7 %copy-start.14 = (f32[2,1024]{1,0:T(2,128)S(1)}, f32[2,1024]{1,0:T(2,128)}, u32[]{:S(2)}) copy-start(f32[2,1024]{1,0:T(2,128)} %param.15) | copy-start | bytes 24580
  51.5 42.4 %collective-permute-start.2 = (bf16[1024,1024]{1,0:T(8,128)(2,1)}, bf16[1024,1024]{1,0:T(8,128)(2,1)}, u32[]{:S(2)}, u32[]{:S(2)}) collective-permute-start(bf16[1024,1024]{1,0:T(8,128)(2,1)} %pad_maximum_fusion), channel_id=1, source_target_pairs={{0,8},{8,0},{1,9},{9,1},{2,10},{10,2},{3,11},{11,3},{4,12},{12,4},... | collective-permute-start | bytes 6291464 | tf_op jit(solution)/shard_map/ppermute | solution.py:20
  51.8 23.0 %collective-permute-start = (f32[2,512]{1,0:T(2,128)S(1)}, f32[2,512]{1,0:T(2,128)S(1)}, u32[]{:S(2)}, u32[]{:S(2)}) collective-permute-start(f32[2,512]{1,0:T(2,128)S(1)} %copy-done.12), channel_id=1, source_target_pairs={{0,16},{16,0},{1,17},{17,1},{2,18},{18,2},{3,19},{19,3},{4,20},{20... | collective-permute-start | bytes 12296 | tf_op jit(solution)/shard_map/ppermute | solution.py:20
  53.6 56.3 %collective-permute-start.10 = (f32[2,2,512]{2,0,1:T(2,128)S(1)}, f32[2,2,512]{2,0,1:T(2,128)S(1)}, u32[]{:S(2)}, u32[]{:S(2)}) collective-permute-start(f32[2,2,512]{2,0,1:T(2,128)S(1)} %get-tuple-element.74), channel_id=1, source_target_pairs={{0,8},{8,0},{1,9},{9,1},{2,10},{10,2},{3,11},{11,3},{4,12},{12,4},... | collective-permute-start | bytes 24584 | tf_op jit(solution)/shard_map/ppermute | solution.py:20
  64.1 19.3 %all-to-all-start.2 = ((bf16[16,48,512]{2,1,0:T(8,128)(2,1)}), bf16[16,48,512]{2,1,0:T(8,128)(2,1)}, u32[]{:S(2)}, u32[]{:S(2)}) async-start(bf16[16,48,512]{2,1,0:T(8,128)(2,1)} %broadcast_in_dim.48), calls=%async_computation.2 | async-start | bytes 1572864 | tf_op jit(solution)/shard_map/all_to_all | solution.py:46
  72.6 1.0 copy-start.4
  74.5 42.6 %collective-permute-start.11 = (bf16[512,512]{1,0:T(8,128)(2,1)}, bf16[512,512]{1,0:T(8,128)(2,1)}, u32[]{:S(2)}, u32[]{:S(2)}) collective-permute-start(bf16[512,512]{1,0:T(8,128)(2,1)} %dynamic-slice_bitcast_fusion), channel_id=1, source_target_pairs={{0,16},{16,0},{1,17},{17,1},{2,18},{18,2},{3,19},{19,3},{4,20},{20... | collective-permute-start | bytes 1572872 | tf_op jit(solution)/shard_map/ppermute | solution.py:20
  96.6 20.5 %copy-start.5 = (bf16[1,1024,512]{2,1,0:T(8,128)(2,1)S(1)}, bf16[1,1024,512]{2,1,0:T(8,128)(2,1)}, u32[]{:S(2)}) copy-start(bf16[1,1024,512]{2,1,0:T(8,128)(2,1)} %copy-done.4) | copy-start | bytes 3145732
  96.6 9.3 %collective-permute-start.3 = (bf16[48,2176]{1,0:T(8,128)(2,1)S(1)}, bf16[48,2176]{1,0:T(8,128)(2,1)S(1)}, u32[]{:S(2)}, u32[]{:S(2)}) collective-permute-start(bf16[48,2176]{1,0:T(8,128)(2,1)S(1)} %get-tuple-element.35), channel_id=1, source_target_pairs={{0,224},{32,0},{64,32},{96,64},{128,96},{160,128},{192,160},{224,1... | collective-permute-start | bytes 626696 | tf_op jit(solution)/shard_map/ppermute | solution.py:33
  102.6 7.3 %collective-permute-start.7 = (bf16[48,2176]{1,0:T(8,128)(2,1)S(1)}, bf16[48,2176]{1,0:T(8,128)(2,1)S(1)}, u32[]{:S(2)}, u32[]{:S(2)}) collective-permute-start(bf16[48,2176]{1,0:T(8,128)(2,1)S(1)} %get-tuple-element.36), channel_id=1, source_target_pairs={{0,32},{32,64},{64,96},{96,128},{128,160},{160,192},{192,224},{224... | collective-permute-start | bytes 626696 | tf_op jit(solution)/shard_map/ppermute | solution.py:39
  106.0 7.3 %collective-permute-start.4 = (bf16[48,2176]{1,0:T(8,128)(2,1)S(1)}, bf16[48,2176]{1,0:T(8,128)(2,1)S(1)}, u32[]{:S(2)}, u32[]{:S(2)}) collective-permute-start(bf16[48,2176]{1,0:T(8,128)(2,1)S(1)} %fusion.30), channel_id=1, source_target_pairs={{0,224},{32,0},{64,32},{96,64},{128,96},{160,128},{192,160},{224,1... | collective-permute-start | bytes 626696 | tf_op jit(solution)/shard_map/ppermute | solution.py:38
  113.3 7.1 %collective-permute-start.5 = (bf16[48,2176]{1,0:T(8,128)(2,1)S(1)}, bf16[48,2176]{1,0:T(8,128)(2,1)S(1)}, u32[]{:S(2)}, u32[]{:S(2)}) collective-permute-start(bf16[48,2176]{1,0:T(8,128)(2,1)S(1)} %get-tuple-element.33), channel_id=1, source_target_pairs={{0,224},{32,0},{64,32},{96,64},{128,96},{160,128},{192,160},{224,1... | collective-permute-start | bytes 626696 | tf_op jit(solution)/shard_map/ppermute | solution.py:38
  117.1 7.0 %collective-permute-start.8 = (bf16[48,2176]{1,0:T(8,128)(2,1)S(1)}, bf16[48,2176]{1,0:T(8,128)(2,1)S(1)}, u32[]{:S(2)}, u32[]{:S(2)}) collective-permute-start(bf16[48,2176]{1,0:T(8,128)(2,1)S(1)} %get-tuple-element.34), channel_id=1, source_target_pairs={{0,32},{32,64},{64,96},{96,128},{128,160},{160,192},{192,224},{224... | collective-permute-start | bytes 626696 | tf_op jit(solution)/shard_map/ppermute | solution.py:39
  118.5 39.5 %collective-permute-start.12 = (bf16[512,1024]{1,0:T(8,128)(2,1)S(1)}, bf16[512,1024]{1,0:T(8,128)(2,1)S(1)}, u32[]{:S(2)}, u32[]{:S(2)}) collective-permute-start(bf16[512,1024]{1,0:T(8,128)(2,1)S(1)} %pad_maximum_fusion.6), channel_id=1, source_target_pairs={{0,8},{8,0},{1,9},{9,1},{2,10},{10,2},{3,11},{11,3},{4,12},{12,4},... | collective-permute-start | bytes 3145736 | tf_op jit(solution)/shard_map/ppermute | solution.py:20
  124.2 6.0 %collective-permute-start.6 = (bf16[48,2176]{1,0:T(8,128)(2,1)S(1)}, bf16[48,2176]{1,0:T(8,128)(2,1)S(1)}, u32[]{:S(2)}, u32[]{:S(2)}) collective-permute-start(bf16[48,2176]{1,0:T(8,128)(2,1)S(1)} %get-tuple-element.31), channel_id=1, source_target_pairs={{0,224},{32,0},{64,32},{96,64},{128,96},{160,128},{192,160},{224,1... | collective-permute-start | bytes 626696 | tf_op jit(solution)/shard_map/ppermute | solution.py:38
  124.3 7.1 %collective-permute-start.9 = (bf16[48,2176]{1,0:T(8,128)(2,1)S(1)}, bf16[48,2176]{1,0:T(8,128)(2,1)S(1)}, u32[]{:S(2)}, u32[]{:S(2)}) collective-permute-start(bf16[48,2176]{1,0:T(8,128)(2,1)S(1)} %get-tuple-element.32), channel_id=1, source_target_pairs={{0,32},{32,64},{64,96},{96,128},{128,160},{160,192},{192,224},{224... | collective-permute-start | bytes 626696 | tf_op jit(solution)/shard_map/ppermute | solution.py:39
  128.7 37.2 %collective-permute-start.13 = (bf16[512,1024]{1,0:T(8,128)(2,1)}, bf16[512,1024]{1,0:T(8,128)(2,1)S(1)}, u32[]{:S(2)}, u32[]{:S(2)}) collective-permute-start(bf16[512,1024]{1,0:T(8,128)(2,1)} %pad_maximum_fusion.8), channel_id=1, source_target_pairs={{0,16},{16,0},{1,17},{17,1},{2,18},{18,2},{3,19},{19,3},{4,20},{20... | collective-permute-start | bytes 3145736 | tf_op jit(solution)/shard_map/ppermute | solution.py:20
  159.0 6.8 %copy-start.11 = (f32[2,512]{1,0:T(2,128)S(1)}, f32[2,512]{1,0:T(2,128)}, u32[]{:S(2)}) copy-start(f32[2,512]{1,0:T(2,128)} %param.17) | copy-start | bytes 12292
  159.0 7.9 %copy-start.6 = (bf16[512,512]{1,0:T(8,128)(2,1)S(1)}, bf16[512,512]{1,0:T(8,128)(2,1)}, u32[]{:S(2)}) copy-start(bf16[512,512]{1,0:T(8,128)(2,1)} %get-tuple-element.43) | copy-start | bytes 1572868
  159.0 7.9 %copy-start.7 = (bf16[512,512]{1,0:T(8,128)(2,1)S(1)}, bf16[512,512]{1,0:T(8,128)(2,1)}, u32[]{:S(2)}) copy-start(bf16[512,512]{1,0:T(8,128)(2,1)} %get-tuple-element.80) | copy-start | bytes 1572868
  160.0 15.5 %all-to-all-start.3 = ((bf16[16,48,512]{2,1,0:T(8,128)(2,1)}), bf16[16,48,512]{2,1,0:T(8,128)(2,1)S(1)}, u32[]{:S(2)}, u32[]{:S(2)}) async-start(bf16[16,48,512]{2,1,0:T(8,128)(2,1)} %bitcast.35), calls=%async_computation.3 | async-start | bytes 1572864 | tf_op jit(solution)/shard_map/all_to_all | solution.py:139
  165.9 1.0 copy-start.9
  168.5 1.7 copy-start.1
  170.2 28.7 %collective-permute-start.14 = (bf16[1024,1024]{1,0:T(8,128)(2,1)}, bf16[1024,1024]{1,0:T(8,128)(2,1)}, u32[]{:S(2)}, u32[]{:S(2)}) collective-permute-start(bf16[1024,1024]{1,0:T(8,128)(2,1)} %pad_maximum_fusion.1), channel_id=1, source_target_pairs={{0,8},{8,0},{1,9},{9,1},{2,10},{10,2},{3,11},{11,3},{4,12},{12,4},... | collective-permute-start | bytes 6291464 | tf_op jit(solution)/shard_map/ppermute | solution.py:20
  176.6 15.2 %all-to-all-start.4 = ((bf16[16,48,512]{2,1,0:T(8,128)(2,1)}), bf16[16,48,512]{2,1,0:T(8,128)(2,1)S(1)}, u32[]{:S(2)}, u32[]{:S(2)}) async-start(bf16[16,48,512]{2,1,0:T(8,128)(2,1)} %broadcast_in_dim.49), calls=%async_computation.4 | async-start | bytes 1572864 | tf_op jit(solution)/shard_map/all_to_all | solution.py:46
  196.6 1.2 copy-start.2
  198.8 2.6 copy-start.10
  201.6 18.9 %copy-start.3 = (bf16[1024,512]{1,0:T(8,128)(2,1)S(1)}, bf16[1024,512]{1,0:T(8,128)(2,1)}, u32[]{:S(2)}) copy-start(bf16[1024,512]{1,0:T(8,128)(2,1)} %get-tuple-element.12) | copy-start | bytes 3145732
  201.7 8.0 %collective-permute-start.15 = (bf16[48,2176]{1,0:T(8,128)(2,1)S(1)}, bf16[48,2176]{1,0:T(8,128)(2,1)S(1)}, u32[]{:S(2)}, u32[]{:S(2)}) collective-permute-start(bf16[48,2176]{1,0:T(8,128)(2,1)S(1)} %get-tuple-element.29), channel_id=1, source_target_pairs={{0,224},{32,0},{64,32},{96,64},{128,96},{160,128},{192,160},{224,1... | collective-permute-start | bytes 626696 | tf_op jit(solution)/shard_map/ppermute | solution.py:33
  202.7 8.6 %collective-permute-start.19 = (bf16[48,2176]{1,0:T(8,128)(2,1)S(1)}, bf16[48,2176]{1,0:T(8,128)(2,1)S(1)}, u32[]{:S(2)}, u32[]{:S(2)}) collective-permute-start(bf16[48,2176]{1,0:T(8,128)(2,1)S(1)} %get-tuple-element.30), channel_id=1, source_target_pairs={{0,32},{32,64},{64,96},{96,128},{128,160},{160,192},{192,224},{224... | collective-permute-start | bytes 626696 | tf_op jit(solution)/shard_map/ppermute | solution.py:39
  209.7 7.0 %collective-permute-start.16 = (bf16[48,2176]{1,0:T(8,128)(2,1)S(1)}, bf16[48,2176]{1,0:T(8,128)(2,1)S(1)}, u32[]{:S(2)}, u32[]{:S(2)}) collective-permute-start(bf16[48,2176]{1,0:T(8,128)(2,1)S(1)} %fusion.25), channel_id=1, source_target_pairs={{0,224},{32,0},{64,32},{96,64},{128,96},{160,128},{192,160},{224,1... | collective-permute-start | bytes 626696 | tf_op jit(solution)/shard_map/ppermute | solution.py:38
  216.8 8.0 %collective-permute-start.17 = (bf16[48,2176]{1,0:T(8,128)(2,1)S(1)}, bf16[48,2176]{1,0:T(8,128)(2,1)S(1)}, u32[]{:S(2)}, u32[]{:S(2)}) collective-permute-start(bf16[48,2176]{1,0:T(8,128)(2,1)S(1)} %get-tuple-element.27), channel_id=1, source_target_pairs={{0,224},{32,0},{64,32},{96,64},{128,96},{160,128},{192,160},{224,1... | collective-permute-start | bytes 626696 | tf_op jit(solution)/shard_map/ppermute | solution.py:38
  220.4 7.8 %collective-permute-start.20 = (bf16[48,2176]{1,0:T(8,128)(2,1)S(1)}, bf16[48,2176]{1,0:T(8,128)(2,1)S(1)}, u32[]{:S(2)}, u32[]{:S(2)}) collective-permute-start(bf16[48,2176]{1,0:T(8,128)(2,1)S(1)} %get-tuple-element.28), channel_id=1, source_target_pairs={{0,32},{32,64},{64,96},{96,128},{128,160},{160,192},{192,224},{224... | collective-permute-start | bytes 626696 | tf_op jit(solution)/shard_map/ppermute | solution.py:39
  220.5 10.0 %collective-permute-start.22 = (bf16[512,512]{1,0:T(8,128)(2,1)S(1)}, bf16[512,512]{1,0:T(8,128)(2,1)S(1)}, u32[]{:S(2)}, u32[]{:S(2)}) collective-permute-start(bf16[512,512]{1,0:T(8,128)(2,1)S(1)} %constant_dynamic-slice_fusion), channel_id=1, source_target_pairs={{0,16},{16,0},{1,17},{17,1},{2,18},{18,2},{3,19},{19,3},{4,20},{20... | collective-permute-start | bytes 1572872 | tf_op jit(solution)/shard_map/ppermute | solution.py:20
  228.4 5.9 %collective-permute-start.18 = (bf16[48,2176]{1,0:T(8,128)(2,1)S(1)}, bf16[48,2176]{1,0:T(8,128)(2,1)S(1)}, u32[]{:S(2)}, u32[]{:S(2)}) collective-permute-start(bf16[48,2176]{1,0:T(8,128)(2,1)S(1)} %get-tuple-element.25), channel_id=1, source_target_pairs={{0,224},{32,0},{64,32},{96,64},{128,96},{160,128},{192,160},{224,1... | collective-permute-start | bytes 626696 | tf_op jit(solution)/shard_map/ppermute | solution.py:38
  228.8 7.0 %collective-permute-start.21 = (bf16[48,2176]{1,0:T(8,128)(2,1)S(1)}, bf16[48,2176]{1,0:T(8,128)(2,1)S(1)}, u32[]{:S(2)}, u32[]{:S(2)}) collective-permute-start(bf16[48,2176]{1,0:T(8,128)(2,1)S(1)} %get-tuple-element.26), channel_id=1, source_target_pairs={{0,32},{32,64},{64,96},{96,128},{128,160},{160,192},{192,224},{224... | collective-permute-start | bytes 626696 | tf_op jit(solution)/shard_map/ppermute | solution.py:39
  230.9 31.2 %collective-permute-start.23 = (bf16[512,1024]{1,0:T(8,128)(2,1)S(1)}, bf16[512,1024]{1,0:T(8,128)(2,1)S(1)}, u32[]{:S(2)}, u32[]{:S(2)}) collective-permute-start(bf16[512,1024]{1,0:T(8,128)(2,1)S(1)} %pad_maximum_fusion.9), channel_id=1, source_target_pairs={{0,8},{8,0},{1,9},{9,1},{2,10},{10,2},{3,11},{11,3},{4,12},{12,4},... | collective-permute-start | bytes 3145736 | tf_op jit(solution)/shard_map/ppermute | solution.py:20

commit v2 on v1

v2 whole, which is shorter than its diff:
```python
import functools

import jax
import jax.numpy as jnp
from jax import lax
from jax.experimental import pallas as pl
from jax.experimental.pallas import tpu as pltpu
from jax.sharding import Mesh, PartitionSpec as P

LAYERS = 2
BF, F32 = jnp.bfloat16, jnp.float32
AXES = ("z", "xl", "c", "xh", "y")
SIZES = (8, 2, 2, 2, 4)
Z = SIZES[0]
PLANE = ("xl", "xh", "y")
OWNERS = ("c", "xh", "y")
N_PLANE = 16
SMALL, LARGE = 18 * 2**20, 57 * 2**20

HBM = pl.BlockSpec(memory_space=pltpu.HBM)
SMEM = pl.BlockSpec(memory_space=pltpu.SMEM)
VMEM = pl.BlockSpec(memory_space=pltpu.VMEM)


def turn(n, by):
    return [(i, (i + by) % n) for i in range(n)]


def swap(value, axis):
    return lax.ppermute(value, axis, turn(2, 1))


def add(*terms):
    return sum(t.astype(F32) for t in terms)


def call(kernel, out_shape, in_specs, out_specs, scratch=(), flops=0, moved=0, vmem=LARGE):
    return pl.pallas_call(
        kernel,
        out_shape=out_shape,
        in_specs=in_specs,
        out_specs=out_specs,
        scratch_shapes=list(scratch),
        compiler_params=pltpu.CompilerParams(vmem_limit_bytes=vmem),
        cost_estimate=pl.CostEstimate(flops=flops, bytes_accessed=moved, transcendentals=0),
    )


def pack_kernel(layer, xl_ref, gate, up, down, mine, *refs):
    *others, held, in_sems, out_sems = refs
    xl = xl_ref[0]
    half = held.shape[2]
    coming, going = [], []
    for side, which in enumerate((1 - xl, xl)):
        units = pl.ds(pl.multiple_of(which * half, half), half)
        for slot, source in enumerate(
            (gate.at[layer, :, units], up.at[layer, :, units], down.at[layer, units, :])
        ):
            n = 3 * side + slot
            copy = pltpu.make_async_copy(source, held.at[n], in_sems.at[n])
            copy.start()
            coming.append(copy)
            target = mine.at[:, pl.ds(slot * half, half)] if side else others[slot]
            going.append(pltpu.make_async_copy(held.at[n], target, out_sems.at[n]))
    for come, go in zip(coming, going):
        come.wait()
        go.start()
    for go in going:
        go.wait()


def pack(layer, xl, gate, up, down):
    _, rows, cols = gate.shape
    half = cols // 2
    return call(
        functools.partial(pack_kernel, layer),
        tuple(jax.ShapeDtypeStruct((rows, n * half), BF) for n in (3, 1, 1, 1)),
        [SMEM, HBM, HBM, HBM],
        (HBM,) * 4,
        [
            pltpu.VMEM((6, rows, half), BF),
            pltpu.SemaphoreType.DMA((6,)),
            pltpu.SemaphoreType.DMA((6,)),
        ],
        moved=24 * rows * half,
    )(xl, gate, up, down)


def flat(value):
    return value.astype(F32).reshape(-1, value.shape[-1])


def store_blocks(out, value, lanes):
    rows = out.shape[1]
    for i in range(out.shape[0]):
        out[i, :, lanes] = value[i * rows : (i + 1) * rows].astype(BF)


def fetch(layout, held, sems):
    copies = []
    for n, (source, at, (slot, row, column), width) in enumerate(layout):
        target = held.at[slot, pl.ds(row, source.shape[0]), pl.ds(column, width)]
        copy = pltpu.make_async_copy(source.at[:, pl.ds(at, width)], target, sems.at[n])
        copy.start()
        copies.append(copy)
    return copies


def gate_up_kernel(layer, at_ref, x, gains, mine, gate, up, mine_sib, gate_sib, up_sib, out, lead, held, sems):
    xl, far = at_ref[0], at_ref[1]
    width = x.shape[3]
    half = held.shape[2]
    layout = []
    for core, (own, *others) in enumerate(((mine, gate, up), (mine_sib, gate_sib, up_sib))):
        for kind, other in enumerate(others):
            slot = 2 * core + kind
            layout += [(own, kind * half, (slot, 0, 0), half), (other, 0, (slot, width, 0), half)]
    copies = fetch(layout, held, sems)
    squares = 0.0
    normed = []
    for place in range(2):
        value = flat(x[xl if place == 0 else 1 - xl])
        for lane in range(0, width, 128):
            part = value[:, lane : lane + 128]
            squares = squares + part * part
        normed.append((value * gains[layer, place][None, :]).astype(BF))
    store_blocks(out, squares, slice(4 * half, 4 * half + 128))
    both = jnp.concatenate(normed, axis=1)
    for slot in range(4):
        for copy in copies[2 * slot : 2 * slot + 2]:
            copy.wait()
        total = jnp.dot(both, held[slot], preferred_element_type=F32)
        store_blocks(out, total, slice(slot * half, (slot + 1) * half))
    lead[...] = out[far]


def gate_up(layer, at, x, gains, weights):
    _, blocks, rows, width = x.shape
    half = weights[1].shape[1]
    tokens = blocks * rows
    out = jax.ShapeDtypeStruct((blocks, rows, 4 * half + 128), BF)
    return call(
        functools.partial(gate_up_kernel, layer),
        (out, jax.ShapeDtypeStruct(out.shape[1:], BF)),
        [SMEM, VMEM, VMEM] + [HBM] * 6,
        (VMEM, VMEM),
        [pltpu.VMEM((4, 2 * width, half), BF), pltpu.SemaphoreType.DMA((8,))],
        flops=16 * tokens * width * half,
        moved=2 * (8 * width * half + 2 * tokens * width + 4 * tokens * half),
        vmem=SMALL,
    )(at, x, gains, *weights)


def act_kernel(layer, width_total, a, b, c, scales, out):
    units = scales.shape[3]

    def summed(at, n):
        return add(*[t[:, at : at + n] for t in (a, b, c)])

    squares = jnp.sum(summed(4 * units, 128), axis=1, keepdims=True)
    inverse = lax.rsqrt(squares / width_total + 1e-05)
    for core in range(2):
        gate, up = (
            summed((2 * core + kind) * units, units) * inverse * scales[layer, core, kind][None, :]
            for kind in range(2)
        )
        value = (gate / (1.0 + jnp.exp(-gate)) * up).astype(BF)
        for i in range(Z):
            out[i, :, core * units : (core + 1) * units] = value


def activate(layer, width_total, terms, scales):
    rows, cols = terms[0].shape
    units = scales.shape[3]
    return call(
        functools.partial(act_kernel, layer, width_total),
        jax.ShapeDtypeStruct((Z, rows, 2 * units), BF),
        [VMEM] * 4,
        VMEM,
        flops=20 * rows * units,
        moved=8 * rows * cols,
        vmem=SMALL,
    )(*terms, scales)


def down_kernel(xl_ref, act, mine, got, mine_sib, got_sib, out, held, rows_held, made, sems):
    xl = xl_ref[0]
    units = act.shape[2] // 2
    width = held.shape[2]
    coming = pltpu.make_async_copy(act, rows_held, sems.at[4])
    coming.start()
    layout = [
        (mine, 2 * units, (0, 0, 0), width),
        (mine_sib, 2 * units, (0, units, 0), width),
        (got, 0, (1, 0, 0), width),
        (got_sib, 0, (1, units, 0), width),
    ]
    copies = fetch(layout, held, sems)
    coming.wait()
    value = rows_held[...].reshape(-1, act.shape[2])
    going = []
    for place in range(2):
        copies[2 * place].wait()
        copies[2 * place + 1].wait()
        total = jnp.dot(value, held[place], preferred_element_type=F32)
        store_blocks(made.at[place], total, slice(0, width))
        target = out.at[xl if place == 0 else 1 - xl]
        go = pltpu.make_async_copy(made.at[place], target, sems.at[5 + place])
        go.start()
        going.append(go)
    for go in going:
        go.wait()


def project(xl, act, weights):
    blocks, rows, cols = act.shape
    units, width = cols // 2, weights[1].shape[1]
    tokens = blocks * rows
    out = jax.ShapeDtypeStruct((2, blocks, rows, width), BF)
    return call(
        down_kernel,
        out,
        [SMEM] + [HBM] * 5,
        HBM,
        [
            pltpu.VMEM((2, 2 * units, width), BF),
            pltpu.VMEM(act.shape, BF),
            pltpu.VMEM(out.shape, BF),
            pltpu.SemaphoreType.DMA((7,)),
        ],
        flops=8 * tokens * units * width,
        moved=2 * (4 * units * width + 4 * tokens * width),
    )(xl, act, *weights)


def update_kernel(layer, pieces, x, scale, out, sent):
    total = add(*[pieces[i] for i in range(pieces.shape[0])])
    value = (x[...].astype(F32) + total * scale[layer][None, :]).astype(BF)
    out[...] = value
    if sent is not None:
        for i in range(sent.shape[0]):
            sent[i] = value


def first_kernel(a, b, out, sent):
    value = add(a[...], b[...]).astype(BF)
    out[...] = value
    for i in range(sent.shape[0]):
        sent[i] = value


def first(a, b):
    one = jax.ShapeDtypeStruct(a.shape, BF)
    many = jax.ShapeDtypeStruct((N_PLANE, *a.shape), BF)
    return call(first_kernel, (one, many), [VMEM] * 2, (VMEM, VMEM), moved=2 * many.size)(a, b)


def half_kernel(xh_ref, pieces, kept, given):
    xh = xh_ref[0]
    for which, out in ((xh, kept), (1 - xh, given)):
        out[...] = add(*[pieces[i, which] for i in range(pieces.shape[0])]).astype(BF)


def sum_half(xh, pieces):
    one = jax.ShapeDtypeStruct(pieces.shape[2:], BF)
    return call(half_kernel, (one, one), [SMEM, VMEM], (VMEM, VMEM), moved=2 * pieces.size)(xh, pieces)


def last_kernel(layer, pieces, x, scale, out):
    update_kernel(layer, pieces, x, scale, out, None)


def update(layer, pieces, x, scale):
    _, rows, width = pieces.shape
    one = jax.ShapeDtypeStruct((rows, width), BF)
    many = jax.ShapeDtypeStruct((N_PLANE, rows, width), BF)
    moved = 2 * pieces.size * 2
    if layer == LAYERS - 1:
        kernel = functools.partial(last_kernel, layer)
        return call(kernel, one, [VMEM] * 3, VMEM, moved=moved)(pieces, x, scale), None
    kernel = functools.partial(update_kernel, layer)
    return call(kernel, (one, many), [VMEM] * 3, (VMEM, VMEM), moved=moved)(pieces, x, scale)


def exchange(value, axes):
    return lax.all_to_all(value, axes, 0, 0, tiled=True)


def after(first, *then):
    *then, _ = lax.optimization_barrier((*then, first))
    return then if len(then) > 1 else then[0]


def together(*values):
    return lax.optimization_barrier(values)


def scatter_sum_z(parts, lead, z):
    def block(offset):
        return lax.dynamic_index_in_dim(parts, lax.rem(z + offset + Z, Z), 0, keepdims=False)

    down = lax.ppermute(lead, "z", turn(Z, -1))
    up = None
    for far in (3, 2, 1):
        down = add(down, block(-far)).astype(BF)
        up = block(far) if up is None else add(up, block(far)).astype(BF)
        down = lax.ppermute(down, "z", turn(Z, -1))
        up = lax.ppermute(up, "z", turn(Z, 1))
    return down, up, block(0)


def per_device(
    token_ids, embed_table, norm_gain, w_gate, w_up, gate_scale, up_scale, w_down, down_scale
):
    z, xl, core, xh = (lax.axis_index(axis) for axis in ("z", "xl", "c", "xh"))
    xl_arg = xl.astype(jnp.int32).reshape(1)
    xh_arg = xh.astype(jnp.int32).reshape(1)
    at_arg = jnp.stack([xl, lax.rem(z + Z // 2, Z)]).astype(jnp.int32)
    owner = lax.axis_index(OWNERS)
    width = norm_gain.shape[1]
    width_total = width * SIZES[0] * SIZES[1]
    rows = token_ids.shape[0]
    units = w_gate.shape[2] // 2
    n_owners = SIZES[2] * SIZES[3] * SIZES[4]

    all_ids = exchange(jnp.broadcast_to(token_ids[None], (n_owners, rows)), OWNERS)
    gains = jnp.stack([norm_gain, swap(norm_gain, "xl")], 1)
    scales = lax.dynamic_slice_in_dim(jnp.stack([gate_scale, up_scale], 1), xl * units, units, 2)
    scales = jnp.stack([scales, swap(scales, "c")], 1)

    mine, other = [None] * LAYERS, [None] * LAYERS
    mine[0], *other[0] = pack(0, xl_arg, w_gate, w_up, w_down)
    mine_sib = [swap(mine[0], "c"), None]
    got = [[None] * 3 for _ in range(LAYERS)]
    sib = [[None] * 3 for _ in range(LAYERS)]
    got[0][0] = swap(other[0][0], "xl")

    vocab_rows = embed_table.shape[0]
    local_ids = all_ids - owner * vocab_rows
    local_ids = local_ids.reshape(*SIZES[2:], rows).transpose(0, 2, 1, 3).reshape(-1)
    inside = (local_ids >= 0) & (local_ids < vocab_rows)
    local_ids = jnp.clip(local_ids, 0, vocab_rows - 1)
    picked = embed_table.at[local_ids].get(mode="promise_in_bounds")
    picked = jnp.where(inside[:, None], picked, jnp.zeros((), BF))
    picked, got[0][0], other[0][1], mine_sib[0], gains = together(
        picked, got[0][0], other[0][1], mine_sib[0], gains
    )
    got[0][1] = swap(other[0][1], "xl")
    pieces = exchange(picked.reshape(-1, rows, width), ("c", "y"))
    pieces = pieces.reshape(-1, SIZES[3], rows, width)
    mine[1], *other[1] = pack(1, xl_arg, *after(got[0][0], w_gate, w_up, w_down))
    pieces, got[0][1], mine[1], *other[1] = together(pieces, got[0][1], mine[1], *other[1])
    kept, given = sum_half(xh_arg, pieces)
    x, sent = first(kept, swap(given, "xh"))
    sib[0][0] = swap(got[0][0], "c")
    sib[0][1] = swap(got[0][1], "c")
    mine_sib[1] = swap(after(x, mine[1]), "c")

    for layer in range(LAYERS):
        everyone = exchange(sent, PLANE).reshape(2, -1, rows, width)
        weights = (mine[layer], *got[layer][:2], mine_sib[layer], *sib[layer][:2])
        parts, lead = gate_up(layer, at_arg, everyone, gains, weights)
        lead, other[layer][2] = together(lead, other[layer][2])
        got[layer][2] = swap(other[layer][2], "xl")
        terms = scatter_sum_z(parts, lead, z)
        act = activate(layer, width_total, terms, scales)
        if layer == 0:
            act, got[0][2], other[1][0], other[1][1] = together(
                act, got[0][2], other[1][0], other[1][1]
            )
            sib[0][2] = swap(got[0][2], "c")
            got[1][:2] = [swap(other[1][n], "xl") for n in range(2)]
        else:
            act, got[1][2] = together(act, got[1][2])
            sib[1][2] = swap(got[1][2], "c")
        act = exchange(act, "z")
        if layer == 0:
            act, got[1][0], got[1][1] = together(act, got[1][0], got[1][1])
            sib[1][:2] = [swap(got[1][n], "c") for n in range(2)]
        weights = (mine[layer], got[layer][2], mine_sib[layer], sib[layer][2])
        terms = project(xl_arg, act, weights)
        pieces = exchange(terms.reshape(N_PLANE, rows, width), PLANE)
        x, sent = update(layer, pieces, x, down_scale)
    return x


def solution(mesh):
    cut = Mesh(mesh.devices.reshape(SIZES), AXES)
    pair, owners = ("z", "xl"), OWNERS
    in_specs = (
        P(owners),
        P(owners, pair),
        P(None, pair),
        P(None, pair, owners),
        P(None, pair, owners),
        P(None, owners),
        P(None, owners),
        P(None, owners, pair),
        P(None, pair),
    )
    return jax.shard_map(
        per_device, mesh=cut, in_specs=in_specs, out_specs=P(owners, pair), check_vma=False
    )
```

time: 279 us -> 270 us (0.968)
  blocking collectives: 66.5 us -> 34.3 us
  Pallas kernels: 0 us -> 31.3 us
  waiting for transfers between devices: 88.7 us -> 110 us
  other arithmetic: 24.6 us -> 4 us
  starting transfers between devices: 59.2 us -> 76 us
  local copies, waits for them, and re-layouts: 28.4 us -> 12.9 us
  matrix products: 10.3 us -> 0 us
    all_gather x2 -> x0, blocking collectives: 52.1 us -> none  [per_device(): act = lax.all_gather(jnp.concatenate(act, axis=1), 'z', axis=0, tiled=True)]
    ppermute x10 -> x17, waiting for transfers between devices: 0.03 us -> 39.4 us  [swap(): return lax.ppermute(value, axis, turn(2, 1))]
    pallas_call x0 -> x12, Pallas kernels: none -> 31.3 us  [the longest x2 8.7 us: gate_up(): call(functools.partial(gate_up_kernel, layer), (out, jax.ShapeDtypeStruct...]
    all_to_all x1 -> x2, blocking collectives: 14.3 us -> 34.3 us  [exchange(): return lax.all_to_all(value, axes, 0, 0, tiled=True)]
    all_to_all x5 -> x6, waiting for transfers between devices: 53.5 us -> 33.8 us  [exchange(): return lax.all_to_all(value, axes, 0, 0, tiled=True)]
    dot_general x6 -> x0, matrix products: 10.3 us -> none  [the longest x2 5.17 us: per_device(): jnp.dot(normed, gu_sib, preferred_element_type=F32).astype(BF)]
    all_to_all x5 -> x6, starting transfers between devices: 25.5 us -> 33.5 us  [exchange(): return lax.all_to_all(value, axes, 0, 0, tiled=True)]
    ppermute x6, starting transfers between devices: 13.4 us -> 20.8 us  [scatter_sum_z(): down = lax.ppermute(down, 'z', turn(Z, -1))]
  transfers between devices with their start and end apart: 29 -> 37, of which waited for: 16 -> 22; matrix products, arithmetic and copies ran while one was open for 17% -> 3% of each run, Pallas kernels for 0% -> 4%
where the time goes in v2:
time: 270 us; the launch traced here: 269 us
  waiting for transfers between devices  110 us (41%)
  starting transfers between devices  76 us (28%)
  blocking collectives  34.3 us (13%)
  Pallas kernels  31.3 us (12%)
  local copies, waits for them, and re-layouts  12.9 us (5%)
  other arithmetic  4 us (1%)
    ppermute x17, waiting for transfers between devices, swap(): return lax.ppermute(value, axis, turn(2, 1))  39.4 us
    all_to_all x2, blocking collectives, exchange(): return lax.all_to_all(value, axes, 0, 0, tiled=True)  34.3 us
    all_to_all x6, waiting for transfers between devices, exchange(): return lax.all_to_all(value, axes, 0, 0, tiled=True)  33.8 us
    all_to_all x6, starting transfers between devices, exchange(): return lax.all_to_all(value, axes, 0, 0, tiled=True)  33.5 us
    ppermute x6, starting transfers between devices, scatter_sum_z(): down = lax.ppermute(down, 'z', turn(Z, -1))  20.8 us
    ppermute x6, waiting for transfers between devices, scatter_sum_z(): down = lax.ppermute(down, 'z', turn(Z, -1))  14.9 us
    ppermute x17, starting transfers between devices, swap(): return lax.ppermute(value, axis, turn(2, 1))  13 us
    ppermute x6, waiting for transfers between devices, scatter_sum_z(): up = lax.ppermute(up, 'z', turn(Z, 1))  12.8 us
  transfers between devices with their start and end apart: 37, of which 22 were waited for; matrix products, arithmetic and copies ran while one was open for 3% of the time, Pallas kernels for 4%

profile of v2, /device:TPU:2, one launch (start us, length us, event | category | flops | bytes accessed | tf_op | source)
XLA Modules:
  0.0 268.8 jit_solution(17183788110815345040)
XLA Ops:
  0.0 2.9 %shard_map.91 = (bf16[512,1536]{1,0:T(8,128)(2,1)}, bf16[512,512]{1,0:T(8,128)(2,1)}, bf16[512,512]{1,0:T(8,128)(2,1)}, bf16[512,512]{1,0:T(8,128)(2,1)}) custom-call(s32[1]{0:T(128)} %bitcast.xl_ref, bf16[2,512,1024]{2,1,0:T(8,128)(2,1)} %gate.2, bf16[2,512,1024]{2,1,0:T(8,128)(2,1)} %up.2, bf16[2,1024,512]{2,1,0:T(8,128)(2,1)} %down.2), custom_call_target="tpu_custom_call" | custom-call | bytes 6291456 | tf_op jit(solution)/shard_map/pallas_call | solution.py:75
  3.6 6.2 %all-to-all-start = ((s32[16,1,48]{2,1,0:T(1,128)}), s32[16,1,48]{2,1,0:T(1,128)S(1)}, u32[]{:S(2)}, u32[]{:S(2)}) async-start(s32[16,1,48]{2,1,0:T(1,128)} %broadcast_in_dim.20), calls=%async_computation | async-start | bytes 16384 | tf_op jit(solution)/shard_map/all_to_all | solution.py:286
  12.0 5.4 %all-to-all-done = s32[16,1,48]{2,1,0:T(1,128)S(1)} async-done(((s32[16,1,48]{2,1,0:T(1,128)}), s32[16,1,48]{2,1,0:T(1,128)S(1)}, u32[]{:S(2)}, u32[]{:S(2)}) %all-to-all-start) | async-done | bytes 3104 | tf_op jit(solution)/shard_map/all_to_all | solution.py:286
  17.6 5.7 %gather_fusion = bf16[768,512]{1,0:T(8,128)(2,1)S(1)} fusion(bf16[4752,512]{1,0:T(8,128)(2,1)} %param.10, s32[1024]{0:T(1024)S(1)} %pad_clamp_fusion), kind=kCustom, calls=%fused_computation | custom fusion | bytes 1575936 | tf_op jit(solution)/shard_map/gather | solution.py:343
  24.5 4.5 %all-to-all-start.1 = ((bf16[16,48,512]{2,1,0:T(8,128)(2,1)}), bf16[16,48,512]{2,1,0:T(8,128)(2,1)}, u32[]{:S(2)}, u32[]{:S(2)}) async-start(bf16[16,48,512]{2,1,0:T(8,128)(2,1)} %bitcast.58), calls=%async_computation.1 | async-start | bytes 1572864 | tf_op jit(solution)/shard_map/all_to_all | solution.py:286
  30.4 2.9 %shard_map.92 = (bf16[512,1536]{1,0:T(8,128)(2,1)}, bf16[512,512]{1,0:T(8,128)(2,1)}, bf16[512,512]{1,0:T(8,128)(2,1)}, bf16[512,512]{1,0:T(8,128)(2,1)}) custom-call(s32[1]{0:T(128)} %bitcast.xl_ref, bf16[2,512,1024]{2,1,0:T(8,128)(2,1)} %gate.2, bf16[2,512,1024]{2,1,0:T(8,128)(2,1)} %up.2, bf16[2,1024,512]{2,1,0:T(8,128)(2,1)} %down.2), custom_call_target="tpu_custom_call" | custom-call | bytes 6291456 | tf_op jit(solution)/shard_map/pallas_call | solution.py:75
  33.3 10.4 %collective-permute-done.3.up = bf16[512,512]{1,0:T(8,128)(2,1)} collective-permute-done((bf16[512,512]{1,0:T(8,128)(2,1)}, bf16[512,512]{1,0:T(8,128)(2,1)}, u32[]{:S(2)}, u32[]{:S(2)}) %collective-permute-start.3) | collective-permute-done | bytes 524320 | tf_op jit(solution)/shard_map/ppermute | solution.py:30
  43.6 1.9 shard_map.93
  45.5 2.9 %collective-permute-start.4 = (bf16[48,512]{1,0:T(8,128)(2,1)}, bf16[48,512]{1,0:T(8,128)(2,1)S(1)}, u32[]{:S(2)}, u32[]{:S(2)}) collective-permute-start(bf16[48,512]{1,0:T(8,128)(2,1)} %get-tuple-element.66), channel_id=1, source_target_pairs={{0,4},{4,0},{1,5},{5,1},{2,6},{6,2},{3,7},{7,3},{8,12},{12,8},{9,1... | collective-permute-start | bytes 147464 | tf_op jit(solution)/shard_map/ppermute | solution.py:30
  48.4 2.9 %collective-permute-done.4.b = bf16[48,512]{1,0:T(8,128)(2,1)S(1)} collective-permute-done((bf16[48,512]{1,0:T(8,128)(2,1)}, bf16[48,512]{1,0:T(8,128)(2,1)S(1)}, u32[]{:S(2)}, u32[]{:S(2)}) %collective-permute-start.4) | collective-permute-done | bytes 49184 | tf_op jit(solution)/shard_map/ppermute | solution.py:30
  51.9 1.8 shard_map.94
  53.7 8.3 %all-to-all-start.2 = ((bf16[16,48,512]{2,1,0:T(8,128)(2,1)}), bf16[16,48,512]{2,1,0:T(8,128)(2,1)}, u32[]{:S(2)}, u32[]{:S(2)}) async-start(bf16[16,48,512]{2,1,0:T(8,128)(2,1)} %get-tuple-element.67), calls=%async_computation.2 | async-start | bytes 1572864 | tf_op jit(solution)/shard_map/all_to_all | solution.py:286
  62.6 1.7 collective-permute-done.5.gate_sib
  65.0 7.9 %all-to-all-done.2 = bf16[16,48,512]{2,1,0:T(8,128)(2,1)} async-done(((bf16[16,48,512]{2,1,0:T(8,128)(2,1)}), bf16[16,48,512]{2,1,0:T(8,128)(2,1)}, u32[]{:S(2)}, u32[]{:S(2)}) %all-to-all-start.2) | async-done | bytes 786464 | tf_op jit(solution)/shard_map/all_to_all | solution.py:286
  74.0 4.1 %shard_map.95 = (bf16[8,48,2176]{2,1,0:T(8,128)(2,1)S(1)}, bf16[48,2176]{1,0:T(8,128)(2,1)S(1)}) custom-call(s32[2]{0:T(128)S(1)} %pad_add_fusion.at_ref, bf16[2,8,48,512]{3,2,1,0:T(8,128)(2,1)} %bitcast.10.x, f32[2,2,512]{2,1,0:T(2,128)S(1)} %pad_maximum_fusion.1.gains, bf16[512,1536]{1,0:T(8,128)(2,1)S(1)} %copy-done.1, bf16[512,512]{1,0:T(8,128)(2,1)S(1)} %copy-done.6, ...), custom_call_target="tpu_custom_call" | custom-call | flops 1610612736 | bytes 6553600 | tf_op jit(solution)/shard_map/pallas_call | solution.py:142
  78.1 5.9 %collective-permute-start.7 = (bf16[48,2176]{1,0:T(8,128)(2,1)S(1)}, bf16[48,2176]{1,0:T(8,128)(2,1)S(1)}, u32[]{:S(2)}, u32[]{:S(2)}) collective-permute-start(bf16[48,2176]{1,0:T(8,128)(2,1)S(1)} %get-tuple-element.73), channel_id=1, source_target_pairs={{0,224},{32,0},{64,32},{96,64},{128,96},{160,128},{192,160},{224,1... | collective-permute-start | bytes 626696 | tf_op jit(solution)/shard_map/ppermute | solution.py:302
  84.2 3.6 %collective-permute-done.7 = bf16[48,2176]{1,0:T(8,128)(2,1)S(1)} collective-permute-done((bf16[48,2176]{1,0:T(8,128)(2,1)S(1)}, bf16[48,2176]{1,0:T(8,128)(2,1)S(1)}, u32[]{:S(2)}, u32[]{:S(2)}) %collective-permute-start.7) | collective-permute-done | bytes 208928 | tf_op jit(solution)/shard_map/ppermute | solution.py:302
  87.8 3.8 %collective-permute-start.8 = (bf16[48,2176]{1,0:T(8,128)(2,1)S(1)}, bf16[48,2176]{1,0:T(8,128)(2,1)S(1)}, u32[]{:S(2)}, u32[]{:S(2)}) collective-permute-start(bf16[48,2176]{1,0:T(8,128)(2,1)S(1)} %fusion.9), channel_id=1, source_target_pairs={{0,224},{32,0},{64,32},{96,64},{128,96},{160,128},{192,160},{224,1... | collective-permute-start | bytes 626696 | tf_op jit(solution)/shard_map/ppermute | solution.py:307
  91.6 3.4 %collective-permute-done.8 = bf16[48,2176]{1,0:T(8,128)(2,1)S(1)} collective-permute-done((bf16[48,2176]{1,0:T(8,128)(2,1)S(1)}, bf16[48,2176]{1,0:T(8,128)(2,1)S(1)}, u32[]{:S(2)}, u32[]{:S(2)}) %collective-permute-start.8) | collective-permute-done | bytes 208928 | tf_op jit(solution)/shard_map/ppermute | solution.py:307
  96.3 3.9 %collective-permute-start.9 = (bf16[48,2176]{1,0:T(8,128)(2,1)S(1)}, bf16[48,2176]{1,0:T(8,128)(2,1)S(1)}, u32[]{:S(2)}, u32[]{:S(2)}) collective-permute-start(bf16[48,2176]{1,0:T(8,128)(2,1)S(1)} %get-tuple-element.108), channel_id=1, source_target_pairs={{0,224},{32,0},{64,32},{96,64},{128,96},{160,128},{192,160},{224,1... | collective-permute-start | bytes 626696 | tf_op jit(solution)/shard_map/ppermute | solution.py:307
  101.7 2.0 collective-permute-done.12
  104.9 3.6 %collective-permute-start.10 = (bf16[48,2176]{1,0:T(8,128)(2,1)S(1)}, bf16[48,2176]{1,0:T(8,128)(2,1)S(1)}, u32[]{:S(2)}, u32[]{:S(2)}) collective-permute-start(bf16[48,2176]{1,0:T(8,128)(2,1)S(1)} %get-tuple-element.106), channel_id=1, source_target_pairs={{0,224},{32,0},{64,32},{96,64},{128,96},{160,128},{192,160},{224,1... | collective-permute-start | bytes 626696 | tf_op jit(solution)/shard_map/ppermute | solution.py:307
  108.6 3.2 %collective-permute-done.10.a = bf16[48,2176]{1,0:T(8,128)(2,1)S(1)} collective-permute-done((bf16[48,2176]{1,0:T(8,128)(2,1)S(1)}, bf16[48,2176]{1,0:T(8,128)(2,1)S(1)}, u32[]{:S(2)}, u32[]{:S(2)}) %collective-permute-start.10) | collective-permute-done | bytes 208928 | tf_op jit(solution)/shard_map/ppermute | solution.py:307
  111.8 3.7 %collective-permute-done.13.b = bf16[48,2176]{1,0:T(8,128)(2,1)S(1)} collective-permute-done((bf16[48,2176]{1,0:T(8,128)(2,1)S(1)}, bf16[48,2176]{1,0:T(8,128)(2,1)S(1)}, u32[]{:S(2)}, u32[]{:S(2)}) %collective-permute-start.13) | collective-permute-done | bytes 208928 | tf_op jit(solution)/shard_map/ppermute | solution.py:308
  116.6 5.5 %all-to-all-start.3 = ((bf16[8,48,1024]{2,1,0:T(8,128)(2,1)}), bf16[8,48,1024]{2,1,0:T(8,128)(2,1)}, u32[]{:S(2)}, u32[]{:S(2)}) async-start(bf16[8,48,1024]{2,1,0:T(8,128)(2,1)} %shard_map.96), calls=%async_computation.3 | async-start | bytes 1572864 | tf_op jit(solution)/shard_map/all_to_all | solution.py:286
  124.7 12.6 %collective-permute-done.16.gate = bf16[512,512]{1,0:T(8,128)(2,1)} collective-permute-done((bf16[512,512]{1,0:T(8,128)(2,1)}, bf16[512,512]{1,0:T(8,128)(2,1)}, u32[]{:S(2)}, u32[]{:S(2)}) %collective-permute-start.16) | collective-permute-done | bytes 524320 | tf_op jit(solution)/shard_map/ppermute | solution.py:30
  137.3 7.6 %collective-permute-done.17.up = bf16[512,512]{1,0:T(8,128)(2,1)} collective-permute-done((bf16[512,512]{1,0:T(8,128)(2,1)}, bf16[512,512]{1,0:T(8,128)(2,1)}, u32[]{:S(2)}, u32[]{:S(2)}) %collective-permute-start.17) | collective-permute-done | bytes 524320 | tf_op jit(solution)/shard_map/ppermute | solution.py:30
  144.9 3.4 %shard_map.97 = bf16[2,8,48,512]{3,2,1,0:T(8,128)(2,1)} custom-call(s32[1]{0:T(128)} %bitcast.xl_ref, bf16[8,48,1024]{2,1,0:T(8,128)(2,1)} %all-to-all-done.3.act, bf16[512,1536]{1,0:T(8,128)(2,1)} %get-tuple-element.53.mine, bf16[512,512]{1,0:T(8,128)(2,1)} %collective-permute-done.15.got, bf16[512,1536]{1,0:T(8,128)(2,1)} %copy-done.2, ...), custom_call_target="tpu_custom_call" | custom-call | flops 805306368 | bytes 3670016 | tf_op jit(solution)/shard_map/pallas_call | solution.py:220
  148.3 16.4 %all_to_all.41.pieces = bf16[16,48,512]{2,1,0:T(8,128)(2,1)} all-to-all(bf16[16,48,512]{2,1,0:T(8,128)(2,1)} %bitcast.60), channel_id=1, replica_groups=mesh['z'=8,'xl'=2,'c'=2,'xh'=2,'y'=4] {'xl','xh','y'}, dimensions={0} | all-to-all | bytes 1572864 | tf_op jit(solution)/shard_map/all_to_all | solution.py:286
  164.8 2.2 shard_map.98
  167.0 5.5 %all-to-all-start.5 = ((bf16[16,48,512]{2,1,0:T(8,128)(2,1)}), bf16[16,48,512]{2,1,0:T(8,128)(2,1)}, u32[]{:S(2)}, u32[]{:S(2)}) async-start(bf16[16,48,512]{2,1,0:T(8,128)(2,1)} %get-tuple-element.84), calls=%async_computation.5 | async-start | bytes 1572864 | tf_op jit(solution)/shard_map/all_to_all | solution.py:286
  173.0 1.6 collective-permute-done.20.gate_sib
  176.2 6.4 %all-to-all-done.5 = bf16[16,48,512]{2,1,0:T(8,128)(2,1)} async-done(((bf16[16,48,512]{2,1,0:T(8,128)(2,1)}), bf16[16,48,512]{2,1,0:T(8,128)(2,1)}, u32[]{:S(2)}, u32[]{:S(2)}) %all-to-all-start.5) | async-done | bytes 786464 | tf_op jit(solution)/shard_map/all_to_all | solution.py:286
  184.7 4.6 %shard_map.99 = (bf16[8,48,2176]{2,1,0:T(8,128)(2,1)S(1)}, bf16[48,2176]{1,0:T(8,128)(2,1)S(1)}) custom-call(s32[2]{0:T(128)S(1)} %pad_add_fusion.at_ref, bf16[2,8,48,512]{3,2,1,0:T(8,128)(2,1)} %bitcast.21.x, f32[2,2,512]{2,1,0:T(2,128)S(1)} %pad_maximum_fusion.1.gains, bf16[512,1536]{1,0:T(8,128)(2,1)S(1)} %copy-done, ...), custom_call_target="tpu_custom_call" | custom-call | flops 1610612736 | bytes 6553600 | tf_op jit(solution)/shard_map/pallas_call | solution.py:142
  191.6 5.5 %collective-permute-done.22 = bf16[48,2176]{1,0:T(8,128)(2,1)S(1)} collective-permute-done((bf16[48,2176]{1,0:T(8,128)(2,1)S(1)}, bf16[48,2176]{1,0:T(8,128)(2,1)S(1)}, u32[]{:S(2)}, u32[]{:S(2)}) %collective-permute-start.22) | collective-permute-done | bytes 208928 | tf_op jit(solution)/shard_map/ppermute | solution.py:302
  197.1 2.8 %collective-permute-start.23 = (bf16[48,2176]{1,0:T(8,128)(2,1)S(1)}, bf16[48,2176]{1,0:T(8,128)(2,1)S(1)}, u32[]{:S(2)}, u32[]{:S(2)}) collective-permute-start(bf16[48,2176]{1,0:T(8,128)(2,1)S(1)} %fusion.4), channel_id=1, source_target_pairs={{0,224},{32,0},{64,32},{96,64},{128,96},{160,128},{192,160},{224,1... | collective-permute-start | bytes 626696 | tf_op jit(solution)/shard_map/ppermute | solution.py:307
  199.9 4.9 %collective-permute-done.23 = bf16[48,2176]{1,0:T(8,128)(2,1)S(1)} collective-permute-done((bf16[48,2176]{1,0:T(8,128)(2,1)S(1)}, bf16[48,2176]{1,0:T(8,128)(2,1)S(1)}, u32[]{:S(2)}, u32[]{:S(2)}) %collective-permute-start.23) | collective-permute-done | bytes 208928 | tf_op jit(solution)/shard_map/ppermute | solution.py:307
  205.3 3.8 %collective-permute-start.24 = (bf16[48,2176]{1,0:T(8,128)(2,1)S(1)}, bf16[48,2176]{1,0:T(8,128)(2,1)S(1)}, u32[]{:S(2)}, u32[]{:S(2)}) collective-permute-start(bf16[48,2176]{1,0:T(8,128)(2,1)S(1)} %get-tuple-element.102), channel_id=1, source_target_pairs={{0,224},{32,0},{64,32},{96,64},{128,96},{160,128},{192,160},{224,1... | collective-permute-start | bytes 626696 | tf_op jit(solution)/shard_map/ppermute | solution.py:307
  210.5 3.1 %collective-permute-done.27 = bf16[48,2176]{1,0:T(8,128)(2,1)S(1)} collective-permute-done((bf16[48,2176]{1,0:T(8,128)(2,1)S(1)}, bf16[48,2176]{1,0:T(8,128)(2,1)S(1)}, u32[]{:S(2)}, u32[]{:S(2)}) %collective-permute-start.27) | collective-permute-done | bytes 208928 | tf_op jit(solution)/shard_map/ppermute | solution.py:308
  213.7 3.0 %collective-permute-start.25 = (bf16[48,2176]{1,0:T(8,128)(2,1)S(1)}, bf16[48,2176]{1,0:T(8,128)(2,1)S(1)}, u32[]{:S(2)}, u32[]{:S(2)}) collective-permute-start(bf16[48,2176]{1,0:T(8,128)(2,1)S(1)} %get-tuple-element.100), channel_id=1, source_target_pairs={{0,224},{32,0},{64,32},{96,64},{128,96},{160,128},{192,160},{224,1... | collective-permute-start | bytes 626696 | tf_op jit(solution)/shard_map/ppermute | solution.py:307
  216.7 3.3 %collective-permute-done.25.a = bf16[48,2176]{1,0:T(8,128)(2,1)S(1)} collective-permute-done((bf16[48,2176]{1,0:T(8,128)(2,1)S(1)}, bf16[48,2176]{1,0:T(8,128)(2,1)S(1)}, u32[]{:S(2)}, u32[]{:S(2)}) %collective-permute-start.25) | collective-permute-done | bytes 208928 | tf_op jit(solution)/shard_map/ppermute | solution.py:307
  220.1 4.0 %collective-permute-done.28.b = bf16[48,2176]{1,0:T(8,128)(2,1)S(1)} collective-permute-done((bf16[48,2176]{1,0:T(8,128)(2,1)S(1)}, bf16[48,2176]{1,0:T(8,128)(2,1)S(1)}, u32[]{:S(2)}, u32[]{:S(2)}) %collective-permute-start.28) | collective-permute-done | bytes 208928 | tf_op jit(solution)/shard_map/ppermute | solution.py:308
  225.2 3.5 %all-to-all-start.6 = ((bf16[8,48,1024]{2,1,0:T(8,128)(2,1)}), bf16[8,48,1024]{2,1,0:T(8,128)(2,1)S(1)}, u32[]{:S(2)}, u32[]{:S(2)}) async-start(bf16[8,48,1024]{2,1,0:T(8,128)(2,1)} %shard_map.100), calls=%async_computation.6 | async-start | bytes 1572864 | tf_op jit(solution)/shard_map/all_to_all | solution.py:286
  228.8 1.9 collective-permute-done.30.got_sib
  230.7 14.0 %all-to-all-done.6.act = bf16[8,48,1024]{2,1,0:T(8,128)(2,1)S(1)} async-done(((bf16[8,48,1024]{2,1,0:T(8,128)(2,1)}), bf16[8,48,1024]{2,1,0:T(8,128)(2,1)S(1)}, u32[]{:S(2)}, u32[]{:S(2)}) %all-to-all-start.6) | async-done | bytes 786464 | tf_op jit(solution)/shard_map/all_to_all | solution.py:286
  245.6 3.4 %shard_map.101 = bf16[2,8,48,512]{3,2,1,0:T(8,128)(2,1)} custom-call(s32[1]{0:T(128)} %bitcast.xl_ref, bf16[8,48,1024]{2,1,0:T(8,128)(2,1)} %copy-done.11, bf16[512,1536]{1,0:T(8,128)(2,1)} %get-tuple-element.88.mine, bf16[512,512]{1,0:T(8,128)(2,1)} %copy-done.12, bf16[512,1536]{1,0:T(8,128)(2,1)} %copy-done.3, bf16[512,512]{1,0:T(8,128)(2,1)} %copy-done.13), custom_call_target="tpu_custom_call" | custom-call | flops 805306368 | bytes 3670016 | tf_op jit(solution)/shard_map/pallas_call | solution.py:220
  249.0 17.9 %all_to_all.42.pieces = bf16[16,48,512]{2,1,0:T(8,128)(2,1)} all-to-all(bf16[16,48,512]{2,1,0:T(8,128)(2,1)} %bitcast.59), channel_id=1, replica_groups=mesh['z'=8,'xl'=2,'c'=2,'xh'=2,'y'=4] {'xl','xh','y'}, dimensions={0} | all-to-all | bytes 1572864 | tf_op jit(solution)/shard_map/all_to_all | solution.py:286
  266.9 1.9 shard_map.102
  (110 shorter events, 26.9 us)
Async XLA Ops:
  0.0 11.4 %copy-start.17 = (f32[2,512]{1,0:T(2,128)S(1)}, f32[2,512]{1,0:T(2,128)}, u32[]{:S(2)}) copy-start(f32[2,512]{1,0:T(2,128)} %param.11) | copy-start | bytes 12292
  2.9 21.5 %collective-permute-start.1 = (bf16[512,1536]{1,0:T(8,128)(2,1)}, bf16[512,1536]{1,0:T(8,128)(2,1)S(1)}, u32[]{:S(2)}, u32[]{:S(2)}) collective-permute-start(bf16[512,1536]{1,0:T(8,128)(2,1)} %get-tuple-element.53.mine), channel_id=1, source_target_pairs={{0,8},{8,0},{1,9},{9,1},{2,10},{10,2},{3,11},{11,3},{4,12},{12,4},... | collective-permute-start | bytes 4718600 | tf_op jit(solution)/shard_map/ppermute | solution.py:30
  3.6 13.7 %all-to-all-start = ((s32[16,1,48]{2,1,0:T(1,128)}), s32[16,1,48]{2,1,0:T(1,128)S(1)}, u32[]{:S(2)}, u32[]{:S(2)}) async-start(s32[16,1,48]{2,1,0:T(1,128)} %broadcast_in_dim.20), calls=%async_computation | async-start | bytes 16384 | tf_op jit(solution)/shard_map/all_to_all | solution.py:286
  9.9 14.6 %collective-permute-start = (bf16[512,512]{1,0:T(8,128)(2,1)}, bf16[512,512]{1,0:T(8,128)(2,1)S(1)}, u32[]{:S(2)}, u32[]{:S(2)}) collective-permute-start(bf16[512,512]{1,0:T(8,128)(2,1)} %get-tuple-element.51), channel_id=1, source_target_pairs={{0,16},{16,0},{1,17},{17,1},{2,18},{18,2},{3,19},{19,3},{4,20},{20... | collective-permute-start | bytes 1572872 | tf_op jit(solution)/shard_map/ppermute | solution.py:30
  11.4 13.0 %collective-permute-start.2 = (f32[2,512]{1,0:T(2,128)S(1)}, f32[2,512]{1,0:T(2,128)S(1)}, u32[]{:S(2)}, u32[]{:S(2)}) collective-permute-start(f32[2,512]{1,0:T(2,128)S(1)} %copy-done.17), channel_id=1, source_target_pairs={{0,16},{16,0},{1,17},{17,1},{2,18},{18,2},{3,19},{19,3},{4,20},{20... | collective-permute-start | bytes 12296 | tf_op jit(solution)/shard_map/ppermute | solution.py:30
  24.5 48.4 %copy-start.2 = (bf16[512,1536]{1,0:T(8,128)(2,1)}, bf16[512,1536]{1,0:T(8,128)(2,1)S(1)}, u32[]{:S(2)}) copy-start(bf16[512,1536]{1,0:T(8,128)(2,1)S(1)} %collective-permute-done.1.mine_sib) | copy-start | bytes 4718596
  24.5 19.2 %all-to-all-start.1 = ((bf16[16,48,512]{2,1,0:T(8,128)(2,1)}), bf16[16,48,512]{2,1,0:T(8,128)(2,1)}, u32[]{:S(2)}, u32[]{:S(2)}) async-start(bf16[16,48,512]{2,1,0:T(8,128)(2,1)} %bitcast.58), calls=%async_computation.1 | async-start | bytes 1572864 | tf_op jit(solution)/shard_map/all_to_all | solution.py:286
  29.0 14.7 %collective-permute-start.3 = (bf16[512,512]{1,0:T(8,128)(2,1)}, bf16[512,512]{1,0:T(8,128)(2,1)}, u32[]{:S(2)}, u32[]{:S(2)}) collective-permute-start(bf16[512,512]{1,0:T(8,128)(2,1)} %get-tuple-element.55), channel_id=1, source_target_pairs={{0,16},{16,0},{1,17},{17,1},{2,18},{18,2},{3,19},{19,3},{4,20},{20... | collective-permute-start | bytes 1572872 | tf_op jit(solution)/shard_map/ppermute | solution.py:30
  33.2 39.7 %copy-start.1 = (bf16[512,1536]{1,0:T(8,128)(2,1)S(1)}, bf16[512,1536]{1,0:T(8,128)(2,1)}, u32[]{:S(2)}) copy-start(bf16[512,1536]{1,0:T(8,128)(2,1)} %get-tuple-element.53.mine) | copy-start | bytes 4718596
  45.5 5.8 %collective-permute-start.4 = (bf16[48,512]{1,0:T(8,128)(2,1)}, bf16[48,512]{1,0:T(8,128)(2,1)S(1)}, u32[]{:S(2)}, u32[]{:S(2)}) collective-permute-start(bf16[48,512]{1,0:T(8,128)(2,1)} %get-tuple-element.66), channel_id=1, source_target_pairs={{0,4},{4,0},{1,5},{5,1},{2,6},{6,2},{3,7},{7,3},{8,12},{12,8},{9,1... | collective-permute-start | bytes 147464 | tf_op jit(solution)/shard_map/ppermute | solution.py:30
  53.7 19.2 %all-to-all-start.2 = ((bf16[16,48,512]{2,1,0:T(8,128)(2,1)}), bf16[16,48,512]{2,1,0:T(8,128)(2,1)}, u32[]{:S(2)}, u32[]{:S(2)}) async-start(bf16[16,48,512]{2,1,0:T(8,128)(2,1)} %get-tuple-element.67), calls=%async_computation.2 | async-start | bytes 1572864 | tf_op jit(solution)/shard_map/all_to_all | solution.py:286
  62.0 2.3 collective-permute-start.5
  62.0 3.0 %collective-permute-start.6 = (bf16[512,512]{1,0:T(8,128)(2,1)}, bf16[512,512]{1,0:T(8,128)(2,1)}, u32[]{:S(2)}, u32[]{:S(2)}) collective-permute-start(bf16[512,512]{1,0:T(8,128)(2,1)} %collective-permute-done.3.up), channel_id=1, source_target_pairs={{0,8},{8,0},{1,9},{9,1},{2,10},{10,2},{3,11},{11,3},{4,12},{12,4},... | collective-permute-start | bytes 1572872 | tf_op jit(solution)/shard_map/ppermute | solution.py:30
  78.1 22.2 %copy-start.15 = (f32[2,1024]{1,0:T(2,128)S(1)}, f32[2,1024]{1,0:T(2,128)}, u32[]{:S(2)}) copy-start(f32[2,1024]{1,0:T(2,128)} %param.14) | copy-start | bytes 24580
  78.1 22.2 %copy-start.16 = (f32[2,1024]{1,0:T(2,128)S(1)}, f32[2,1024]{1,0:T(2,128)}, u32[]{:S(2)}) copy-start(f32[2,1024]{1,0:T(2,128)} %param.15) | copy-start | bytes 24580
  78.1 22.3 %copy-start.20 = (bf16[512,512]{1,0:T(8,128)(2,1)S(1)}, bf16[512,512]{1,0:T(8,128)(2,1)}, u32[]{:S(2)}) copy-start(bf16[512,512]{1,0:T(8,128)(2,1)} %get-tuple-element.75) | copy-start | bytes 1572868
  78.1 9.7 %collective-permute-start.7 = (bf16[48,2176]{1,0:T(8,128)(2,1)S(1)}, bf16[48,2176]{1,0:T(8,128)(2,1)S(1)}, u32[]{:S(2)}, u32[]{:S(2)}) collective-permute-start(bf16[48,2176]{1,0:T(8,128)(2,1)S(1)} %get-tuple-element.73), channel_id=1, source_target_pairs={{0,224},{32,0},{64,32},{96,64},{128,96},{160,128},{192,160},{224,1... | collective-permute-start | bytes 626696 | tf_op jit(solution)/shard_map/ppermute | solution.py:302
  84.1 7.5 %collective-permute-start.11 = (bf16[48,2176]{1,0:T(8,128)(2,1)S(1)}, bf16[48,2176]{1,0:T(8,128)(2,1)S(1)}, u32[]{:S(2)}, u32[]{:S(2)}) collective-permute-start(bf16[48,2176]{1,0:T(8,128)(2,1)S(1)} %get-tuple-element.104), channel_id=1, source_target_pairs={{0,32},{32,64},{64,96},{96,128},{128,160},{160,192},{192,224},{224... | collective-permute-start | bytes 626696 | tf_op jit(solution)/shard_map/ppermute | solution.py:308
  87.8 7.2 %collective-permute-start.8 = (bf16[48,2176]{1,0:T(8,128)(2,1)S(1)}, bf16[48,2176]{1,0:T(8,128)(2,1)S(1)}, u32[]{:S(2)}, u32[]{:S(2)}) collective-permute-start(bf16[48,2176]{1,0:T(8,128)(2,1)S(1)} %fusion.9), channel_id=1, source_target_pairs={{0,224},{32,0},{64,32},{96,64},{128,96},{160,128},{192,160},{224,1... | collective-permute-start | bytes 626696 | tf_op jit(solution)/shard_map/ppermute | solution.py:307
  96.2 7.5 %collective-permute-start.12 = (bf16[48,2176]{1,0:T(8,128)(2,1)S(1)}, bf16[48,2176]{1,0:T(8,128)(2,1)S(1)}, u32[]{:S(2)}, u32[]{:S(2)}) collective-permute-start(bf16[48,2176]{1,0:T(8,128)(2,1)S(1)} %get-tuple-element.107), channel_id=1, source_target_pairs={{0,32},{32,64},{64,96},{96,128},{128,160},{160,192},{192,224},{224... | collective-permute-start | bytes 626696 | tf_op jit(solution)/shard_map/ppermute | solution.py:308
  96.3 7.5 %collective-permute-start.9 = (bf16[48,2176]{1,0:T(8,128)(2,1)S(1)}, bf16[48,2176]{1,0:T(8,128)(2,1)S(1)}, u32[]{:S(2)}, u32[]{:S(2)}) collective-permute-start(bf16[48,2176]{1,0:T(8,128)(2,1)S(1)} %get-tuple-element.108), channel_id=1, source_target_pairs={{0,224},{32,0},{64,32},{96,64},{128,96},{160,128},{192,160},{224,1... | collective-permute-start | bytes 626696 | tf_op jit(solution)/shard_map/ppermute | solution.py:307
  100.4 8.2 %collective-permute-start.14 = (f32[2,2,512]{2,1,0:T(2,128)S(1)}, f32[2,2,512]{2,1,0:T(2,128)S(1)}, u32[]{:S(2)}, u32[]{:S(2)}) collective-permute-start(f32[2,2,512]{2,1,0:T(2,128)S(1)} %fusion.10), channel_id=1, source_target_pairs={{0,8},{8,0},{1,9},{9,1},{2,10},{10,2},{3,11},{11,3},{4,12},{12,4},... | collective-permute-start | bytes 24584 | tf_op jit(solution)/shard_map/ppermute | solution.py:30
  100.4 16.2 %collective-permute-start.15 = (bf16[512,512]{1,0:T(8,128)(2,1)S(1)}, bf16[512,512]{1,0:T(8,128)(2,1)}, u32[]{:S(2)}, u32[]{:S(2)}) collective-permute-start(bf16[512,512]{1,0:T(8,128)(2,1)S(1)} %copy-done.20), channel_id=1, source_target_pairs={{0,16},{16,0},{1,17},{17,1},{2,18},{18,2},{3,19},{19,3},{4,20},{20... | collective-permute-start | bytes 1572872 | tf_op jit(solution)/shard_map/ppermute | solution.py:30
  104.9 19.3 %copy-start = (bf16[512,1536]{1,0:T(8,128)(2,1)S(1)}, bf16[512,1536]{1,0:T(8,128)(2,1)}, u32[]{:S(2)}) copy-start(bf16[512,1536]{1,0:T(8,128)(2,1)} %get-tuple-element.88.mine) | copy-start | bytes 4718596
  104.9 6.9 %collective-permute-start.10 = (bf16[48,2176]{1,0:T(8,128)(2,1)S(1)}, bf16[48,2176]{1,0:T(8,128)(2,1)S(1)}, u32[]{:S(2)}, u32[]{:S(2)}) collective-permute-start(bf16[48,2176]{1,0:T(8,128)(2,1)S(1)} %get-tuple-element.106), channel_id=1, source_target_pairs={{0,224},{32,0},{64,32},{96,64},{128,96},{160,128},{192,160},{224,1... | collective-permute-start | bytes 626696 | tf_op jit(solution)/shard_map/ppermute | solution.py:307
  108.5 7.0 %collective-permute-start.13 = (bf16[48,2176]{1,0:T(8,128)(2,1)S(1)}, bf16[48,2176]{1,0:T(8,128)(2,1)S(1)}, u32[]{:S(2)}, u32[]{:S(2)}) collective-permute-start(bf16[48,2176]{1,0:T(8,128)(2,1)S(1)} %get-tuple-element.105), channel_id=1, source_target_pairs={{0,32},{32,64},{64,96},{96,128},{128,160},{160,192},{192,224},{224... | collective-permute-start | bytes 626696 | tf_op jit(solution)/shard_map/ppermute | solution.py:308
  116.6 28.3 %all-to-all-start.3 = ((bf16[8,48,1024]{2,1,0:T(8,128)(2,1)}), bf16[8,48,1024]{2,1,0:T(8,128)(2,1)}, u32[]{:S(2)}, u32[]{:S(2)}) async-start(bf16[8,48,1024]{2,1,0:T(8,128)(2,1)} %shard_map.96), calls=%async_computation.3 | async-start | bytes 1572864 | tf_op jit(solution)/shard_map/all_to_all | solution.py:286
  122.1 15.2 %collective-permute-start.16 = (bf16[512,512]{1,0:T(8,128)(2,1)}, bf16[512,512]{1,0:T(8,128)(2,1)}, u32[]{:S(2)}, u32[]{:S(2)}) collective-permute-start(bf16[512,512]{1,0:T(8,128)(2,1)} %get-tuple-element.79), channel_id=1, source_target_pairs={{0,16},{16,0},{1,17},{17,1},{2,18},{18,2},{3,19},{19,3},{4,20},{20... | collective-permute-start | bytes 1572872 | tf_op jit(solution)/shard_map/ppermute | solution.py:30
  123.4 21.5 %collective-permute-start.17 = (bf16[512,512]{1,0:T(8,128)(2,1)}, bf16[512,512]{1,0:T(8,128)(2,1)}, u32[]{:S(2)}, u32[]{:S(2)}) collective-permute-start(bf16[512,512]{1,0:T(8,128)(2,1)} %get-tuple-element.80), channel_id=1, source_target_pairs={{0,16},{16,0},{1,17},{17,1},{2,18},{18,2},{3,19},{19,3},{4,20},{20... | collective-permute-start | bytes 1572872 | tf_op jit(solution)/shard_map/ppermute | solution.py:30
  124.2 20.8 %collective-permute-start.18 = (bf16[512,512]{1,0:T(8,128)(2,1)}, bf16[512,512]{1,0:T(8,128)(2,1)}, u32[]{:S(2)}, u32[]{:S(2)}) collective-permute-start(bf16[512,512]{1,0:T(8,128)(2,1)} %collective-permute-done.15.got), channel_id=1, source_target_pairs={{0,8},{8,0},{1,9},{9,1},{2,10},{10,2},{3,11},{11,3},{4,12},{12,4},... | collective-permute-start | bytes 1572872 | tf_op jit(solution)/shard_map/ppermute | solution.py:30
  124.2 48.8 %collective-permute-start.19 = (bf16[512,1536]{1,0:T(8,128)(2,1)S(1)}, bf16[512,1536]{1,0:T(8,128)(2,1)S(1)}, u32[]{:S(2)}, u32[]{:S(2)}) collective-permute-start(bf16[512,1536]{1,0:T(8,128)(2,1)S(1)} %copy-done), channel_id=1, source_target_pairs={{0,8},{8,0},{1,9},{9,1},{2,10},{10,2},{3,11},{11,3},{4,12},{12,4},... | collective-permute-start | bytes 4718600 | tf_op jit(solution)/shard_map/ppermute | solution.py:30
  167.0 15.6 %all-to-all-start.5 = ((bf16[16,48,512]{2,1,0:T(8,128)(2,1)}), bf16[16,48,512]{2,1,0:T(8,128)(2,1)}, u32[]{:S(2)}, u32[]{:S(2)}) async-start(bf16[16,48,512]{2,1,0:T(8,128)(2,1)} %get-tuple-element.84), calls=%async_computation.5 | async-start | bytes 1572864 | tf_op jit(solution)/shard_map/all_to_all | solution.py:286
  172.5 2.1 collective-permute-start.20
  172.5 2.9 %collective-permute-start.21 = (bf16[512,512]{1,0:T(8,128)(2,1)}, bf16[512,512]{1,0:T(8,128)(2,1)S(1)}, u32[]{:S(2)}, u32[]{:S(2)}) collective-permute-start(bf16[512,512]{1,0:T(8,128)(2,1)} %collective-permute-done.17.up), channel_id=1, source_target_pairs={{0,8},{8,0},{1,9},{9,1},{2,10},{10,2},{3,11},{11,3},{4,12},{12,4},... | collective-permute-start | bytes 1572872 | tf_op jit(solution)/shard_map/ppermute | solution.py:30
  173.0 16.3 %copy-start.3 = (bf16[512,1536]{1,0:T(8,128)(2,1)}, bf16[512,1536]{1,0:T(8,128)(2,1)S(1)}, u32[]{:S(2)}) copy-start(bf16[512,1536]{1,0:T(8,128)(2,1)S(1)} %collective-permute-done.19.mine_sib) | copy-start | bytes 4718596
  189.3 19.7 %copy-start.19 = (bf16[512,512]{1,0:T(8,128)(2,1)S(1)}, bf16[512,512]{1,0:T(8,128)(2,1)}, u32[]{:S(2)}) copy-start(bf16[512,512]{1,0:T(8,128)(2,1)} %get-tuple-element.93) | copy-start | bytes 1572868
  189.3 7.7 %collective-permute-start.22 = (bf16[48,2176]{1,0:T(8,128)(2,1)S(1)}, bf16[48,2176]{1,0:T(8,128)(2,1)S(1)}, u32[]{:S(2)}, u32[]{:S(2)}) collective-permute-start(bf16[48,2176]{1,0:T(8,128)(2,1)S(1)} %get-tuple-element.91), channel_id=1, source_target_pairs={{0,224},{32,0},{64,32},{96,64},{128,96},{160,128},{192,160},{224,1... | collective-permute-start | bytes 626696 | tf_op jit(solution)/shard_map/ppermute | solution.py:302
  190.9 9.0 %collective-permute-start.26 = (bf16[48,2176]{1,0:T(8,128)(2,1)S(1)}, bf16[48,2176]{1,0:T(8,128)(2,1)S(1)}, u32[]{:S(2)}, u32[]{:S(2)}) collective-permute-start(bf16[48,2176]{1,0:T(8,128)(2,1)S(1)} %get-tuple-element.98), channel_id=1, source_target_pairs={{0,32},{32,64},{64,96},{96,128},{128,160},{160,192},{192,224},{224... | collective-permute-start | bytes 626696 | tf_op jit(solution)/shard_map/ppermute | solution.py:308
  197.1 7.7 %collective-permute-start.23 = (bf16[48,2176]{1,0:T(8,128)(2,1)S(1)}, bf16[48,2176]{1,0:T(8,128)(2,1)S(1)}, u32[]{:S(2)}, u32[]{:S(2)}) collective-permute-start(bf16[48,2176]{1,0:T(8,128)(2,1)S(1)} %fusion.4), channel_id=1, source_target_pairs={{0,224},{32,0},{64,32},{96,64},{128,96},{160,128},{192,160},{224,1... | collective-permute-start | bytes 626696 | tf_op jit(solution)/shard_map/ppermute | solution.py:307
  204.9 8.7 %collective-permute-start.27 = (bf16[48,2176]{1,0:T(8,128)(2,1)S(1)}, bf16[48,2176]{1,0:T(8,128)(2,1)S(1)}, u32[]{:S(2)}, u32[]{:S(2)}) collective-permute-start(bf16[48,2176]{1,0:T(8,128)(2,1)S(1)} %get-tuple-element.101), channel_id=1, source_target_pairs={{0,32},{32,64},{64,96},{96,128},{128,160},{160,192},{192,224},{224... | collective-permute-start | bytes 626696 | tf_op jit(solution)/shard_map/ppermute | solution.py:308
  205.3 8.3 %collective-permute-start.24 = (bf16[48,2176]{1,0:T(8,128)(2,1)S(1)}, bf16[48,2176]{1,0:T(8,128)(2,1)S(1)}, u32[]{:S(2)}, u32[]{:S(2)}) collective-permute-start(bf16[48,2176]{1,0:T(8,128)(2,1)S(1)} %get-tuple-element.102), channel_id=1, source_target_pairs={{0,224},{32,0},{64,32},{96,64},{128,96},{160,128},{192,160},{224,1... | collective-permute-start | bytes 626696 | tf_op jit(solution)/shard_map/ppermute | solution.py:307
  209.0 16.1 %collective-permute-start.29 = (bf16[512,512]{1,0:T(8,128)(2,1)S(1)}, bf16[512,512]{1,0:T(8,128)(2,1)S(1)}, u32[]{:S(2)}, u32[]{:S(2)}) collective-permute-start(bf16[512,512]{1,0:T(8,128)(2,1)S(1)} %copy-done.19), channel_id=1, source_target_pairs={{0,16},{16,0},{1,17},{17,1},{2,18},{18,2},{3,19},{19,3},{4,20},{20... | collective-permute-start | bytes 1572872 | tf_op jit(solution)/shard_map/ppermute | solution.py:30
  213.7 6.3 %collective-permute-start.25 = (bf16[48,2176]{1,0:T(8,128)(2,1)S(1)}, bf16[48,2176]{1,0:T(8,128)(2,1)S(1)}, u32[]{:S(2)}, u32[]{:S(2)}) collective-permute-start(bf16[48,2176]{1,0:T(8,128)(2,1)S(1)} %get-tuple-element.100), channel_id=1, source_target_pairs={{0,224},{32,0},{64,32},{96,64},{128,96},{160,128},{192,160},{224,1... | collective-permute-start | bytes 626696 | tf_op jit(solution)/shard_map/ppermute | solution.py:307
  216.7 7.3 %collective-permute-start.28 = (bf16[48,2176]{1,0:T(8,128)(2,1)S(1)}, bf16[48,2176]{1,0:T(8,128)(2,1)S(1)}, u32[]{:S(2)}, u32[]{:S(2)}) collective-permute-start(bf16[48,2176]{1,0:T(8,128)(2,1)S(1)} %get-tuple-element.99), channel_id=1, source_target_pairs={{0,32},{32,64},{64,96},{96,128},{128,160},{160,192},{192,224},{224... | collective-permute-start | bytes 626696 | tf_op jit(solution)/shard_map/ppermute | solution.py:308
  225.2 19.6 %copy-start.12 = (bf16[512,512]{1,0:T(8,128)(2,1)}, bf16[512,512]{1,0:T(8,128)(2,1)S(1)}, u32[]{:S(2)}) copy-start(bf16[512,512]{1,0:T(8,128)(2,1)S(1)} %collective-permute-done.29.got) | copy-start | bytes 1572868
  225.2 19.6 %all-to-all-start.6 = ((bf16[8,48,1024]{2,1,0:T(8,128)(2,1)}), bf16[8,48,1024]{2,1,0:T(8,128)(2,1)S(1)}, u32[]{:S(2)}, u32[]{:S(2)}) async-start(bf16[8,48,1024]{2,1,0:T(8,128)(2,1)} %shard_map.100), calls=%async_computation.6 | async-start | bytes 1572864 | tf_op jit(solution)/shard_map/all_to_all | solution.py:286
  228.7 2.0 collective-permute-start.30
  230.7 14.1 %copy-start.13 = (bf16[512,512]{1,0:T(8,128)(2,1)}, bf16[512,512]{1,0:T(8,128)(2,1)S(1)}, u32[]{:S(2)}) copy-start(bf16[512,512]{1,0:T(8,128)(2,1)S(1)} %collective-permute-done.30.got_sib) | copy-start | bytes 1572868
  (10 other events, 24.9 us)

commit v3 on v2

--- a/solution.py
+++ b/solution.py
@@ -60,7 +60,12 @@
             copy = pltpu.make_async_copy(source, held.at[n], in_sems.at[n])
             copy.start()
             coming.append(copy)
-            target = mine.at[:, pl.ds(slot * half, half)] if side else others[slot]
+            if side:
+                target = mine.at[:, pl.ds(slot * half, half)]
+            elif len(others) == 2 and slot < 2:
+                target = others[0].at[:, pl.ds(slot * half, half)]
+            else:
+                target = others[slot - 3]
             going.append(pltpu.make_async_copy(held.at[n], target, out_sems.at[n]))
     for come, go in zip(coming, going):
         come.wait()
@@ -69,14 +74,15 @@
         go.wait()
 
 
-def pack(layer, xl, gate, up, down):
+def pack(layer, xl, gate, up, down, joined):
     _, rows, cols = gate.shape
     half = cols // 2
+    widths = (3, 2, 1) if joined else (3, 1, 1, 1)
     return call(
         functools.partial(pack_kernel, layer),
-        tuple(jax.ShapeDtypeStruct((rows, n * half), BF) for n in (3, 1, 1, 1)),
+        tuple(jax.ShapeDtypeStruct((rows, n * half), BF) for n in widths),
         [SMEM, HBM, HBM, HBM],
-        (HBM,) * 4,
+        (HBM,) * len(widths),
         [
             pltpu.VMEM((6, rows, half), BF),
             pltpu.SemaphoreType.DMA((6,)),
@@ -106,15 +112,18 @@
     return copies
 
 
-def gate_up_kernel(layer, at_ref, x, gains, mine, gate, up, mine_sib, gate_sib, up_sib, out, lead, held, sems):
+def gate_up_kernel(layer, at_ref, x, gains, *refs):
+    *weights, out, lead, held, sems = refs
     xl, far = at_ref[0], at_ref[1]
     width = x.shape[3]
     half = held.shape[2]
     layout = []
-    for core, (own, *others) in enumerate(((mine, gate, up), (mine_sib, gate_sib, up_sib))):
-        for kind, other in enumerate(others):
+    for core in range(2):
+        own, *others = weights[core * len(weights) // 2 : (core + 1) * len(weights) // 2]
+        for kind in range(2):
             slot = 2 * core + kind
-            layout += [(own, kind * half, (slot, 0, 0), half), (other, 0, (slot, width, 0), half)]
+            other, at = (others[kind], 0) if len(others) == 2 else (others[0], kind * half)
+            layout += [(own, kind * half, (slot, 0, 0), half), (other, at, (slot, width, 0), half)]
     copies = fetch(layout, held, sems)
     squares = 0.0
     normed = []
@@ -136,13 +145,13 @@
 
 def gate_up(layer, at, x, gains, weights):
     _, blocks, rows, width = x.shape
-    half = weights[1].shape[1]
+    half = weights[0].shape[1] // 3
     tokens = blocks * rows
     out = jax.ShapeDtypeStruct((blocks, rows, 4 * half + 128), BF)
     return call(
         functools.partial(gate_up_kernel, layer),
         (out, jax.ShapeDtypeStruct(out.shape[1:], BF)),
-        [SMEM, VMEM, VMEM] + [HBM] * 6,
+        [SMEM, VMEM, VMEM] + [HBM] * len(weights),
         (VMEM, VMEM),
         [pltpu.VMEM((4, 2 * width, half), BF), pltpu.SemaphoreType.DMA((8,))],
         flops=16 * tokens * width * half,
@@ -242,28 +251,17 @@
             sent[i] = value
 
 
-def first_kernel(a, b, out, sent):
-    value = add(a[...], b[...]).astype(BF)
+def first_kernel(pieces, out, sent):
+    value = add(*[pieces[i] for i in range(pieces.shape[0])]).astype(BF)
     out[...] = value
     for i in range(sent.shape[0]):
         sent[i] = value
 
 
-def first(a, b):
-    one = jax.ShapeDtypeStruct(a.shape, BF)
-    many = jax.ShapeDtypeStruct((N_PLANE, *a.shape), BF)
-    return call(first_kernel, (one, many), [VMEM] * 2, (VMEM, VMEM), moved=2 * many.size)(a, b)
-
-
-def half_kernel(xh_ref, pieces, kept, given):
-    xh = xh_ref[0]
-    for which, out in ((xh, kept), (1 - xh, given)):
-        out[...] = add(*[pieces[i, which] for i in range(pieces.shape[0])]).astype(BF)
-
-
-def sum_half(xh, pieces):
-    one = jax.ShapeDtypeStruct(pieces.shape[2:], BF)
-    return call(half_kernel, (one, one), [SMEM, VMEM], (VMEM, VMEM), moved=2 * pieces.size)(xh, pieces)
+def first(pieces):
+    one = jax.ShapeDtypeStruct(pieces.shape[1:], BF)
+    many = jax.ShapeDtypeStruct((N_PLANE, *one.shape), BF)
+    return call(first_kernel, (one, many), [VMEM], (VMEM, VMEM), moved=2 * many.size)(pieces)
 
 
 def last_kernel(layer, pieces, x, scale, out):
@@ -314,7 +312,6 @@
 ):
     z, xl, core, xh = (lax.axis_index(axis) for axis in ("z", "xl", "c", "xh"))
     xl_arg = xl.astype(jnp.int32).reshape(1)
-    xh_arg = xh.astype(jnp.int32).reshape(1)
     at_arg = jnp.stack([xl, lax.rem(z + Z // 2, Z)]).astype(jnp.int32)
     owner = lax.axis_index(OWNERS)
     width = norm_gain.shape[1]
@@ -323,62 +320,58 @@
     units = w_gate.shape[2] // 2
     n_owners = SIZES[2] * SIZES[3] * SIZES[4]
 
-    all_ids = exchange(jnp.broadcast_to(token_ids[None], (n_owners, rows)), OWNERS)
+    near = jnp.stack([token_ids, swap(token_ids, "xh")])
+    near = jnp.where(xh == 0, near, near[::-1])
     gains = jnp.stack([norm_gain, swap(norm_gain, "xl")], 1)
     scales = lax.dynamic_slice_in_dim(jnp.stack([gate_scale, up_scale], 1), xl * units, units, 2)
     scales = jnp.stack([scales, swap(scales, "c")], 1)
 
-    mine, other = [None] * LAYERS, [None] * LAYERS
-    mine[0], *other[0] = pack(0, xl_arg, w_gate, w_up, w_down)
-    mine_sib = [swap(mine[0], "c"), None]
-    got = [[None] * 3 for _ in range(LAYERS)]
-    sib = [[None] * 3 for _ in range(LAYERS)]
-    got[0][0] = swap(other[0][0], "xl")
+    mine, mine_sib = [None] * LAYERS, [None] * LAYERS
+    mine[0], g_out, u_out, d_out = pack(0, xl_arg, w_gate, w_up, w_down, False)
+    near, g_out, gains = together(near, g_out, gains)
+    g_got = swap(g_out, "xl")
+    all_ids = exchange(jnp.broadcast_to(near[None], (n_owners // 2, 2, rows)), ("c", "y"))
+    all_ids = all_ids.reshape(2, -1, 2, rows).transpose(0, 2, 1, 3).reshape(-1)
 
     vocab_rows = embed_table.shape[0]
     local_ids = all_ids - owner * vocab_rows
-    local_ids = local_ids.reshape(*SIZES[2:], rows).transpose(0, 2, 1, 3).reshape(-1)
     inside = (local_ids >= 0) & (local_ids < vocab_rows)
     local_ids = jnp.clip(local_ids, 0, vocab_rows - 1)
+    local_ids, g_got = together(local_ids, g_got)
+    u_got = swap(u_out, "xl")
     picked = embed_table.at[local_ids].get(mode="promise_in_bounds")
-    picked = jnp.where(inside[:, None], picked, jnp.zeros((), BF))
-    picked, got[0][0], other[0][1], mine_sib[0], gains = together(
-        picked, got[0][0], other[0][1], mine_sib[0], gains
+    picked = jnp.where(inside[:, None], picked, jnp.zeros((), BF)).reshape(2, -1, rows, width)
+    picked, u_got = together(picked, u_got)
+    kept = lax.dynamic_index_in_dim(picked, core, 0, keepdims=False)
+    given = swap(lax.dynamic_index_in_dim(picked, 1 - core, 0, keepdims=False), "c")
+    both = add(kept, given).astype(BF)
+    both, g_got, u_got, later = together(both, g_got, u_got, mine[0])
+    mine_sib[0], g_sib, u_sib = swap(later, "c"), swap(g_got, "c"), swap(u_got, "c")
+    pieces = exchange(both, ("xh", "y"))
+    mine[1], gu_out, last_out = pack(1, xl_arg, *after(both, w_gate, w_up, w_down), True)
+    pieces, mine_sib[0], g_sib, u_sib, mine[1], gu_out, last_out = together(
+        pieces, mine_sib[0], g_sib, u_sib, mine[1], gu_out, last_out
     )
-    got[0][1] = swap(other[0][1], "xl")
-    pieces = exchange(picked.reshape(-1, rows, width), ("c", "y"))
-    pieces = pieces.reshape(-1, SIZES[3], rows, width)
-    mine[1], *other[1] = pack(1, xl_arg, *after(got[0][0], w_gate, w_up, w_down))
-    pieces, got[0][1], mine[1], *other[1] = together(pieces, got[0][1], mine[1], *other[1])
-    kept, given = sum_half(xh_arg, pieces)
-    x, sent = first(kept, swap(given, "xh"))
-    sib[0][0] = swap(got[0][0], "c")
-    sib[0][1] = swap(got[0][1], "c")
+    x, sent = first(pieces)
+    others, others_sib = (g_got, u_got), (g_sib, u_sib)
     mine_sib[1] = swap(after(x, mine[1]), "c")
 
     for layer in range(LAYERS):
         everyone = exchange(sent, PLANE).reshape(2, -1, rows, width)
-        weights = (mine[layer], *got[layer][:2], mine_sib[layer], *sib[layer][:2])
+        weights = (mine[layer], *others, mine_sib[layer], *others_sib)
         parts, lead = gate_up(layer, at_arg, everyone, gains, weights)
-        lead, other[layer][2] = together(lead, other[layer][2])
-        got[layer][2] = swap(other[layer][2], "xl")
-        terms = scatter_sum_z(parts, lead, z)
-        act = activate(layer, width_total, terms, scales)
+        lead, begun = together(lead, d_out if layer == 0 else last_out)
+        down = swap(begun, "xl")
+        act = activate(layer, width_total, scatter_sum_z(parts, lead, z), scales)
+        act, down, gu_out = together(act, down, gu_out)
+        down_sib = swap(down, "c")
         if layer == 0:
-            act, got[0][2], other[1][0], other[1][1] = together(
-                act, got[0][2], other[1][0], other[1][1]
-            )
-            sib[0][2] = swap(got[0][2], "c")
-            got[1][:2] = [swap(other[1][n], "xl") for n in range(2)]
-        else:
-            act, got[1][2] = together(act, got[1][2])
-            sib[1][2] = swap(got[1][2], "c")
+            gu_got = swap(gu_out, "xl")
         act = exchange(act, "z")
         if layer == 0:
-            act, got[1][0], got[1][1] = together(act, got[1][0], got[1][1])
-            sib[1][:2] = [swap(got[1][n], "c") for n in range(2)]
-        weights = (mine[layer], got[layer][2], mine_sib[layer], sib[layer][2])
-        terms = project(xl_arg, act, weights)
+            act, gu_got = together(act, gu_got)
+            others, others_sib = (gu_got,), (swap(gu_got, "c"),)
+        terms = project(xl_arg, act, (mine[layer], down, mine_sib[layer], down_sib))
         pieces = exchange(terms.reshape(N_PLANE, rows, width), PLANE)
         x, sent = update(layer, pieces, x, down_scale)
     return x

time: 270 us -> 262 us (0.970)
  blocking collectives: 34.3 us -> 15.6 us
  waiting for transfers between devices: 110 us -> 121 us
    all_to_all x6 -> x7, waiting for transfers between devices: 33.8 us -> 56.8 us  [exchange(): return lax.all_to_all(value, axes, 0, 0, tiled=True)]
    all_to_all x2 -> x1, blocking collectives: 34.3 us -> 15.6 us  [exchange(): return lax.all_to_all(value, axes, 0, 0, tiled=True)]
    ppermute x17 -> x16, waiting for transfers between devices: 39.4 us -> 31 us  [swap(): return lax.ppermute(value, axis, turn(2, 1))]
    unnamed x42 -> x38, local copies, waits for them, and re-layouts: 6.3 us -> 3.73 us
    all_to_all x6 -> x7, starting transfers between devices: 33.5 us -> 34.8 us  [exchange(): return lax.all_to_all(value, axes, 0, 0, tiled=True)]
    ppermute x17 -> x16, starting transfers between devices: 13 us -> 13.1 us  [swap(): return lax.ppermute(value, axis, turn(2, 1))]
  transfers between devices with their start and end apart: 37 -> 37, of which waited for: 22 -> 21; matrix products, arithmetic and copies ran while one was open for 3% -> 4% of each run, Pallas kernels for 4% -> 5%
where the time goes in v3:
time: 262 us; the launch traced here: 261 us
  waiting for transfers between devices  121 us (46%)
  starting transfers between devices  78.3 us (30%)
  Pallas kernels  29.4 us (11%)
  blocking collectives  15.6 us (6%)
  local copies, waits for them, and re-layouts  11.2 us (4%)
  other arithmetic  4.96 us (2%)
    all_to_all x7, waiting for transfers between devices, exchange(): return lax.all_to_all(value, axes, 0, 0, tiled=True)  56.8 us
    all_to_all x7, starting transfers between devices, exchange(): return lax.all_to_all(value, axes, 0, 0, tiled=True)  34.8 us
    ppermute x16, waiting for transfers between devices, swap(): return lax.ppermute(value, axis, turn(2, 1))  31 us
    ppermute x6, starting transfers between devices, scatter_sum_z(): down = lax.ppermute(down, 'z', turn(Z, -1))  20 us
    all_to_all x1, blocking collectives, exchange(): return lax.all_to_all(value, axes, 0, 0, tiled=True)  15.6 us
    ppermute x6, waiting for transfers between devices, scatter_sum_z(): down = lax.ppermute(down, 'z', turn(Z, -1))  13.9 us
    ppermute x16, starting transfers between devices, swap(): return lax.ppermute(value, axis, turn(2, 1))  13.1 us
    ppermute x6, waiting for transfers between devices, scatter_sum_z(): up = lax.ppermute(up, 'z', turn(Z, 1))  12.1 us
  transfers between devices with their start and end apart: 37, of which 21 were waited for; matrix products, arithmetic and copies ran while one was open for 4% of the time, Pallas kernels for 5%

profile of v3, /device:TPU:2, one launch (start us, length us, event | category | flops | bytes accessed | tf_op | source)
XLA Modules:
  0.0 260.9 jit_solution(2994421903070259724)
XLA Ops:
  0.0 2.1 collective-permute-start
  4.3 2.9 %shard_map.91 = (bf16[512,1536]{1,0:T(8,128)(2,1)}, bf16[512,512]{1,0:T(8,128)(2,1)}, bf16[512,512]{1,0:T(8,128)(2,1)}, bf16[512,512]{1,0:T(8,128)(2,1)}) custom-call(s32[1]{0:T(128)} %bitcast.xl_ref, bf16[2,512,1024]{2,1,0:T(8,128)(2,1)} %gate.2, bf16[2,512,1024]{2,1,0:T(8,128)(2,1)} %up.2, bf16[2,1024,512]{2,1,0:T(8,128)(2,1)} %down.2), custom_call_target="tpu_custom_call" | custom-call | bytes 6291456 | tf_op jit(solution)/shard_map/pallas_call | solution.py:81
  8.5 4.5 %all-to-all-start = ((s32[8,2,48]{2,1,0:T(2,128)}), s32[8,2,48]{2,1,0:T(2,128)S(1)}, u32[]{:S(2)}, u32[]{:S(2)}) async-start(s32[8,2,48]{2,1,0:T(2,128)} %broadcast_in_dim.22), calls=%async_computation | async-start | bytes 16384 | tf_op jit(solution)/shard_map/all_to_all | solution.py:284
  14.4 3.8 %all-to-all-done = s32[8,2,48]{2,1,0:T(2,128)S(1)} async-done(((s32[8,2,48]{2,1,0:T(2,128)}), s32[8,2,48]{2,1,0:T(2,128)S(1)}, u32[]{:S(2)}, u32[]{:S(2)}) %all-to-all-start) | async-done | bytes 3104 | tf_op jit(solution)/shard_map/all_to_all | solution.py:284
  18.4 4.0 %collective-permute-done.2.refs_1_ = bf16[512,512]{1,0:T(8,128)(2,1)S(1)} collective-permute-done((bf16[512,512]{1,0:T(8,128)(2,1)}, bf16[512,512]{1,0:T(8,128)(2,1)S(1)}, u32[]{:S(2)}, u32[]{:S(2)}) %collective-permute-start.2) | collective-permute-done | bytes 524320 | tf_op jit(solution)/shard_map/ppermute | solution.py:30
  22.4 5.9 %gather_fusion = bf16[768,512]{1,0:T(8,128)(2,1)S(1)} fusion(bf16[4752,512]{1,0:T(8,128)(2,1)} %param.10, s32[1024]{0:T(1024)S(1)} %pad_clamp_fusion), kind=kCustom, calls=%fused_computation | custom fusion | bytes 1575936 | tf_op jit(solution)/shard_map/gather | solution.py:342
  28.6 3.3 %collective-permute-done.3.refs_2_ = bf16[512,512]{1,0:T(8,128)(2,1)S(1)} collective-permute-done((bf16[512,512]{1,0:T(8,128)(2,1)}, bf16[512,512]{1,0:T(8,128)(2,1)S(1)}, u32[]{:S(2)}, u32[]{:S(2)}) %collective-permute-start.3) | collective-permute-done | bytes 524320 | tf_op jit(solution)/shard_map/ppermute | solution.py:30
  33.7 1.9 fusion
  36.3 4.5 %all-to-all-start.1 = ((bf16[8,48,512]{2,1,0:T(8,128)(2,1)}), bf16[8,48,512]{2,1,0:T(8,128)(2,1)S(1)}, u32[]{:S(2)}, u32[]{:S(2)}) async-start(bf16[8,48,512]{2,1,0:T(8,128)(2,1)} %fusion), calls=%async_computation.1 | async-start | bytes 786432 | tf_op jit(solution)/shard_map/all_to_all | solution.py:284
  40.7 2.9 %shard_map.92 = (bf16[512,1536]{1,0:T(8,128)(2,1)}, bf16[512,1024]{1,0:T(8,128)(2,1)}, bf16[512,512]{1,0:T(8,128)(2,1)}) custom-call(s32[1]{0:T(128)} %bitcast.xl_ref, bf16[2,512,1024]{2,1,0:T(8,128)(2,1)} %gate.2, bf16[2,512,1024]{2,1,0:T(8,128)(2,1)} %up.2, bf16[2,1024,512]{2,1,0:T(8,128)(2,1)} %down.2), custom_call_target="tpu_custom_call" | custom-call | bytes 6291456 | tf_op jit(solution)/shard_map/pallas_call | solution.py:81
  43.6 7.3 %all-to-all-done.1.pieces = bf16[8,48,512]{2,1,0:T(8,128)(2,1)S(1)} async-done(((bf16[8,48,512]{2,1,0:T(8,128)(2,1)}), bf16[8,48,512]{2,1,0:T(8,128)(2,1)S(1)}, u32[]{:S(2)}, u32[]{:S(2)}) %all-to-all-start.1) | async-done | bytes 393248 | tf_op jit(solution)/shard_map/all_to_all | solution.py:284
  51.7 2.0 shard_map.93
  53.6 6.1 %all-to-all-start.2 = ((bf16[16,48,512]{2,1,0:T(8,128)(2,1)}), bf16[16,48,512]{2,1,0:T(8,128)(2,1)}, u32[]{:S(2)}, u32[]{:S(2)}) async-start(bf16[16,48,512]{2,1,0:T(8,128)(2,1)} %get-tuple-element.73), calls=%async_computation.2 | async-start | bytes 1572864 | tf_op jit(solution)/shard_map/all_to_all | solution.py:284
  59.8 11.9 %all-to-all-done.2 = bf16[16,48,512]{2,1,0:T(8,128)(2,1)} async-done(((bf16[16,48,512]{2,1,0:T(8,128)(2,1)}), bf16[16,48,512]{2,1,0:T(8,128)(2,1)}, u32[]{:S(2)}, u32[]{:S(2)}) %all-to-all-start.2) | async-done | bytes 786464 | tf_op jit(solution)/shard_map/all_to_all | solution.py:284
  73.8 4.0 %shard_map.94 = (bf16[8,48,2176]{2,1,0:T(8,128)(2,1)S(1)}, bf16[48,2176]{1,0:T(8,128)(2,1)S(1)}) custom-call(s32[2]{0:T(128)S(1)} %pad_add_fusion.1.at_ref, bf16[2,8,48,512]{3,2,1,0:T(8,128)(2,1)} %bitcast.12.x, f32[2,2,512]{2,1,0:T(2,128)S(1)} %pad_maximum_fusion.1.gains, bf16[512,1536]{1,0:T(8,128)(2,1)S(1)} %copy-done.1, bf16[512,512]{1,0:T(8,128)(2,1)S(1)} %copy-done.6, ...), custom_call_target="tpu_custom_call" | custom-call | flops 1610612736 | bytes 6553600 | tf_op jit(solution)/shard_map/pallas_call | solution.py:151
  77.9 5.9 %collective-permute-start.8 = (bf16[48,2176]{1,0:T(8,128)(2,1)S(1)}, bf16[48,2176]{1,0:T(8,128)(2,1)S(1)}, u32[]{:S(2)}, u32[]{:S(2)}) collective-permute-start(bf16[48,2176]{1,0:T(8,128)(2,1)S(1)} %get-tuple-element.80), channel_id=1, source_target_pairs={{0,224},{32,0},{64,32},{96,64},{128,96},{160,128},{192,160},{224,1... | collective-permute-start | bytes 626696 | tf_op jit(solution)/shard_map/ppermute | solution.py:300
  83.9 3.2 %collective-permute-done.8 = bf16[48,2176]{1,0:T(8,128)(2,1)S(1)} collective-permute-done((bf16[48,2176]{1,0:T(8,128)(2,1)S(1)}, bf16[48,2176]{1,0:T(8,128)(2,1)S(1)}, u32[]{:S(2)}, u32[]{:S(2)}) %collective-permute-start.8) | collective-permute-done | bytes 208928 | tf_op jit(solution)/shard_map/ppermute | solution.py:300
  87.2 3.8 %collective-permute-start.9 = (bf16[48,2176]{1,0:T(8,128)(2,1)S(1)}, bf16[48,2176]{1,0:T(8,128)(2,1)S(1)}, u32[]{:S(2)}, u32[]{:S(2)}) collective-permute-start(bf16[48,2176]{1,0:T(8,128)(2,1)S(1)} %fusion.10), channel_id=1, source_target_pairs={{0,224},{32,0},{64,32},{96,64},{128,96},{160,128},{192,160},{224,1... | collective-permute-start | bytes 626696 | tf_op jit(solution)/shard_map/ppermute | solution.py:305
  91.0 3.3 %collective-permute-done.9 = bf16[48,2176]{1,0:T(8,128)(2,1)S(1)} collective-permute-done((bf16[48,2176]{1,0:T(8,128)(2,1)S(1)}, bf16[48,2176]{1,0:T(8,128)(2,1)S(1)}, u32[]{:S(2)}, u32[]{:S(2)}) %collective-permute-start.9) | collective-permute-done | bytes 208928 | tf_op jit(solution)/shard_map/ppermute | solution.py:305
  95.5 3.9 %collective-permute-start.10 = (bf16[48,2176]{1,0:T(8,128)(2,1)S(1)}, bf16[48,2176]{1,0:T(8,128)(2,1)S(1)}, u32[]{:S(2)}, u32[]{:S(2)}) collective-permute-start(bf16[48,2176]{1,0:T(8,128)(2,1)S(1)} %get-tuple-element.112), channel_id=1, source_target_pairs={{0,224},{32,0},{64,32},{96,64},{128,96},{160,128},{192,160},{224,1... | collective-permute-start | bytes 626696 | tf_op jit(solution)/shard_map/ppermute | solution.py:305
  99.7 1.8 collective-permute-start.16
  104.1 3.6 %collective-permute-start.11 = (bf16[48,2176]{1,0:T(8,128)(2,1)S(1)}, bf16[48,2176]{1,0:T(8,128)(2,1)S(1)}, u32[]{:S(2)}, u32[]{:S(2)}) collective-permute-start(bf16[48,2176]{1,0:T(8,128)(2,1)S(1)} %get-tuple-element.110), channel_id=1, source_target_pairs={{0,224},{32,0},{64,32},{96,64},{128,96},{160,128},{192,160},{224,1... | collective-permute-start | bytes 626696 | tf_op jit(solution)/shard_map/ppermute | solution.py:305
  107.8 3.2 %collective-permute-done.11.a = bf16[48,2176]{1,0:T(8,128)(2,1)S(1)} collective-permute-done((bf16[48,2176]{1,0:T(8,128)(2,1)S(1)}, bf16[48,2176]{1,0:T(8,128)(2,1)S(1)}, u32[]{:S(2)}, u32[]{:S(2)}) %collective-permute-start.11) | collective-permute-done | bytes 208928 | tf_op jit(solution)/shard_map/ppermute | solution.py:305
  111.0 3.7 %collective-permute-done.14.b = bf16[48,2176]{1,0:T(8,128)(2,1)S(1)} collective-permute-done((bf16[48,2176]{1,0:T(8,128)(2,1)S(1)}, bf16[48,2176]{1,0:T(8,128)(2,1)S(1)}, u32[]{:S(2)}, u32[]{:S(2)}) %collective-permute-start.14) | collective-permute-done | bytes 208928 | tf_op jit(solution)/shard_map/ppermute | solution.py:306
  115.8 4.2 %all-to-all-start.3 = ((bf16[8,48,1024]{2,1,0:T(8,128)(2,1)}), bf16[8,48,1024]{2,1,0:T(8,128)(2,1)}, u32[]{:S(2)}, u32[]{:S(2)}) async-start(bf16[8,48,1024]{2,1,0:T(8,128)(2,1)} %shard_map.95), calls=%async_computation.3 | async-start | bytes 1572864 | tf_op jit(solution)/shard_map/all_to_all | solution.py:284
  120.0 3.0 %collective-permute-start.17 = (bf16[512,1024]{1,0:T(8,128)(2,1)}, bf16[512,1024]{1,0:T(8,128)(2,1)}, u32[]{:S(2)}, u32[]{:S(2)}) collective-permute-start(bf16[512,1024]{1,0:T(8,128)(2,1)} %get-tuple-element.85), channel_id=1, source_target_pairs={{0,16},{16,0},{1,17},{17,1},{2,18},{18,2},{3,19},{19,3},{4,20},{20... | collective-permute-start | bytes 3145736 | tf_op jit(solution)/shard_map/ppermute | solution.py:30
  123.5 20.0 %collective-permute-done.17.refs_1_ = bf16[512,1024]{1,0:T(8,128)(2,1)} collective-permute-done((bf16[512,1024]{1,0:T(8,128)(2,1)}, bf16[512,1024]{1,0:T(8,128)(2,1)}, u32[]{:S(2)}, u32[]{:S(2)}) %collective-permute-start.17) | collective-permute-done | bytes 1048608 | tf_op jit(solution)/shard_map/ppermute | solution.py:30
  143.5 3.4 %shard_map.96 = bf16[2,8,48,512]{3,2,1,0:T(8,128)(2,1)} custom-call(s32[1]{0:T(128)} %bitcast.xl_ref, bf16[8,48,1024]{2,1,0:T(8,128)(2,1)} %all-to-all-done.3.act, bf16[512,1536]{1,0:T(8,128)(2,1)} %get-tuple-element.63.refs_0_.mine, bf16[512,512]{1,0:T(8,128)(2,1)} %collective-permute-done.16.got, bf16[512,1536]{1,0:T(8,128)(2,1)} %copy-done.2, ...), custom_call_target="tpu_custom_call" | custom-call | flops 805306368 | bytes 3670016 | tf_op jit(solution)/shard_map/pallas_call | solution.py:229
  146.9 5.6 %all-to-all-start.4 = ((bf16[16,48,512]{2,1,0:T(8,128)(2,1)}), bf16[16,48,512]{2,1,0:T(8,128)(2,1)}, u32[]{:S(2)}, u32[]{:S(2)}) async-start(bf16[16,48,512]{2,1,0:T(8,128)(2,1)} %bitcast.64), calls=%async_computation.4 | async-start | bytes 1572864 | tf_op jit(solution)/shard_map/all_to_all | solution.py:284
  152.5 9.8 %all-to-all-done.4.pieces = bf16[16,48,512]{2,1,0:T(8,128)(2,1)} async-done(((bf16[16,48,512]{2,1,0:T(8,128)(2,1)}), bf16[16,48,512]{2,1,0:T(8,128)(2,1)}, u32[]{:S(2)}, u32[]{:S(2)}) %all-to-all-start.4) | async-done | bytes 786464 | tf_op jit(solution)/shard_map/all_to_all | solution.py:284
  162.3 2.2 shard_map.97
  164.5 5.5 %all-to-all-start.5 = ((bf16[16,48,512]{2,1,0:T(8,128)(2,1)}), bf16[16,48,512]{2,1,0:T(8,128)(2,1)}, u32[]{:S(2)}, u32[]{:S(2)}) async-start(bf16[16,48,512]{2,1,0:T(8,128)(2,1)} %get-tuple-element.89), calls=%async_computation.5 | async-start | bytes 1572864 | tf_op jit(solution)/shard_map/all_to_all | solution.py:284
  170.0 9.8 %all-to-all-done.5 = bf16[16,48,512]{2,1,0:T(8,128)(2,1)} async-done(((bf16[16,48,512]{2,1,0:T(8,128)(2,1)}), bf16[16,48,512]{2,1,0:T(8,128)(2,1)}, u32[]{:S(2)}, u32[]{:S(2)}) %all-to-all-start.5) | async-done | bytes 786464 | tf_op jit(solution)/shard_map/all_to_all | solution.py:284
  179.8 4.6 %shard_map.98 = (bf16[8,48,2176]{2,1,0:T(8,128)(2,1)S(1)}, bf16[48,2176]{1,0:T(8,128)(2,1)S(1)}) custom-call(s32[2]{0:T(128)S(1)} %pad_add_fusion.1.at_ref, bf16[2,8,48,512]{3,2,1,0:T(8,128)(2,1)} %bitcast.23.x, f32[2,2,512]{2,1,0:T(2,128)S(1)} %pad_maximum_fusion.1.gains, bf16[512,1536]{1,0:T(8,128)(2,1)S(1)} %copy-done, ...), custom_call_target="tpu_custom_call" | custom-call | flops 1610612736 | bytes 6553600 | tf_op jit(solution)/shard_map/pallas_call | solution.py:151
  184.4 3.0 %collective-permute-start.21 = (bf16[48,2176]{1,0:T(8,128)(2,1)S(1)}, bf16[48,2176]{1,0:T(8,128)(2,1)S(1)}, u32[]{:S(2)}, u32[]{:S(2)}) collective-permute-start(bf16[48,2176]{1,0:T(8,128)(2,1)S(1)} %get-tuple-element.95), channel_id=1, source_target_pairs={{0,224},{32,0},{64,32},{96,64},{128,96},{160,128},{192,160},{224,1... | collective-permute-start | bytes 626696 | tf_op jit(solution)/shard_map/ppermute | solution.py:300
  187.5 4.0 %collective-permute-done.21 = bf16[48,2176]{1,0:T(8,128)(2,1)S(1)} collective-permute-done((bf16[48,2176]{1,0:T(8,128)(2,1)S(1)}, bf16[48,2176]{1,0:T(8,128)(2,1)S(1)}, u32[]{:S(2)}, u32[]{:S(2)}) %collective-permute-start.21) | collective-permute-done | bytes 208928 | tf_op jit(solution)/shard_map/ppermute | solution.py:300
  191.6 3.8 %collective-permute-start.22 = (bf16[48,2176]{1,0:T(8,128)(2,1)S(1)}, bf16[48,2176]{1,0:T(8,128)(2,1)S(1)}, u32[]{:S(2)}, u32[]{:S(2)}) collective-permute-start(bf16[48,2176]{1,0:T(8,128)(2,1)S(1)} %fusion.5), channel_id=1, source_target_pairs={{0,224},{32,0},{64,32},{96,64},{128,96},{160,128},{192,160},{224,1... | collective-permute-start | bytes 626696 | tf_op jit(solution)/shard_map/ppermute | solution.py:305
  195.4 3.6 %collective-permute-done.22 = bf16[48,2176]{1,0:T(8,128)(2,1)S(1)} collective-permute-done((bf16[48,2176]{1,0:T(8,128)(2,1)S(1)}, bf16[48,2176]{1,0:T(8,128)(2,1)S(1)}, u32[]{:S(2)}, u32[]{:S(2)}) %collective-permute-start.22) | collective-permute-done | bytes 208928 | tf_op jit(solution)/shard_map/ppermute | solution.py:305
  199.8 3.4 %collective-permute-start.23 = (bf16[48,2176]{1,0:T(8,128)(2,1)S(1)}, bf16[48,2176]{1,0:T(8,128)(2,1)S(1)}, u32[]{:S(2)}, u32[]{:S(2)}) collective-permute-start(bf16[48,2176]{1,0:T(8,128)(2,1)S(1)} %get-tuple-element.106), channel_id=1, source_target_pairs={{0,224},{32,0},{64,32},{96,64},{128,96},{160,128},{192,160},{224,1... | collective-permute-start | bytes 626696 | tf_op jit(solution)/shard_map/ppermute | solution.py:305
  204.6 4.2 %collective-permute-done.26 = bf16[48,2176]{1,0:T(8,128)(2,1)S(1)} collective-permute-done((bf16[48,2176]{1,0:T(8,128)(2,1)S(1)}, bf16[48,2176]{1,0:T(8,128)(2,1)S(1)}, u32[]{:S(2)}, u32[]{:S(2)}) %collective-permute-start.26) | collective-permute-done | bytes 208928 | tf_op jit(solution)/shard_map/ppermute | solution.py:306
  211.1 3.8 %collective-permute-done.24.a = bf16[48,2176]{1,0:T(8,128)(2,1)S(1)} collective-permute-done((bf16[48,2176]{1,0:T(8,128)(2,1)S(1)}, bf16[48,2176]{1,0:T(8,128)(2,1)S(1)}, u32[]{:S(2)}, u32[]{:S(2)}) %collective-permute-start.24) | collective-permute-done | bytes 208928 | tf_op jit(solution)/shard_map/ppermute | solution.py:305
  214.8 2.6 %collective-permute-done.27.b = bf16[48,2176]{1,0:T(8,128)(2,1)S(1)} collective-permute-done((bf16[48,2176]{1,0:T(8,128)(2,1)S(1)}, bf16[48,2176]{1,0:T(8,128)(2,1)S(1)}, u32[]{:S(2)}, u32[]{:S(2)}) %collective-permute-start.27) | collective-permute-done | bytes 208928 | tf_op jit(solution)/shard_map/ppermute | solution.py:306
  218.6 4.4 %all-to-all-start.6 = ((bf16[8,48,1024]{2,1,0:T(8,128)(2,1)}), bf16[8,48,1024]{2,1,0:T(8,128)(2,1)S(1)}, u32[]{:S(2)}, u32[]{:S(2)}) async-start(bf16[8,48,1024]{2,1,0:T(8,128)(2,1)} %shard_map.99), calls=%async_computation.6 | async-start | bytes 1572864 | tf_op jit(solution)/shard_map/all_to_all | solution.py:284
  223.0 1.9 collective-permute-done.29.got_sib
  224.9 14.2 %all-to-all-done.6.act = bf16[8,48,1024]{2,1,0:T(8,128)(2,1)S(1)} async-done(((bf16[8,48,1024]{2,1,0:T(8,128)(2,1)}), bf16[8,48,1024]{2,1,0:T(8,128)(2,1)S(1)}, u32[]{:S(2)}, u32[]{:S(2)}) %all-to-all-start.6) | async-done | bytes 786464 | tf_op jit(solution)/shard_map/all_to_all | solution.py:284
  240.0 3.4 %shard_map.100 = bf16[2,8,48,512]{3,2,1,0:T(8,128)(2,1)} custom-call(s32[1]{0:T(128)} %bitcast.xl_ref, bf16[8,48,1024]{2,1,0:T(8,128)(2,1)} %copy-done.10, bf16[512,1536]{1,0:T(8,128)(2,1)} %get-tuple-element.92.refs_0_.mine, bf16[512,512]{1,0:T(8,128)(2,1)} %copy-done.12, bf16[512,1536]{1,0:T(8,128)(2,1)} %copy-done.3, bf16[512,512]{1,0:T(8,128)(2,1)} %copy-done.13), custom_call_target="tpu_custom_call" | custom-call | flops 805306368 | bytes 3670016 | tf_op jit(solution)/shard_map/pallas_call | solution.py:229
  243.4 15.6 %all_to_all.40.pieces = bf16[16,48,512]{2,1,0:T(8,128)(2,1)} all-to-all(bf16[16,48,512]{2,1,0:T(8,128)(2,1)} %bitcast.65), channel_id=1, replica_groups=mesh['z'=8,'xl'=2,'c'=2,'xh'=2,'y'=4] {'xl','xh','y'}, dimensions={0} | all-to-all | bytes 1572864 | tf_op jit(solution)/shard_map/all_to_all | solution.py:284
  259.0 1.9 shard_map.101
  (108 shorter events, 23.1 us)
Async XLA Ops:
  0.0 7.2 %collective-permute-start = (s32[48]{0:T(128)}, s32[48]{0:T(128)S(1)}, u32[]{:S(2)}, u32[]{:S(2)}) collective-permute-start(s32[48]{0:T(128)} %param.9), channel_id=1, source_target_pairs={{0,4},{4,0},{1,5},{5,1},{2,6},{6,2},{3,7},{7,3},{8,12},{12,8},{9,1... | collective-permute-start | bytes 584 | tf_op jit(solution)/shard_map/ppermute | solution.py:30
  2.1 5.1 %collective-permute-start.1 = (f32[2,512]{1,0:T(2,128)}, f32[2,512]{1,0:T(2,128)S(1)}, u32[]{:S(2)}, u32[]{:S(2)}) collective-permute-start(f32[2,512]{1,0:T(2,128)} %param.11), channel_id=1, source_target_pairs={{0,16},{16,0},{1,17},{17,1},{2,18},{18,2},{3,19},{19,3},{4,20},{20... | collective-permute-start | bytes 12296 | tf_op jit(solution)/shard_map/ppermute | solution.py:30
  7.3 15.2 %collective-permute-start.2 = (bf16[512,512]{1,0:T(8,128)(2,1)}, bf16[512,512]{1,0:T(8,128)(2,1)S(1)}, u32[]{:S(2)}, u32[]{:S(2)}) collective-permute-start(bf16[512,512]{1,0:T(8,128)(2,1)} %get-tuple-element.55), channel_id=1, source_target_pairs={{0,16},{16,0},{1,17},{17,1},{2,18},{18,2},{3,19},{19,3},{4,20},{20... | collective-permute-start | bytes 1572872 | tf_op jit(solution)/shard_map/ppermute | solution.py:30
  8.5 9.7 %all-to-all-start = ((s32[8,2,48]{2,1,0:T(2,128)}), s32[8,2,48]{2,1,0:T(2,128)S(1)}, u32[]{:S(2)}, u32[]{:S(2)}) async-start(s32[8,2,48]{2,1,0:T(2,128)} %broadcast_in_dim.22), calls=%async_computation | async-start | bytes 16384 | tf_op jit(solution)/shard_map/all_to_all | solution.py:284
  13.0 18.9 %collective-permute-start.3 = (bf16[512,512]{1,0:T(8,128)(2,1)}, bf16[512,512]{1,0:T(8,128)(2,1)S(1)}, u32[]{:S(2)}, u32[]{:S(2)}) collective-permute-start(bf16[512,512]{1,0:T(8,128)(2,1)} %get-tuple-element.57), channel_id=1, source_target_pairs={{0,16},{16,0},{1,17},{17,1},{2,18},{18,2},{3,19},{19,3},{4,20},{20... | collective-permute-start | bytes 1572872 | tf_op jit(solution)/shard_map/ppermute | solution.py:30
  28.4 7.2 %copy-start.1 = (bf16[512,1536]{1,0:T(8,128)(2,1)S(1)}, bf16[512,1536]{1,0:T(8,128)(2,1)}, u32[]{:S(2)}) copy-start(bf16[512,1536]{1,0:T(8,128)(2,1)} %get-tuple-element.63.refs_0_.mine) | copy-start | bytes 4718596
  31.9 1.8 collective-permute-start.4
  35.6 15.3 %collective-permute-start.5 = (bf16[512,1536]{1,0:T(8,128)(2,1)S(1)}, bf16[512,1536]{1,0:T(8,128)(2,1)S(1)}, u32[]{:S(2)}, u32[]{:S(2)}) collective-permute-start(bf16[512,1536]{1,0:T(8,128)(2,1)S(1)} %copy-done.1), channel_id=1, source_target_pairs={{0,8},{8,0},{1,9},{9,1},{2,10},{10,2},{3,11},{11,3},{4,12},{12,4},... | collective-permute-start | bytes 4718600 | tf_op jit(solution)/shard_map/ppermute | solution.py:30
  35.7 15.2 %collective-permute-start.6 = (bf16[512,512]{1,0:T(8,128)(2,1)}, bf16[512,512]{1,0:T(8,128)(2,1)}, u32[]{:S(2)}, u32[]{:S(2)}) collective-permute-start(bf16[512,512]{1,0:T(8,128)(2,1)} %copy-done.5), channel_id=1, source_target_pairs={{0,8},{8,0},{1,9},{9,1},{2,10},{10,2},{3,11},{11,3},{4,12},{12,4},... | collective-permute-start | bytes 1572872 | tf_op jit(solution)/shard_map/ppermute | solution.py:30
  36.1 14.8 %collective-permute-start.7 = (bf16[512,512]{1,0:T(8,128)(2,1)}, bf16[512,512]{1,0:T(8,128)(2,1)}, u32[]{:S(2)}, u32[]{:S(2)}) collective-permute-start(bf16[512,512]{1,0:T(8,128)(2,1)} %copy-done.7), channel_id=1, source_target_pairs={{0,8},{8,0},{1,9},{9,1},{2,10},{10,2},{3,11},{11,3},{4,12},{12,4},... | collective-permute-start | bytes 1572872 | tf_op jit(solution)/shard_map/ppermute | solution.py:30
  36.3 14.7 %all-to-all-start.1 = ((bf16[8,48,512]{2,1,0:T(8,128)(2,1)}), bf16[8,48,512]{2,1,0:T(8,128)(2,1)S(1)}, u32[]{:S(2)}, u32[]{:S(2)}) async-start(bf16[8,48,512]{2,1,0:T(8,128)(2,1)} %fusion), calls=%async_computation.1 | async-start | bytes 786432 | tf_op jit(solution)/shard_map/all_to_all | solution.py:284
  50.9 26.9 %copy-start.2 = (bf16[512,1536]{1,0:T(8,128)(2,1)}, bf16[512,1536]{1,0:T(8,128)(2,1)S(1)}, u32[]{:S(2)}) copy-start(bf16[512,1536]{1,0:T(8,128)(2,1)S(1)} %collective-permute-done.5.refs_3_.mine_sib) | copy-start | bytes 4718596
  53.6 18.1 %all-to-all-start.2 = ((bf16[16,48,512]{2,1,0:T(8,128)(2,1)}), bf16[16,48,512]{2,1,0:T(8,128)(2,1)}, u32[]{:S(2)}, u32[]{:S(2)}) async-start(bf16[16,48,512]{2,1,0:T(8,128)(2,1)} %get-tuple-element.73), calls=%async_computation.2 | async-start | bytes 1572864 | tf_op jit(solution)/shard_map/all_to_all | solution.py:284
  77.8 9.3 %copy-start.4 = (bf16[8,48,2176]{2,1,0:T(8,128)(2,1)}, bf16[8,48,2176]{2,1,0:T(8,128)(2,1)S(1)}, u32[]{:S(2)}) copy-start(bf16[8,48,2176]{2,1,0:T(8,128)(2,1)S(1)} %get-tuple-element.81) | copy-start | bytes 5013508
  77.9 21.6 %copy-start.14 = (f32[2,1024]{1,0:T(2,128)S(1)}, f32[2,1024]{1,0:T(2,128)}, u32[]{:S(2)}) copy-start(f32[2,1024]{1,0:T(2,128)} %param.14) | copy-start | bytes 24580
  77.9 21.6 %copy-start.15 = (f32[2,1024]{1,0:T(2,128)S(1)}, f32[2,1024]{1,0:T(2,128)}, u32[]{:S(2)}) copy-start(f32[2,1024]{1,0:T(2,128)} %param.15) | copy-start | bytes 24580
  77.9 21.8 %copy-start.18 = (bf16[512,512]{1,0:T(8,128)(2,1)S(1)}, bf16[512,512]{1,0:T(8,128)(2,1)}, u32[]{:S(2)}) copy-start(bf16[512,512]{1,0:T(8,128)(2,1)} %get-tuple-element.82) | copy-start | bytes 1572868
  77.9 9.3 %collective-permute-start.8 = (bf16[48,2176]{1,0:T(8,128)(2,1)S(1)}, bf16[48,2176]{1,0:T(8,128)(2,1)S(1)}, u32[]{:S(2)}, u32[]{:S(2)}) collective-permute-start(bf16[48,2176]{1,0:T(8,128)(2,1)S(1)} %get-tuple-element.80), channel_id=1, source_target_pairs={{0,224},{32,0},{64,32},{96,64},{128,96},{160,128},{192,160},{224,1... | collective-permute-start | bytes 626696 | tf_op jit(solution)/shard_map/ppermute | solution.py:300
  83.9 7.1 %collective-permute-start.12 = (bf16[48,2176]{1,0:T(8,128)(2,1)S(1)}, bf16[48,2176]{1,0:T(8,128)(2,1)S(1)}, u32[]{:S(2)}, u32[]{:S(2)}) collective-permute-start(bf16[48,2176]{1,0:T(8,128)(2,1)S(1)} %get-tuple-element.108), channel_id=1, source_target_pairs={{0,32},{32,64},{64,96},{96,128},{128,160},{160,192},{192,224},{224... | collective-permute-start | bytes 626696 | tf_op jit(solution)/shard_map/ppermute | solution.py:306
  87.2 7.1 %collective-permute-start.9 = (bf16[48,2176]{1,0:T(8,128)(2,1)S(1)}, bf16[48,2176]{1,0:T(8,128)(2,1)S(1)}, u32[]{:S(2)}, u32[]{:S(2)}) collective-permute-start(bf16[48,2176]{1,0:T(8,128)(2,1)S(1)} %fusion.10), channel_id=1, source_target_pairs={{0,224},{32,0},{64,32},{96,64},{128,96},{160,128},{192,160},{224,1... | collective-permute-start | bytes 626696 | tf_op jit(solution)/shard_map/ppermute | solution.py:305
  95.4 7.5 %collective-permute-start.13 = (bf16[48,2176]{1,0:T(8,128)(2,1)S(1)}, bf16[48,2176]{1,0:T(8,128)(2,1)S(1)}, u32[]{:S(2)}, u32[]{:S(2)}) collective-permute-start(bf16[48,2176]{1,0:T(8,128)(2,1)S(1)} %get-tuple-element.111), channel_id=1, source_target_pairs={{0,32},{32,64},{64,96},{96,128},{128,160},{160,192},{192,224},{224... | collective-permute-start | bytes 626696 | tf_op jit(solution)/shard_map/ppermute | solution.py:306
  95.5 7.5 %collective-permute-start.10 = (bf16[48,2176]{1,0:T(8,128)(2,1)S(1)}, bf16[48,2176]{1,0:T(8,128)(2,1)S(1)}, u32[]{:S(2)}, u32[]{:S(2)}) collective-permute-start(bf16[48,2176]{1,0:T(8,128)(2,1)S(1)} %get-tuple-element.112), channel_id=1, source_target_pairs={{0,224},{32,0},{64,32},{96,64},{128,96},{160,128},{192,160},{224,1... | collective-permute-start | bytes 626696 | tf_op jit(solution)/shard_map/ppermute | solution.py:305
  99.6 8.2 %collective-permute-start.15 = (f32[2,2,512]{2,1,0:T(2,128)S(1)}, f32[2,2,512]{2,1,0:T(2,128)S(1)}, u32[]{:S(2)}, u32[]{:S(2)}) collective-permute-start(f32[2,2,512]{2,1,0:T(2,128)S(1)} %fusion.11), channel_id=1, source_target_pairs={{0,8},{8,0},{1,9},{9,1},{2,10},{10,2},{3,11},{11,3},{4,12},{12,4},... | collective-permute-start | bytes 24584 | tf_op jit(solution)/shard_map/ppermute | solution.py:30
  99.7 16.2 %collective-permute-start.16 = (bf16[512,512]{1,0:T(8,128)(2,1)S(1)}, bf16[512,512]{1,0:T(8,128)(2,1)}, u32[]{:S(2)}, u32[]{:S(2)}) collective-permute-start(bf16[512,512]{1,0:T(8,128)(2,1)S(1)} %copy-done.18), channel_id=1, source_target_pairs={{0,16},{16,0},{1,17},{17,1},{2,18},{18,2},{3,19},{19,3},{4,20},{20... | collective-permute-start | bytes 1572872 | tf_op jit(solution)/shard_map/ppermute | solution.py:30
  104.1 18.9 %copy-start = (bf16[512,1536]{1,0:T(8,128)(2,1)S(1)}, bf16[512,1536]{1,0:T(8,128)(2,1)}, u32[]{:S(2)}) copy-start(bf16[512,1536]{1,0:T(8,128)(2,1)} %get-tuple-element.92.refs_0_.mine) | copy-start | bytes 4718596
  104.1 6.9 %collective-permute-start.11 = (bf16[48,2176]{1,0:T(8,128)(2,1)S(1)}, bf16[48,2176]{1,0:T(8,128)(2,1)S(1)}, u32[]{:S(2)}, u32[]{:S(2)}) collective-permute-start(bf16[48,2176]{1,0:T(8,128)(2,1)S(1)} %get-tuple-element.110), channel_id=1, source_target_pairs={{0,224},{32,0},{64,32},{96,64},{128,96},{160,128},{192,160},{224,1... | collective-permute-start | bytes 626696 | tf_op jit(solution)/shard_map/ppermute | solution.py:305
  107.7 7.0 %collective-permute-start.14 = (bf16[48,2176]{1,0:T(8,128)(2,1)S(1)}, bf16[48,2176]{1,0:T(8,128)(2,1)S(1)}, u32[]{:S(2)}, u32[]{:S(2)}) collective-permute-start(bf16[48,2176]{1,0:T(8,128)(2,1)S(1)} %get-tuple-element.109), channel_id=1, source_target_pairs={{0,32},{32,64},{64,96},{96,128},{128,160},{160,192},{192,224},{224... | collective-permute-start | bytes 626696 | tf_op jit(solution)/shard_map/ppermute | solution.py:306
  115.8 27.6 %all-to-all-start.3 = ((bf16[8,48,1024]{2,1,0:T(8,128)(2,1)}), bf16[8,48,1024]{2,1,0:T(8,128)(2,1)}, u32[]{:S(2)}, u32[]{:S(2)}) async-start(bf16[8,48,1024]{2,1,0:T(8,128)(2,1)} %shard_map.95), calls=%async_computation.3 | async-start | bytes 1572864 | tf_op jit(solution)/shard_map/all_to_all | solution.py:284
  120.0 23.4 %collective-permute-start.17 = (bf16[512,1024]{1,0:T(8,128)(2,1)}, bf16[512,1024]{1,0:T(8,128)(2,1)}, u32[]{:S(2)}, u32[]{:S(2)}) collective-permute-start(bf16[512,1024]{1,0:T(8,128)(2,1)} %get-tuple-element.85), channel_id=1, source_target_pairs={{0,16},{16,0},{1,17},{17,1},{2,18},{18,2},{3,19},{19,3},{4,20},{20... | collective-permute-start | bytes 3145736 | tf_op jit(solution)/shard_map/ppermute | solution.py:30
  123.0 20.5 %collective-permute-start.18 = (bf16[512,512]{1,0:T(8,128)(2,1)}, bf16[512,512]{1,0:T(8,128)(2,1)}, u32[]{:S(2)}, u32[]{:S(2)}) collective-permute-start(bf16[512,512]{1,0:T(8,128)(2,1)} %collective-permute-done.16.got), channel_id=1, source_target_pairs={{0,8},{8,0},{1,9},{9,1},{2,10},{10,2},{3,11},{11,3},{4,12},{12,4},... | collective-permute-start | bytes 1572872 | tf_op jit(solution)/shard_map/ppermute | solution.py:30
  123.0 47.0 %collective-permute-start.19 = (bf16[512,1536]{1,0:T(8,128)(2,1)S(1)}, bf16[512,1536]{1,0:T(8,128)(2,1)S(1)}, u32[]{:S(2)}, u32[]{:S(2)}) collective-permute-start(bf16[512,1536]{1,0:T(8,128)(2,1)S(1)} %copy-done), channel_id=1, source_target_pairs={{0,8},{8,0},{1,9},{9,1},{2,10},{10,2},{3,11},{11,3},{4,12},{12,4},... | collective-permute-start | bytes 4718600 | tf_op jit(solution)/shard_map/ppermute | solution.py:30
  146.9 15.4 %all-to-all-start.4 = ((bf16[16,48,512]{2,1,0:T(8,128)(2,1)}), bf16[16,48,512]{2,1,0:T(8,128)(2,1)}, u32[]{:S(2)}, u32[]{:S(2)}) async-start(bf16[16,48,512]{2,1,0:T(8,128)(2,1)} %bitcast.64), calls=%async_computation.4 | async-start | bytes 1572864 | tf_op jit(solution)/shard_map/all_to_all | solution.py:284
  152.5 17.5 %collective-permute-start.20 = (bf16[512,1024]{1,0:T(8,128)(2,1)}, bf16[512,1024]{1,0:T(8,128)(2,1)}, u32[]{:S(2)}, u32[]{:S(2)}) collective-permute-start(bf16[512,1024]{1,0:T(8,128)(2,1)} %collective-permute-done.17.refs_1_), channel_id=1, source_target_pairs={{0,8},{8,0},{1,9},{9,1},{2,10},{10,2},{3,11},{11,3},{4,12},{12,4},... | collective-permute-start | bytes 3145736 | tf_op jit(solution)/shard_map/ppermute | solution.py:30
  164.5 15.3 %all-to-all-start.5 = ((bf16[16,48,512]{2,1,0:T(8,128)(2,1)}), bf16[16,48,512]{2,1,0:T(8,128)(2,1)}, u32[]{:S(2)}, u32[]{:S(2)}) async-start(bf16[16,48,512]{2,1,0:T(8,128)(2,1)} %get-tuple-element.89), calls=%async_computation.5 | async-start | bytes 1572864 | tf_op jit(solution)/shard_map/all_to_all | solution.py:284
  170.0 14.4 %copy-start.3 = (bf16[512,1536]{1,0:T(8,128)(2,1)}, bf16[512,1536]{1,0:T(8,128)(2,1)S(1)}, u32[]{:S(2)}) copy-start(bf16[512,1536]{1,0:T(8,128)(2,1)S(1)} %collective-permute-done.19.refs_2_.mine_sib) | copy-start | bytes 4718596
  184.4 18.8 %copy-start.17 = (bf16[512,512]{1,0:T(8,128)(2,1)S(1)}, bf16[512,512]{1,0:T(8,128)(2,1)}, u32[]{:S(2)}) copy-start(bf16[512,512]{1,0:T(8,128)(2,1)} %get-tuple-element.97) | copy-start | bytes 1572868
  184.4 7.2 %collective-permute-start.21 = (bf16[48,2176]{1,0:T(8,128)(2,1)S(1)}, bf16[48,2176]{1,0:T(8,128)(2,1)S(1)}, u32[]{:S(2)}, u32[]{:S(2)}) collective-permute-start(bf16[48,2176]{1,0:T(8,128)(2,1)S(1)} %get-tuple-element.95), channel_id=1, source_target_pairs={{0,224},{32,0},{64,32},{96,64},{128,96},{160,128},{192,160},{224,1... | collective-permute-start | bytes 626696 | tf_op jit(solution)/shard_map/ppermute | solution.py:300
  187.4 8.0 %collective-permute-start.25 = (bf16[48,2176]{1,0:T(8,128)(2,1)S(1)}, bf16[48,2176]{1,0:T(8,128)(2,1)S(1)}, u32[]{:S(2)}, u32[]{:S(2)}) collective-permute-start(bf16[48,2176]{1,0:T(8,128)(2,1)S(1)} %get-tuple-element.102), channel_id=1, source_target_pairs={{0,32},{32,64},{64,96},{96,128},{128,160},{160,192},{192,224},{224... | collective-permute-start | bytes 626696 | tf_op jit(solution)/shard_map/ppermute | solution.py:306
  191.6 7.4 %collective-permute-start.22 = (bf16[48,2176]{1,0:T(8,128)(2,1)S(1)}, bf16[48,2176]{1,0:T(8,128)(2,1)S(1)}, u32[]{:S(2)}, u32[]{:S(2)}) collective-permute-start(bf16[48,2176]{1,0:T(8,128)(2,1)S(1)} %fusion.5), channel_id=1, source_target_pairs={{0,224},{32,0},{64,32},{96,64},{128,96},{160,128},{192,160},{224,1... | collective-permute-start | bytes 626696 | tf_op jit(solution)/shard_map/ppermute | solution.py:305
  199.2 9.7 %collective-permute-start.26 = (bf16[48,2176]{1,0:T(8,128)(2,1)S(1)}, bf16[48,2176]{1,0:T(8,128)(2,1)S(1)}, u32[]{:S(2)}, u32[]{:S(2)}) collective-permute-start(bf16[48,2176]{1,0:T(8,128)(2,1)S(1)} %get-tuple-element.105), channel_id=1, source_target_pairs={{0,32},{32,64},{64,96},{96,128},{128,160},{160,192},{192,224},{224... | collective-permute-start | bytes 626696 | tf_op jit(solution)/shard_map/ppermute | solution.py:306
  199.8 9.0 %collective-permute-start.23 = (bf16[48,2176]{1,0:T(8,128)(2,1)S(1)}, bf16[48,2176]{1,0:T(8,128)(2,1)S(1)}, u32[]{:S(2)}, u32[]{:S(2)}) collective-permute-start(bf16[48,2176]{1,0:T(8,128)(2,1)S(1)} %get-tuple-element.106), channel_id=1, source_target_pairs={{0,224},{32,0},{64,32},{96,64},{128,96},{160,128},{192,160},{224,1... | collective-permute-start | bytes 626696 | tf_op jit(solution)/shard_map/ppermute | solution.py:305
  203.2 15.3 %collective-permute-start.28 = (bf16[512,512]{1,0:T(8,128)(2,1)S(1)}, bf16[512,512]{1,0:T(8,128)(2,1)S(1)}, u32[]{:S(2)}, u32[]{:S(2)}) collective-permute-start(bf16[512,512]{1,0:T(8,128)(2,1)S(1)} %copy-done.17), channel_id=1, source_target_pairs={{0,16},{16,0},{1,17},{17,1},{2,18},{18,2},{3,19},{19,3},{4,20},{20... | collective-permute-start | bytes 1572872 | tf_op jit(solution)/shard_map/ppermute | solution.py:30
  208.9 5.9 %collective-permute-start.24 = (bf16[48,2176]{1,0:T(8,128)(2,1)S(1)}, bf16[48,2176]{1,0:T(8,128)(2,1)S(1)}, u32[]{:S(2)}, u32[]{:S(2)}) collective-permute-start(bf16[48,2176]{1,0:T(8,128)(2,1)S(1)} %get-tuple-element.104), channel_id=1, source_target_pairs={{0,224},{32,0},{64,32},{96,64},{128,96},{160,128},{192,160},{224,1... | collective-permute-start | bytes 626696 | tf_op jit(solution)/shard_map/ppermute | solution.py:305
  210.4 7.0 %collective-permute-start.27 = (bf16[48,2176]{1,0:T(8,128)(2,1)S(1)}, bf16[48,2176]{1,0:T(8,128)(2,1)S(1)}, u32[]{:S(2)}, u32[]{:S(2)}) collective-permute-start(bf16[48,2176]{1,0:T(8,128)(2,1)S(1)} %get-tuple-element.103), channel_id=1, source_target_pairs={{0,32},{32,64},{64,96},{96,128},{128,160},{160,192},{192,224},{224... | collective-permute-start | bytes 626696 | tf_op jit(solution)/shard_map/ppermute | solution.py:306
  218.6 20.5 %copy-start.12 = (bf16[512,512]{1,0:T(8,128)(2,1)}, bf16[512,512]{1,0:T(8,128)(2,1)S(1)}, u32[]{:S(2)}) copy-start(bf16[512,512]{1,0:T(8,128)(2,1)S(1)} %collective-permute-done.28.got) | copy-start | bytes 1572868
  218.6 20.5 %all-to-all-start.6 = ((bf16[8,48,1024]{2,1,0:T(8,128)(2,1)}), bf16[8,48,1024]{2,1,0:T(8,128)(2,1)S(1)}, u32[]{:S(2)}, u32[]{:S(2)}) async-start(bf16[8,48,1024]{2,1,0:T(8,128)(2,1)} %shard_map.99), calls=%async_computation.6 | async-start | bytes 1572864 | tf_op jit(solution)/shard_map/all_to_all | solution.py:284
  223.0 1.9 collective-permute-start.29
  224.9 14.2 %copy-start.13 = (bf16[512,512]{1,0:T(8,128)(2,1)}, bf16[512,512]{1,0:T(8,128)(2,1)S(1)}, u32[]{:S(2)}) copy-start(bf16[512,512]{1,0:T(8,128)(2,1)S(1)} %collective-permute-done.29.got_sib) | copy-start | bytes 1572868
  (8 other events, 19.6 us)

commit v4 on v3

--- a/solution.py
+++ b/solution.py
@@ -46,50 +46,74 @@
     )
 
 
-def pack_kernel(layer, xl_ref, gate, up, down, mine, *refs):
-    *others, held, in_sems, out_sems = refs
+def pack_kernel(layer, plan, xl_ref, gate, up, down, *refs):
+    outs, (held, in_sems, out_sems) = refs[: len(plan)], refs[len(plan) :]
     xl = xl_ref[0]
     half = held.shape[2]
-    coming, going = [], []
-    for side, which in enumerate((1 - xl, xl)):
-        units = pl.ds(pl.multiple_of(which * half, half), half)
-        for slot, source in enumerate(
-            (gate.at[layer, :, units], up.at[layer, :, units], down.at[layer, units, :])
-        ):
-            n = 3 * side + slot
-            copy = pltpu.make_async_copy(source, held.at[n], in_sems.at[n])
-            copy.start()
-            coming.append(copy)
-            if side:
-                target = mine.at[:, pl.ds(slot * half, half)]
-            elif len(others) == 2 and slot < 2:
-                target = others[0].at[:, pl.ds(slot * half, half)]
-            else:
-                target = others[slot - 3]
-            going.append(pltpu.make_async_copy(held.at[n], target, out_sems.at[n]))
-    for come, go in zip(coming, going):
+    copies = []
+    for out, parts in zip(outs, plan):
+        for place, (stays, kind) in enumerate(parts):
+            n = len(copies)
+            units = pl.ds(pl.multiple_of((xl if stays else 1 - xl) * half, half), half)
+            source = (gate.at[layer, :, units], up.at[layer, :, units], down.at[layer, units, :])[kind]
+            target = out.at[:, pl.ds(place * half, half)]
+            come = pltpu.make_async_copy(source, held.at[n], in_sems.at[n])
+            come.start()
+            copies.append((come, pltpu.make_async_copy(held.at[n], target, out_sems.at[n])))
+    for come, go in copies:
         come.wait()
         go.start()
-    for go in going:
+    for _, go in copies:
         go.wait()
 
 
-def pack(layer, xl, gate, up, down, joined):
+def pack(layer, plan, xl, gate, up, down):
     _, rows, cols = gate.shape
     half = cols // 2
-    widths = (3, 2, 1) if joined else (3, 1, 1, 1)
+    pieces = sum(map(len, plan))
     return call(
-        functools.partial(pack_kernel, layer),
-        tuple(jax.ShapeDtypeStruct((rows, n * half), BF) for n in widths),
+        functools.partial(pack_kernel, layer, plan),
+        tuple(jax.ShapeDtypeStruct((rows, len(parts) * half), BF) for parts in plan),
         [SMEM, HBM, HBM, HBM],
-        (HBM,) * len(widths),
+        (HBM,) * len(plan),
         [
-            pltpu.VMEM((6, rows, half), BF),
-            pltpu.SemaphoreType.DMA((6,)),
-            pltpu.SemaphoreType.DMA((6,)),
+            pltpu.VMEM((pieces, rows, half), BF),
+            pltpu.SemaphoreType.DMA((pieces,)),
+            pltpu.SemaphoreType.DMA((pieces,)),
         ],
-        moved=24 * rows * half,
+        moved=4 * pieces * rows * half,
     )(xl, gate, up, down)
+
+
+def join_kernel(a, b, out, held, in_sems, out_sems):
+    half = held.shape[2]
+    copies = []
+    for n, source in enumerate((a, b)):
+        come = pltpu.make_async_copy(source, held.at[n], in_sems.at[n])
+        come.start()
+        target = out.at[:, pl.ds(n * half, half)]
+        copies.append((come, pltpu.make_async_copy(held.at[n], target, out_sems.at[n])))
+    for come, go in copies:
+        come.wait()
+        go.start()
+    for _, go in copies:
+        go.wait()
+
+
+def join(a, b):
+    rows, half = a.shape
+    return call(
+        join_kernel,
+        jax.ShapeDtypeStruct((rows, 2 * half), BF),
+        [HBM, HBM],
+        HBM,
+        [
+            pltpu.VMEM((2, rows, half), BF),
+            pltpu.SemaphoreType.DMA((2,)),
+            pltpu.SemaphoreType.DMA((2,)),
+        ],
+        moved=8 * rows * half,
+    )(a, b)
 
 
 def flat(value):
@@ -327,7 +351,8 @@
     scales = jnp.stack([scales, swap(scales, "c")], 1)
 
     mine, mine_sib = [None] * LAYERS, [None] * LAYERS
-    mine[0], g_out, u_out, d_out = pack(0, xl_arg, w_gate, w_up, w_down, False)
+    g_out, u_out = pack(0, (((0, 0),), ((0, 1),)), xl_arg, w_gate, w_up, w_down)
+    stay = ((1, 0), (1, 1), (1, 2))
     near, g_out, gains = together(near, g_out, gains)
     g_got = swap(g_out, "xl")
     all_ids = exchange(jnp.broadcast_to(near[None], (n_owners // 2, 2, rows)), ("c", "y"))
@@ -337,7 +362,8 @@
     local_ids = all_ids - owner * vocab_rows
     inside = (local_ids >= 0) & (local_ids < vocab_rows)
     local_ids = jnp.clip(local_ids, 0, vocab_rows - 1)
-    local_ids, g_got = together(local_ids, g_got)
+    mine[0], d_out = pack(0, (stay, ((0, 2),)), xl_arg, *after(g_out, w_gate, w_up, w_down))
+    local_ids, g_got, mine[0], d_out = together(local_ids, g_got, mine[0], d_out)
     u_got = swap(u_out, "xl")
     picked = embed_table.at[local_ids].get(mode="promise_in_bounds")
     picked = jnp.where(inside[:, None], picked, jnp.zeros((), BF)).reshape(2, -1, rows, width)
@@ -346,14 +372,19 @@
     given = swap(lax.dynamic_index_in_dim(picked, 1 - core, 0, keepdims=False), "c")
     both = add(kept, given).astype(BF)
     both, g_got, u_got, later = together(both, g_got, u_got, mine[0])
-    mine_sib[0], g_sib, u_sib = swap(later, "c"), swap(g_got, "c"), swap(u_got, "c")
+    mine_sib[0] = swap(later, "c")
+    gu_got = join(g_got, u_got)
+    gu_sib = swap(gu_got, "c")
     pieces = exchange(both, ("xh", "y"))
-    mine[1], gu_out, last_out = pack(1, xl_arg, *after(both, w_gate, w_up, w_down), True)
-    pieces, mine_sib[0], g_sib, u_sib, mine[1], gu_out, last_out = together(
-        pieces, mine_sib[0], g_sib, u_sib, mine[1], gu_out, last_out
+    mine[1], gu_out, last_out = pack(
+        1, (stay, ((0, 0), (0, 1)), ((0, 2),)), xl_arg, *after(both, w_gate, w_up, w_down)
+    )
+    pieces, mine_sib[0], mine[1], gu_out, last_out = together(
+        pieces, mine_sib[0], mine[1], gu_out, last_out
     )
     x, sent = first(pieces)
-    others, others_sib = (g_got, u_got), (g_sib, u_sib)
+    sent, gu_sib = together(sent, gu_sib)
+    others, others_sib = (gu_got,), (gu_sib,)
     mine_sib[1] = swap(after(x, mine[1]), "c")
 
     for layer in range(LAYERS):

time: 262 us -> 262 us (level)
  Pallas kernels: 29.4 us -> 33.3 us
    pallas_call x2 -> x4, Pallas kernels: 5.72 us -> 9.53 us  [the longest x3 7.37 us: pack(): call(functools.partial(pack_kernel, layer, plan), tuple((jax.ShapeDtypeSt...]
    all_to_all x7, waiting for transfers between devices: 56.8 us -> 54.2 us  [exchange(): return lax.all_to_all(value, axes, 0, 0, tiled=True)]
    ppermute x16 -> x15, waiting for transfers between devices: 31 us -> 30.5 us  [swap(): return lax.ppermute(value, axis, turn(2, 1))]
    ppermute x16 -> x15, starting transfers between devices: 13.1 us -> 12.9 us  [swap(): return lax.ppermute(value, axis, turn(2, 1))]
  transfers between devices with their start and end apart: 37 -> 36, of which waited for: 21 -> 21; matrix products, arithmetic and copies ran while one was open for 4% -> 4% of each run, Pallas kernels for 5% -> 7%
where the time goes in v4:
time: 262 us; the launch traced here: 261 us
  waiting for transfers between devices  119 us (45%)
  starting transfers between devices  78.7 us (30%)
  Pallas kernels  33.3 us (13%)
  blocking collectives  15.6 us (6%)
  local copies, waits for them, and re-layouts  10.4 us (4%)
  other arithmetic  3.95 us (2%)
    all_to_all x7, waiting for transfers between devices, exchange(): return lax.all_to_all(value, axes, 0, 0, tiled=True)  54.2 us
    all_to_all x7, starting transfers between devices, exchange(): return lax.all_to_all(value, axes, 0, 0, tiled=True)  35.3 us
    ppermute x15, waiting for transfers between devices, swap(): return lax.ppermute(value, axis, turn(2, 1))  30.5 us
    ppermute x6, starting transfers between devices, scatter_sum_z(): down = lax.ppermute(down, 'z', turn(Z, -1))  20.8 us
    all_to_all x1, blocking collectives, exchange(): return lax.all_to_all(value, axes, 0, 0, tiled=True)  15.6 us
    ppermute x6, waiting for transfers between devices, scatter_sum_z(): down = lax.ppermute(down, 'z', turn(Z, -1))  14.3 us
    ppermute x15, starting transfers between devices, swap(): return lax.ppermute(value, axis, turn(2, 1))  12.9 us
    ppermute x6, waiting for transfers between devices, scatter_sum_z(): up = lax.ppermute(up, 'z', turn(Z, 1))  12.1 us
  transfers between devices with their start and end apart: 36, of which 21 were waited for; matrix products, arithmetic and copies ran while one was open for 4% of the time, Pallas kernels for 7%

profile of v4, /device:TPU:2, one launch (start us, length us, event | category | flops | bytes accessed | tf_op | source)
XLA Modules:
  0.0 261.0 jit_solution(4198312180425728567)
XLA Ops:
  0.0 2.1 collective-permute-start
  4.3 2.1 shard_map.91
  8.2 4.3 %all-to-all-start = ((s32[8,2,48]{2,1,0:T(2,128)}), s32[8,2,48]{2,1,0:T(2,128)S(1)}, u32[]{:S(2)}, u32[]{:S(2)}) async-start(s32[8,2,48]{2,1,0:T(2,128)} %broadcast_in_dim.22), calls=%async_computation | async-start | bytes 16384 | tf_op jit(solution)/shard_map/all_to_all | solution.py:308
  13.7 2.4 shard_map.92
  18.0 3.7 %collective-permute-done.2.a = bf16[512,512]{1,0:T(8,128)(2,1)S(1)} collective-permute-done((bf16[512,512]{1,0:T(8,128)(2,1)}, bf16[512,512]{1,0:T(8,128)(2,1)S(1)}, u32[]{:S(2)}, u32[]{:S(2)}) %collective-permute-start.2) | collective-permute-done | bytes 524320 | tf_op jit(solution)/shard_map/ppermute | solution.py:30
  21.6 5.9 %gather_fusion = bf16[768,512]{1,0:T(8,128)(2,1)S(1)} fusion(bf16[4752,512]{1,0:T(8,128)(2,1)} %param.10, s32[1024]{0:T(1024)S(1)} %pad_clamp_fusion), kind=kCustom, calls=%fused_computation | custom fusion | bytes 1575936 | tf_op jit(solution)/shard_map/gather | solution.py:368
  27.7 3.5 %collective-permute-done.3.b = bf16[512,512]{1,0:T(8,128)(2,1)} collective-permute-done((bf16[512,512]{1,0:T(8,128)(2,1)}, bf16[512,512]{1,0:T(8,128)(2,1)}, u32[]{:S(2)}, u32[]{:S(2)}) %collective-permute-start.3) | collective-permute-done | bytes 524320 | tf_op jit(solution)/shard_map/ppermute | solution.py:30
  34.0 2.2 shard_map.95.refs_1_
  36.7 4.5 %all-to-all-start.1 = ((bf16[8,48,512]{2,1,0:T(8,128)(2,1)}), bf16[8,48,512]{2,1,0:T(8,128)(2,1)S(1)}, u32[]{:S(2)}, u32[]{:S(2)}) async-start(bf16[8,48,512]{2,1,0:T(8,128)(2,1)} %fusion), calls=%async_computation.1 | async-start | bytes 786432 | tf_op jit(solution)/shard_map/all_to_all | solution.py:308
  41.1 2.9 %shard_map.93 = (bf16[512,1536]{1,0:T(8,128)(2,1)}, bf16[512,1024]{1,0:T(8,128)(2,1)}, bf16[512,512]{1,0:T(8,128)(2,1)}) custom-call(s32[1]{0:T(128)} %bitcast.xl_ref, bf16[2,512,1024]{2,1,0:T(8,128)(2,1)} %gate.3, bf16[2,512,1024]{2,1,0:T(8,128)(2,1)} %up.3, bf16[2,1024,512]{2,1,0:T(8,128)(2,1)} %down.3), custom_call_target="tpu_custom_call" | custom-call | bytes 6291456 | tf_op jit(solution)/shard_map/pallas_call | solution.py:74
  44.0 7.3 %all-to-all-done.1.pieces = bf16[8,48,512]{2,1,0:T(8,128)(2,1)S(1)} async-done(((bf16[8,48,512]{2,1,0:T(8,128)(2,1)}), bf16[8,48,512]{2,1,0:T(8,128)(2,1)S(1)}, u32[]{:S(2)}, u32[]{:S(2)}) %all-to-all-start.1) | async-done | bytes 393248 | tf_op jit(solution)/shard_map/all_to_all | solution.py:308
  52.0 2.0 shard_map.94
  54.0 6.1 %all-to-all-start.2 = ((bf16[16,48,512]{2,1,0:T(8,128)(2,1)}), bf16[16,48,512]{2,1,0:T(8,128)(2,1)}, u32[]{:S(2)}, u32[]{:S(2)}) async-start(bf16[16,48,512]{2,1,0:T(8,128)(2,1)} %get-tuple-element.84), calls=%async_computation.2 | async-start | bytes 1572864 | tf_op jit(solution)/shard_map/all_to_all | solution.py:308
  60.2 11.7 %all-to-all-done.2 = bf16[16,48,512]{2,1,0:T(8,128)(2,1)} async-done(((bf16[16,48,512]{2,1,0:T(8,128)(2,1)}), bf16[16,48,512]{2,1,0:T(8,128)(2,1)}, u32[]{:S(2)}, u32[]{:S(2)}) %all-to-all-start.2) | async-done | bytes 786464 | tf_op jit(solution)/shard_map/all_to_all | solution.py:308
  73.2 4.0 %shard_map.96 = (bf16[8,48,2176]{2,1,0:T(8,128)(2,1)S(1)}, bf16[48,2176]{1,0:T(8,128)(2,1)S(1)}) custom-call(s32[2]{0:T(128)S(1)} %pad_add_fusion.1.at_ref, bf16[2,8,48,512]{3,2,1,0:T(8,128)(2,1)} %bitcast.12.x, f32[2,2,512]{2,1,0:T(2,128)S(1)} %pad_maximum_fusion.1.gains, bf16[512,1536]{1,0:T(8,128)(2,1)S(1)} %copy-done.1, bf16[512,1024]{1,0:T(8,128)(2,1)S(1)} %copy-done.4, ...), custom_call_target="tpu_custom_call" | custom-call | flops 1610612736 | bytes 6553600 | tf_op jit(solution)/shard_map/pallas_call | solution.py:175
  77.3 5.9 %collective-permute-start.7 = (bf16[48,2176]{1,0:T(8,128)(2,1)S(1)}, bf16[48,2176]{1,0:T(8,128)(2,1)S(1)}, u32[]{:S(2)}, u32[]{:S(2)}) collective-permute-start(bf16[48,2176]{1,0:T(8,128)(2,1)S(1)} %get-tuple-element.90), channel_id=1, source_target_pairs={{0,224},{32,0},{64,32},{96,64},{128,96},{160,128},{192,160},{224,1... | collective-permute-start | bytes 626696 | tf_op jit(solution)/shard_map/ppermute | solution.py:324
  83.4 3.2 %collective-permute-done.7 = bf16[48,2176]{1,0:T(8,128)(2,1)S(1)} collective-permute-done((bf16[48,2176]{1,0:T(8,128)(2,1)S(1)}, bf16[48,2176]{1,0:T(8,128)(2,1)S(1)}, u32[]{:S(2)}, u32[]{:S(2)}) %collective-permute-start.7) | collective-permute-done | bytes 208928 | tf_op jit(solution)/shard_map/ppermute | solution.py:324
  86.6 3.8 %collective-permute-start.8 = (bf16[48,2176]{1,0:T(8,128)(2,1)S(1)}, bf16[48,2176]{1,0:T(8,128)(2,1)S(1)}, u32[]{:S(2)}, u32[]{:S(2)}) collective-permute-start(bf16[48,2176]{1,0:T(8,128)(2,1)S(1)} %fusion.10), channel_id=1, source_target_pairs={{0,224},{32,0},{64,32},{96,64},{128,96},{160,128},{192,160},{224,1... | collective-permute-start | bytes 626696 | tf_op jit(solution)/shard_map/ppermute | solution.py:329
  90.4 3.3 %collective-permute-done.8 = bf16[48,2176]{1,0:T(8,128)(2,1)S(1)} collective-permute-done((bf16[48,2176]{1,0:T(8,128)(2,1)S(1)}, bf16[48,2176]{1,0:T(8,128)(2,1)S(1)}, u32[]{:S(2)}, u32[]{:S(2)}) %collective-permute-start.8) | collective-permute-done | bytes 208928 | tf_op jit(solution)/shard_map/ppermute | solution.py:329
  94.9 3.9 %collective-permute-start.9 = (bf16[48,2176]{1,0:T(8,128)(2,1)S(1)}, bf16[48,2176]{1,0:T(8,128)(2,1)S(1)}, u32[]{:S(2)}, u32[]{:S(2)}) collective-permute-start(bf16[48,2176]{1,0:T(8,128)(2,1)S(1)} %get-tuple-element.122), channel_id=1, source_target_pairs={{0,224},{32,0},{64,32},{96,64},{128,96},{160,128},{192,160},{224,1... | collective-permute-start | bytes 626696 | tf_op jit(solution)/shard_map/ppermute | solution.py:329
  103.6 3.6 %collective-permute-start.10 = (bf16[48,2176]{1,0:T(8,128)(2,1)S(1)}, bf16[48,2176]{1,0:T(8,128)(2,1)S(1)}, u32[]{:S(2)}, u32[]{:S(2)}) collective-permute-start(bf16[48,2176]{1,0:T(8,128)(2,1)S(1)} %get-tuple-element.120), channel_id=1, source_target_pairs={{0,224},{32,0},{64,32},{96,64},{128,96},{160,128},{192,160},{224,1... | collective-permute-start | bytes 626696 | tf_op jit(solution)/shard_map/ppermute | solution.py:329
  107.2 3.2 %collective-permute-done.10.a = bf16[48,2176]{1,0:T(8,128)(2,1)S(1)} collective-permute-done((bf16[48,2176]{1,0:T(8,128)(2,1)S(1)}, bf16[48,2176]{1,0:T(8,128)(2,1)S(1)}, u32[]{:S(2)}, u32[]{:S(2)}) %collective-permute-start.10) | collective-permute-done | bytes 208928 | tf_op jit(solution)/shard_map/ppermute | solution.py:329
  110.5 3.7 %collective-permute-done.13.b = bf16[48,2176]{1,0:T(8,128)(2,1)S(1)} collective-permute-done((bf16[48,2176]{1,0:T(8,128)(2,1)S(1)}, bf16[48,2176]{1,0:T(8,128)(2,1)S(1)}, u32[]{:S(2)}, u32[]{:S(2)}) %collective-permute-start.13) | collective-permute-done | bytes 208928 | tf_op jit(solution)/shard_map/ppermute | solution.py:330
  115.2 4.7 %all-to-all-start.3 = ((bf16[8,48,1024]{2,1,0:T(8,128)(2,1)}), bf16[8,48,1024]{2,1,0:T(8,128)(2,1)}, u32[]{:S(2)}, u32[]{:S(2)}) async-start(bf16[8,48,1024]{2,1,0:T(8,128)(2,1)} %shard_map.97), calls=%async_computation.3 | async-start | bytes 1572864 | tf_op jit(solution)/shard_map/all_to_all | solution.py:308
  119.9 2.7 %collective-permute-start.16 = (bf16[512,1024]{1,0:T(8,128)(2,1)}, bf16[512,1024]{1,0:T(8,128)(2,1)}, u32[]{:S(2)}, u32[]{:S(2)}) collective-permute-start(bf16[512,1024]{1,0:T(8,128)(2,1)} %get-tuple-element.95), channel_id=1, source_target_pairs={{0,16},{16,0},{1,17},{17,1},{2,18},{18,2},{3,19},{19,3},{4,20},{20... | collective-permute-start | bytes 3145736 | tf_op jit(solution)/shard_map/ppermute | solution.py:30
  123.1 19.7 %collective-permute-done.16.refs_1_ = bf16[512,1024]{1,0:T(8,128)(2,1)} collective-permute-done((bf16[512,1024]{1,0:T(8,128)(2,1)}, bf16[512,1024]{1,0:T(8,128)(2,1)}, u32[]{:S(2)}, u32[]{:S(2)}) %collective-permute-start.16) | collective-permute-done | bytes 1048608 | tf_op jit(solution)/shard_map/ppermute | solution.py:30
  142.8 3.4 %shard_map.98 = bf16[2,8,48,512]{3,2,1,0:T(8,128)(2,1)} custom-call(s32[1]{0:T(128)} %bitcast.xl_ref, bf16[8,48,1024]{2,1,0:T(8,128)(2,1)} %all-to-all-done.3.act, bf16[512,1536]{1,0:T(8,128)(2,1)} %get-tuple-element.73.refs_0_.mine, bf16[512,512]{1,0:T(8,128)(2,1)} %collective-permute-done.15.got, bf16[512,1536]{1,0:T(8,128)(2,1)} %copy-done.2, ...), custom_call_target="tpu_custom_call" | custom-call | flops 805306368 | bytes 3670016 | tf_op jit(solution)/shard_map/pallas_call | solution.py:253
  146.3 5.8 %all-to-all-start.4 = ((bf16[16,48,512]{2,1,0:T(8,128)(2,1)}), bf16[16,48,512]{2,1,0:T(8,128)(2,1)}, u32[]{:S(2)}, u32[]{:S(2)}) async-start(bf16[16,48,512]{2,1,0:T(8,128)(2,1)} %bitcast.64), calls=%async_computation.4 | async-start | bytes 1572864 | tf_op jit(solution)/shard_map/all_to_all | solution.py:308
  152.0 9.8 %all-to-all-done.4.pieces = bf16[16,48,512]{2,1,0:T(8,128)(2,1)} async-done(((bf16[16,48,512]{2,1,0:T(8,128)(2,1)}), bf16[16,48,512]{2,1,0:T(8,128)(2,1)}, u32[]{:S(2)}, u32[]{:S(2)}) %all-to-all-start.4) | async-done | bytes 786464 | tf_op jit(solution)/shard_map/all_to_all | solution.py:308
  161.8 2.2 shard_map.99
  164.1 5.5 %all-to-all-start.5 = ((bf16[16,48,512]{2,1,0:T(8,128)(2,1)}), bf16[16,48,512]{2,1,0:T(8,128)(2,1)}, u32[]{:S(2)}, u32[]{:S(2)}) async-start(bf16[16,48,512]{2,1,0:T(8,128)(2,1)} %get-tuple-element.99), calls=%async_computation.5 | async-start | bytes 1572864 | tf_op jit(solution)/shard_map/all_to_all | solution.py:308
  169.6 9.8 %all-to-all-done.5 = bf16[16,48,512]{2,1,0:T(8,128)(2,1)} async-done(((bf16[16,48,512]{2,1,0:T(8,128)(2,1)}), bf16[16,48,512]{2,1,0:T(8,128)(2,1)}, u32[]{:S(2)}, u32[]{:S(2)}) %all-to-all-start.5) | async-done | bytes 786464 | tf_op jit(solution)/shard_map/all_to_all | solution.py:308
  179.3 4.6 %shard_map.100 = (bf16[8,48,2176]{2,1,0:T(8,128)(2,1)S(1)}, bf16[48,2176]{1,0:T(8,128)(2,1)S(1)}) custom-call(s32[2]{0:T(128)S(1)} %pad_add_fusion.1.at_ref, bf16[2,8,48,512]{3,2,1,0:T(8,128)(2,1)} %bitcast.23.x, f32[2,2,512]{2,1,0:T(2,128)S(1)} %pad_maximum_fusion.1.gains, bf16[512,1536]{1,0:T(8,128)(2,1)S(1)} %copy-done, ...), custom_call_target="tpu_custom_call" | custom-call | flops 1610612736 | bytes 6553600 | tf_op jit(solution)/shard_map/pallas_call | solution.py:175
  184.0 3.0 %collective-permute-start.20 = (bf16[48,2176]{1,0:T(8,128)(2,1)S(1)}, bf16[48,2176]{1,0:T(8,128)(2,1)S(1)}, u32[]{:S(2)}, u32[]{:S(2)}) collective-permute-start(bf16[48,2176]{1,0:T(8,128)(2,1)S(1)} %get-tuple-element.105), channel_id=1, source_target_pairs={{0,224},{32,0},{64,32},{96,64},{128,96},{160,128},{192,160},{224,1... | collective-permute-start | bytes 626696 | tf_op jit(solution)/shard_map/ppermute | solution.py:324
  187.1 4.4 %collective-permute-done.20 = bf16[48,2176]{1,0:T(8,128)(2,1)S(1)} collective-permute-done((bf16[48,2176]{1,0:T(8,128)(2,1)S(1)}, bf16[48,2176]{1,0:T(8,128)(2,1)S(1)}, u32[]{:S(2)}, u32[]{:S(2)}) %collective-permute-start.20) | collective-permute-done | bytes 208928 | tf_op jit(solution)/shard_map/ppermute | solution.py:324
  191.5 3.8 %collective-permute-start.21 = (bf16[48,2176]{1,0:T(8,128)(2,1)S(1)}, bf16[48,2176]{1,0:T(8,128)(2,1)S(1)}, u32[]{:S(2)}, u32[]{:S(2)}) collective-permute-start(bf16[48,2176]{1,0:T(8,128)(2,1)S(1)} %fusion.5), channel_id=1, source_target_pairs={{0,224},{32,0},{64,32},{96,64},{128,96},{160,128},{192,160},{224,1... | collective-permute-start | bytes 626696 | tf_op jit(solution)/shard_map/ppermute | solution.py:329
  195.3 4.0 %collective-permute-done.21 = bf16[48,2176]{1,0:T(8,128)(2,1)S(1)} collective-permute-done((bf16[48,2176]{1,0:T(8,128)(2,1)S(1)}, bf16[48,2176]{1,0:T(8,128)(2,1)S(1)}, u32[]{:S(2)}, u32[]{:S(2)}) %collective-permute-start.21) | collective-permute-done | bytes 208928 | tf_op jit(solution)/shard_map/ppermute | solution.py:329
  199.5 4.0 %collective-permute-start.22 = (bf16[48,2176]{1,0:T(8,128)(2,1)S(1)}, bf16[48,2176]{1,0:T(8,128)(2,1)S(1)}, u32[]{:S(2)}, u32[]{:S(2)}) collective-permute-start(bf16[48,2176]{1,0:T(8,128)(2,1)S(1)} %get-tuple-element.116), channel_id=1, source_target_pairs={{0,224},{32,0},{64,32},{96,64},{128,96},{160,128},{192,160},{224,1... | collective-permute-start | bytes 626696 | tf_op jit(solution)/shard_map/ppermute | solution.py:329
  205.0 3.8 %collective-permute-done.25 = bf16[48,2176]{1,0:T(8,128)(2,1)S(1)} collective-permute-done((bf16[48,2176]{1,0:T(8,128)(2,1)S(1)}, bf16[48,2176]{1,0:T(8,128)(2,1)S(1)}, u32[]{:S(2)}, u32[]{:S(2)}) %collective-permute-start.25) | collective-permute-done | bytes 208928 | tf_op jit(solution)/shard_map/ppermute | solution.py:330
  208.9 1.8 collective-permute-start.23
  211.0 3.8 %collective-permute-done.23.a = bf16[48,2176]{1,0:T(8,128)(2,1)S(1)} collective-permute-done((bf16[48,2176]{1,0:T(8,128)(2,1)S(1)}, bf16[48,2176]{1,0:T(8,128)(2,1)S(1)}, u32[]{:S(2)}, u32[]{:S(2)}) %collective-permute-start.23) | collective-permute-done | bytes 208928 | tf_op jit(solution)/shard_map/ppermute | solution.py:329
  214.8 2.9 %collective-permute-done.26.b = bf16[48,2176]{1,0:T(8,128)(2,1)S(1)} collective-permute-done((bf16[48,2176]{1,0:T(8,128)(2,1)S(1)}, bf16[48,2176]{1,0:T(8,128)(2,1)S(1)}, u32[]{:S(2)}, u32[]{:S(2)}) %collective-permute-start.26) | collective-permute-done | bytes 208928 | tf_op jit(solution)/shard_map/ppermute | solution.py:330
  218.8 4.5 %all-to-all-start.6 = ((bf16[8,48,1024]{2,1,0:T(8,128)(2,1)}), bf16[8,48,1024]{2,1,0:T(8,128)(2,1)S(1)}, u32[]{:S(2)}, u32[]{:S(2)}) async-start(bf16[8,48,1024]{2,1,0:T(8,128)(2,1)} %shard_map.101), calls=%async_computation.6 | async-start | bytes 1572864 | tf_op jit(solution)/shard_map/all_to_all | solution.py:308
  223.3 1.9 collective-permute-done.28.got_sib
  225.2 13.9 %all-to-all-done.6.act = bf16[8,48,1024]{2,1,0:T(8,128)(2,1)S(1)} async-done(((bf16[8,48,1024]{2,1,0:T(8,128)(2,1)}), bf16[8,48,1024]{2,1,0:T(8,128)(2,1)S(1)}, u32[]{:S(2)}, u32[]{:S(2)}) %all-to-all-start.6) | async-done | bytes 786464 | tf_op jit(solution)/shard_map/all_to_all | solution.py:308
  240.0 3.4 %shard_map.102 = bf16[2,8,48,512]{3,2,1,0:T(8,128)(2,1)} custom-call(s32[1]{0:T(128)} %bitcast.xl_ref, bf16[8,48,1024]{2,1,0:T(8,128)(2,1)} %copy-done.6, bf16[512,1536]{1,0:T(8,128)(2,1)} %get-tuple-element.102.refs_0_.mine, bf16[512,512]{1,0:T(8,128)(2,1)} %copy-done.8, bf16[512,1536]{1,0:T(8,128)(2,1)} %copy-done.3, bf16[512,512]{1,0:T(8,128)(2,1)} %copy-done.9), custom_call_target="tpu_custom_call" | custom-call | flops 805306368 | bytes 3670016 | tf_op jit(solution)/shard_map/pallas_call | solution.py:253
  243.4 15.6 %all_to_all.40.pieces = bf16[16,48,512]{2,1,0:T(8,128)(2,1)} all-to-all(bf16[16,48,512]{2,1,0:T(8,128)(2,1)} %bitcast.65), channel_id=1, replica_groups=mesh['z'=8,'xl'=2,'c'=2,'xh'=2,'y'=4] {'xl','xh','y'}, dimensions={0} | all-to-all | bytes 1572864 | tf_op jit(solution)/shard_map/all_to_all | solution.py:308
  259.1 1.9 shard_map.103
  (102 shorter events, 24.5 us)
Async XLA Ops:
  0.0 6.4 %collective-permute-start = (s32[48]{0:T(128)}, s32[48]{0:T(128)S(1)}, u32[]{:S(2)}, u32[]{:S(2)}) collective-permute-start(s32[48]{0:T(128)} %param.9), channel_id=1, source_target_pairs={{0,4},{4,0},{1,5},{5,1},{2,6},{6,2},{3,7},{7,3},{8,12},{12,8},{9,1... | collective-permute-start | bytes 584 | tf_op jit(solution)/shard_map/ppermute | solution.py:30
  2.1 4.3 %collective-permute-start.1 = (f32[2,512]{1,0:T(2,128)}, f32[2,512]{1,0:T(2,128)S(1)}, u32[]{:S(2)}, u32[]{:S(2)}) collective-permute-start(f32[2,512]{1,0:T(2,128)} %param.11), channel_id=1, source_target_pairs={{0,16},{16,0},{1,17},{17,1},{2,18},{18,2},{3,19},{19,3},{4,20},{20... | collective-permute-start | bytes 12296 | tf_op jit(solution)/shard_map/ppermute | solution.py:30
  6.5 15.2 %collective-permute-start.2 = (bf16[512,512]{1,0:T(8,128)(2,1)}, bf16[512,512]{1,0:T(8,128)(2,1)S(1)}, u32[]{:S(2)}, u32[]{:S(2)}) collective-permute-start(bf16[512,512]{1,0:T(8,128)(2,1)} %get-tuple-element.60), channel_id=1, source_target_pairs={{0,16},{16,0},{1,17},{17,1},{2,18},{18,2},{3,19},{19,3},{4,20},{20... | collective-permute-start | bytes 1572872 | tf_op jit(solution)/shard_map/ppermute | solution.py:30
  8.2 9.6 %all-to-all-start = ((s32[8,2,48]{2,1,0:T(2,128)}), s32[8,2,48]{2,1,0:T(2,128)S(1)}, u32[]{:S(2)}, u32[]{:S(2)}) async-start(s32[8,2,48]{2,1,0:T(2,128)} %broadcast_in_dim.22), calls=%async_computation | async-start | bytes 16384 | tf_op jit(solution)/shard_map/all_to_all | solution.py:308
  12.6 18.6 %collective-permute-start.3 = (bf16[512,512]{1,0:T(8,128)(2,1)}, bf16[512,512]{1,0:T(8,128)(2,1)}, u32[]{:S(2)}, u32[]{:S(2)}) collective-permute-start(bf16[512,512]{1,0:T(8,128)(2,1)} %get-tuple-element.67), channel_id=1, source_target_pairs={{0,16},{16,0},{1,17},{17,1},{2,18},{18,2},{3,19},{19,3},{4,20},{20... | collective-permute-start | bytes 1572872 | tf_op jit(solution)/shard_map/ppermute | solution.py:30
  21.6 5.9 %copy-start.10 = (bf16[512,512]{1,0:T(8,128)(2,1)}, bf16[512,512]{1,0:T(8,128)(2,1)S(1)}, u32[]{:S(2)}) copy-start(bf16[512,512]{1,0:T(8,128)(2,1)S(1)} %collective-permute-done.2.a) | copy-start | bytes 1572868
  27.6 6.3 %copy-start.1 = (bf16[512,1536]{1,0:T(8,128)(2,1)S(1)}, bf16[512,1536]{1,0:T(8,128)(2,1)}, u32[]{:S(2)}) copy-start(bf16[512,1536]{1,0:T(8,128)(2,1)} %get-tuple-element.73.refs_0_.mine) | copy-start | bytes 4718596
  31.2 1.8 collective-permute-start.4
  33.9 17.4 %collective-permute-start.5 = (bf16[512,1536]{1,0:T(8,128)(2,1)S(1)}, bf16[512,1536]{1,0:T(8,128)(2,1)S(1)}, u32[]{:S(2)}, u32[]{:S(2)}) collective-permute-start(bf16[512,1536]{1,0:T(8,128)(2,1)S(1)} %copy-done.1), channel_id=1, source_target_pairs={{0,8},{8,0},{1,9},{9,1},{2,10},{10,2},{3,11},{11,3},{4,12},{12,4},... | collective-permute-start | bytes 4718600 | tf_op jit(solution)/shard_map/ppermute | solution.py:30
  36.2 17.8 %collective-permute-start.6 = (bf16[512,1024]{1,0:T(8,128)(2,1)}, bf16[512,1024]{1,0:T(8,128)(2,1)}, u32[]{:S(2)}, u32[]{:S(2)}) collective-permute-start(bf16[512,1024]{1,0:T(8,128)(2,1)} %shard_map.95.refs_1_), channel_id=1, source_target_pairs={{0,8},{8,0},{1,9},{9,1},{2,10},{10,2},{3,11},{11,3},{4,12},{12,4},... | collective-permute-start | bytes 3145736 | tf_op jit(solution)/shard_map/ppermute | solution.py:30
  36.7 14.6 %all-to-all-start.1 = ((bf16[8,48,512]{2,1,0:T(8,128)(2,1)}), bf16[8,48,512]{2,1,0:T(8,128)(2,1)S(1)}, u32[]{:S(2)}, u32[]{:S(2)}) async-start(bf16[8,48,512]{2,1,0:T(8,128)(2,1)} %fusion), calls=%async_computation.1 | async-start | bytes 786432 | tf_op jit(solution)/shard_map/all_to_all | solution.py:308
  51.3 25.9 %copy-start.2 = (bf16[512,1536]{1,0:T(8,128)(2,1)}, bf16[512,1536]{1,0:T(8,128)(2,1)S(1)}, u32[]{:S(2)}) copy-start(bf16[512,1536]{1,0:T(8,128)(2,1)S(1)} %collective-permute-done.5.refs_2_.mine_sib) | copy-start | bytes 4718596
  54.0 17.9 %all-to-all-start.2 = ((bf16[16,48,512]{2,1,0:T(8,128)(2,1)}), bf16[16,48,512]{2,1,0:T(8,128)(2,1)}, u32[]{:S(2)}, u32[]{:S(2)}) async-start(bf16[16,48,512]{2,1,0:T(8,128)(2,1)} %get-tuple-element.84), calls=%async_computation.2 | async-start | bytes 1572864 | tf_op jit(solution)/shard_map/all_to_all | solution.py:308
  77.2 9.3 %copy-start.5 = (bf16[8,48,2176]{2,1,0:T(8,128)(2,1)}, bf16[8,48,2176]{2,1,0:T(8,128)(2,1)S(1)}, u32[]{:S(2)}) copy-start(bf16[8,48,2176]{2,1,0:T(8,128)(2,1)S(1)} %get-tuple-element.91) | copy-start | bytes 5013508
  77.3 21.6 %copy-start.11 = (f32[2,1024]{1,0:T(2,128)S(1)}, f32[2,1024]{1,0:T(2,128)}, u32[]{:S(2)}) copy-start(f32[2,1024]{1,0:T(2,128)} %param.14) | copy-start | bytes 24580
  77.3 21.6 %copy-start.12 = (f32[2,1024]{1,0:T(2,128)S(1)}, f32[2,1024]{1,0:T(2,128)}, u32[]{:S(2)}) copy-start(f32[2,1024]{1,0:T(2,128)} %param.15) | copy-start | bytes 24580
  77.3 21.8 %copy-start.15 = (bf16[512,512]{1,0:T(8,128)(2,1)S(1)}, bf16[512,512]{1,0:T(8,128)(2,1)}, u32[]{:S(2)}) copy-start(bf16[512,512]{1,0:T(8,128)(2,1)} %get-tuple-element.92) | copy-start | bytes 1572868
  77.3 9.3 %collective-permute-start.7 = (bf16[48,2176]{1,0:T(8,128)(2,1)S(1)}, bf16[48,2176]{1,0:T(8,128)(2,1)S(1)}, u32[]{:S(2)}, u32[]{:S(2)}) collective-permute-start(bf16[48,2176]{1,0:T(8,128)(2,1)S(1)} %get-tuple-element.90), channel_id=1, source_target_pairs={{0,224},{32,0},{64,32},{96,64},{128,96},{160,128},{192,160},{224,1... | collective-permute-start | bytes 626696 | tf_op jit(solution)/shard_map/ppermute | solution.py:324
  83.3 7.1 %collective-permute-start.11 = (bf16[48,2176]{1,0:T(8,128)(2,1)S(1)}, bf16[48,2176]{1,0:T(8,128)(2,1)S(1)}, u32[]{:S(2)}, u32[]{:S(2)}) collective-permute-start(bf16[48,2176]{1,0:T(8,128)(2,1)S(1)} %get-tuple-element.118), channel_id=1, source_target_pairs={{0,32},{32,64},{64,96},{96,128},{128,160},{160,192},{192,224},{224... | collective-permute-start | bytes 626696 | tf_op jit(solution)/shard_map/ppermute | solution.py:330
  86.6 7.1 %collective-permute-start.8 = (bf16[48,2176]{1,0:T(8,128)(2,1)S(1)}, bf16[48,2176]{1,0:T(8,128)(2,1)S(1)}, u32[]{:S(2)}, u32[]{:S(2)}) collective-permute-start(bf16[48,2176]{1,0:T(8,128)(2,1)S(1)} %fusion.10), channel_id=1, source_target_pairs={{0,224},{32,0},{64,32},{96,64},{128,96},{160,128},{192,160},{224,1... | collective-permute-start | bytes 626696 | tf_op jit(solution)/shard_map/ppermute | solution.py:329
  94.8 7.5 %collective-permute-start.12 = (bf16[48,2176]{1,0:T(8,128)(2,1)S(1)}, bf16[48,2176]{1,0:T(8,128)(2,1)S(1)}, u32[]{:S(2)}, u32[]{:S(2)}) collective-permute-start(bf16[48,2176]{1,0:T(8,128)(2,1)S(1)} %get-tuple-element.121), channel_id=1, source_target_pairs={{0,32},{32,64},{64,96},{96,128},{128,160},{160,192},{192,224},{224... | collective-permute-start | bytes 626696 | tf_op jit(solution)/shard_map/ppermute | solution.py:330
  94.9 7.5 %collective-permute-start.9 = (bf16[48,2176]{1,0:T(8,128)(2,1)S(1)}, bf16[48,2176]{1,0:T(8,128)(2,1)S(1)}, u32[]{:S(2)}, u32[]{:S(2)}) collective-permute-start(bf16[48,2176]{1,0:T(8,128)(2,1)S(1)} %get-tuple-element.122), channel_id=1, source_target_pairs={{0,224},{32,0},{64,32},{96,64},{128,96},{160,128},{192,160},{224,1... | collective-permute-start | bytes 626696 | tf_op jit(solution)/shard_map/ppermute | solution.py:329
  99.0 8.2 %collective-permute-start.14 = (f32[2,2,512]{2,1,0:T(2,128)S(1)}, f32[2,2,512]{2,1,0:T(2,128)S(1)}, u32[]{:S(2)}, u32[]{:S(2)}) collective-permute-start(f32[2,2,512]{2,1,0:T(2,128)S(1)} %fusion.11), channel_id=1, source_target_pairs={{0,8},{8,0},{1,9},{9,1},{2,10},{10,2},{3,11},{11,3},{4,12},{12,4},... | collective-permute-start | bytes 24584 | tf_op jit(solution)/shard_map/ppermute | solution.py:30
  99.1 16.2 %collective-permute-start.15 = (bf16[512,512]{1,0:T(8,128)(2,1)S(1)}, bf16[512,512]{1,0:T(8,128)(2,1)}, u32[]{:S(2)}, u32[]{:S(2)}) collective-permute-start(bf16[512,512]{1,0:T(8,128)(2,1)S(1)} %copy-done.15), channel_id=1, source_target_pairs={{0,16},{16,0},{1,17},{17,1},{2,18},{18,2},{3,19},{19,3},{4,20},{20... | collective-permute-start | bytes 1572872 | tf_op jit(solution)/shard_map/ppermute | solution.py:30
  103.5 19.0 %copy-start = (bf16[512,1536]{1,0:T(8,128)(2,1)S(1)}, bf16[512,1536]{1,0:T(8,128)(2,1)}, u32[]{:S(2)}) copy-start(bf16[512,1536]{1,0:T(8,128)(2,1)} %get-tuple-element.102.refs_0_.mine) | copy-start | bytes 4718596
  103.6 6.9 %collective-permute-start.10 = (bf16[48,2176]{1,0:T(8,128)(2,1)S(1)}, bf16[48,2176]{1,0:T(8,128)(2,1)S(1)}, u32[]{:S(2)}, u32[]{:S(2)}) collective-permute-start(bf16[48,2176]{1,0:T(8,128)(2,1)S(1)} %get-tuple-element.120), channel_id=1, source_target_pairs={{0,224},{32,0},{64,32},{96,64},{128,96},{160,128},{192,160},{224,1... | collective-permute-start | bytes 626696 | tf_op jit(solution)/shard_map/ppermute | solution.py:329
  107.1 7.0 %collective-permute-start.13 = (bf16[48,2176]{1,0:T(8,128)(2,1)S(1)}, bf16[48,2176]{1,0:T(8,128)(2,1)S(1)}, u32[]{:S(2)}, u32[]{:S(2)}) collective-permute-start(bf16[48,2176]{1,0:T(8,128)(2,1)S(1)} %get-tuple-element.119), channel_id=1, source_target_pairs={{0,32},{32,64},{64,96},{96,128},{128,160},{160,192},{192,224},{224... | collective-permute-start | bytes 626696 | tf_op jit(solution)/shard_map/ppermute | solution.py:330
  115.2 27.6 %all-to-all-start.3 = ((bf16[8,48,1024]{2,1,0:T(8,128)(2,1)}), bf16[8,48,1024]{2,1,0:T(8,128)(2,1)}, u32[]{:S(2)}, u32[]{:S(2)}) async-start(bf16[8,48,1024]{2,1,0:T(8,128)(2,1)} %shard_map.97), calls=%async_computation.3 | async-start | bytes 1572864 | tf_op jit(solution)/shard_map/all_to_all | solution.py:308
  119.9 22.9 %collective-permute-start.16 = (bf16[512,1024]{1,0:T(8,128)(2,1)}, bf16[512,1024]{1,0:T(8,128)(2,1)}, u32[]{:S(2)}, u32[]{:S(2)}) collective-permute-start(bf16[512,1024]{1,0:T(8,128)(2,1)} %get-tuple-element.95), channel_id=1, source_target_pairs={{0,16},{16,0},{1,17},{17,1},{2,18},{18,2},{3,19},{19,3},{4,20},{20... | collective-permute-start | bytes 3145736 | tf_op jit(solution)/shard_map/ppermute | solution.py:30
  122.6 20.3 %collective-permute-start.17 = (bf16[512,512]{1,0:T(8,128)(2,1)}, bf16[512,512]{1,0:T(8,128)(2,1)}, u32[]{:S(2)}, u32[]{:S(2)}) collective-permute-start(bf16[512,512]{1,0:T(8,128)(2,1)} %collective-permute-done.15.got), channel_id=1, source_target_pairs={{0,8},{8,0},{1,9},{9,1},{2,10},{10,2},{3,11},{11,3},{4,12},{12,4},... | collective-permute-start | bytes 1572872 | tf_op jit(solution)/shard_map/ppermute | solution.py:30
  122.6 47.0 %collective-permute-start.18 = (bf16[512,1536]{1,0:T(8,128)(2,1)S(1)}, bf16[512,1536]{1,0:T(8,128)(2,1)S(1)}, u32[]{:S(2)}, u32[]{:S(2)}) collective-permute-start(bf16[512,1536]{1,0:T(8,128)(2,1)S(1)} %copy-done), channel_id=1, source_target_pairs={{0,8},{8,0},{1,9},{9,1},{2,10},{10,2},{3,11},{11,3},{4,12},{12,4},... | collective-permute-start | bytes 4718600 | tf_op jit(solution)/shard_map/ppermute | solution.py:30
  146.3 15.6 %all-to-all-start.4 = ((bf16[16,48,512]{2,1,0:T(8,128)(2,1)}), bf16[16,48,512]{2,1,0:T(8,128)(2,1)}, u32[]{:S(2)}, u32[]{:S(2)}) async-start(bf16[16,48,512]{2,1,0:T(8,128)(2,1)} %bitcast.64), calls=%async_computation.4 | async-start | bytes 1572864 | tf_op jit(solution)/shard_map/all_to_all | solution.py:308
  152.0 17.5 %collective-permute-start.19 = (bf16[512,1024]{1,0:T(8,128)(2,1)}, bf16[512,1024]{1,0:T(8,128)(2,1)}, u32[]{:S(2)}, u32[]{:S(2)}) collective-permute-start(bf16[512,1024]{1,0:T(8,128)(2,1)} %collective-permute-done.16.refs_1_), channel_id=1, source_target_pairs={{0,8},{8,0},{1,9},{9,1},{2,10},{10,2},{3,11},{11,3},{4,12},{12,4},... | collective-permute-start | bytes 3145736 | tf_op jit(solution)/shard_map/ppermute | solution.py:30
  164.1 15.3 %all-to-all-start.5 = ((bf16[16,48,512]{2,1,0:T(8,128)(2,1)}), bf16[16,48,512]{2,1,0:T(8,128)(2,1)}, u32[]{:S(2)}, u32[]{:S(2)}) async-start(bf16[16,48,512]{2,1,0:T(8,128)(2,1)} %get-tuple-element.99), calls=%async_computation.5 | async-start | bytes 1572864 | tf_op jit(solution)/shard_map/all_to_all | solution.py:308
  169.5 14.4 %copy-start.3 = (bf16[512,1536]{1,0:T(8,128)(2,1)}, bf16[512,1536]{1,0:T(8,128)(2,1)S(1)}, u32[]{:S(2)}) copy-start(bf16[512,1536]{1,0:T(8,128)(2,1)S(1)} %collective-permute-done.18.refs_2_.mine_sib) | copy-start | bytes 4718596
  184.0 19.5 %copy-start.14 = (bf16[512,512]{1,0:T(8,128)(2,1)S(1)}, bf16[512,512]{1,0:T(8,128)(2,1)}, u32[]{:S(2)}) copy-start(bf16[512,512]{1,0:T(8,128)(2,1)} %get-tuple-element.107) | copy-start | bytes 1572868
  184.0 7.5 %collective-permute-start.20 = (bf16[48,2176]{1,0:T(8,128)(2,1)S(1)}, bf16[48,2176]{1,0:T(8,128)(2,1)S(1)}, u32[]{:S(2)}, u32[]{:S(2)}) collective-permute-start(bf16[48,2176]{1,0:T(8,128)(2,1)S(1)} %get-tuple-element.105), channel_id=1, source_target_pairs={{0,224},{32,0},{64,32},{96,64},{128,96},{160,128},{192,160},{224,1... | collective-permute-start | bytes 626696 | tf_op jit(solution)/shard_map/ppermute | solution.py:324
  187.0 8.3 %collective-permute-start.24 = (bf16[48,2176]{1,0:T(8,128)(2,1)S(1)}, bf16[48,2176]{1,0:T(8,128)(2,1)S(1)}, u32[]{:S(2)}, u32[]{:S(2)}) collective-permute-start(bf16[48,2176]{1,0:T(8,128)(2,1)S(1)} %get-tuple-element.112), channel_id=1, source_target_pairs={{0,32},{32,64},{64,96},{96,128},{128,160},{160,192},{192,224},{224... | collective-permute-start | bytes 626696 | tf_op jit(solution)/shard_map/ppermute | solution.py:330
  191.5 7.8 %collective-permute-start.21 = (bf16[48,2176]{1,0:T(8,128)(2,1)S(1)}, bf16[48,2176]{1,0:T(8,128)(2,1)S(1)}, u32[]{:S(2)}, u32[]{:S(2)}) collective-permute-start(bf16[48,2176]{1,0:T(8,128)(2,1)S(1)} %fusion.5), channel_id=1, source_target_pairs={{0,224},{32,0},{64,32},{96,64},{128,96},{160,128},{192,160},{224,1... | collective-permute-start | bytes 626696 | tf_op jit(solution)/shard_map/ppermute | solution.py:329
  199.4 9.4 %collective-permute-start.25 = (bf16[48,2176]{1,0:T(8,128)(2,1)S(1)}, bf16[48,2176]{1,0:T(8,128)(2,1)S(1)}, u32[]{:S(2)}, u32[]{:S(2)}) collective-permute-start(bf16[48,2176]{1,0:T(8,128)(2,1)S(1)} %get-tuple-element.115), channel_id=1, source_target_pairs={{0,32},{32,64},{64,96},{96,128},{128,160},{160,192},{192,224},{224... | collective-permute-start | bytes 626696 | tf_op jit(solution)/shard_map/ppermute | solution.py:330
  199.5 9.3 %collective-permute-start.22 = (bf16[48,2176]{1,0:T(8,128)(2,1)S(1)}, bf16[48,2176]{1,0:T(8,128)(2,1)S(1)}, u32[]{:S(2)}, u32[]{:S(2)}) collective-permute-start(bf16[48,2176]{1,0:T(8,128)(2,1)S(1)} %get-tuple-element.116), channel_id=1, source_target_pairs={{0,224},{32,0},{64,32},{96,64},{128,96},{160,128},{192,160},{224,1... | collective-permute-start | bytes 626696 | tf_op jit(solution)/shard_map/ppermute | solution.py:329
  203.5 15.3 %collective-permute-start.27 = (bf16[512,512]{1,0:T(8,128)(2,1)S(1)}, bf16[512,512]{1,0:T(8,128)(2,1)S(1)}, u32[]{:S(2)}, u32[]{:S(2)}) collective-permute-start(bf16[512,512]{1,0:T(8,128)(2,1)S(1)} %copy-done.14), channel_id=1, source_target_pairs={{0,16},{16,0},{1,17},{17,1},{2,18},{18,2},{3,19},{19,3},{4,20},{20... | collective-permute-start | bytes 1572872 | tf_op jit(solution)/shard_map/ppermute | solution.py:30
  208.9 5.9 %collective-permute-start.23 = (bf16[48,2176]{1,0:T(8,128)(2,1)S(1)}, bf16[48,2176]{1,0:T(8,128)(2,1)S(1)}, u32[]{:S(2)}, u32[]{:S(2)}) collective-permute-start(bf16[48,2176]{1,0:T(8,128)(2,1)S(1)} %get-tuple-element.114), channel_id=1, source_target_pairs={{0,224},{32,0},{64,32},{96,64},{128,96},{160,128},{192,160},{224,1... | collective-permute-start | bytes 626696 | tf_op jit(solution)/shard_map/ppermute | solution.py:329
  210.7 7.0 %collective-permute-start.26 = (bf16[48,2176]{1,0:T(8,128)(2,1)S(1)}, bf16[48,2176]{1,0:T(8,128)(2,1)S(1)}, u32[]{:S(2)}, u32[]{:S(2)}) collective-permute-start(bf16[48,2176]{1,0:T(8,128)(2,1)S(1)} %get-tuple-element.113), channel_id=1, source_target_pairs={{0,32},{32,64},{64,96},{96,128},{128,160},{160,192},{192,224},{224... | collective-permute-start | bytes 626696 | tf_op jit(solution)/shard_map/ppermute | solution.py:330
  218.8 20.3 %copy-start.8 = (bf16[512,512]{1,0:T(8,128)(2,1)}, bf16[512,512]{1,0:T(8,128)(2,1)S(1)}, u32[]{:S(2)}) copy-start(bf16[512,512]{1,0:T(8,128)(2,1)S(1)} %collective-permute-done.27.got) | copy-start | bytes 1572868
  218.8 20.3 %all-to-all-start.6 = ((bf16[8,48,1024]{2,1,0:T(8,128)(2,1)}), bf16[8,48,1024]{2,1,0:T(8,128)(2,1)S(1)}, u32[]{:S(2)}, u32[]{:S(2)}) async-start(bf16[8,48,1024]{2,1,0:T(8,128)(2,1)} %shard_map.101), calls=%async_computation.6 | async-start | bytes 1572864 | tf_op jit(solution)/shard_map/all_to_all | solution.py:308
  223.3 1.9 collective-permute-start.28
  225.2 13.9 %copy-start.9 = (bf16[512,512]{1,0:T(8,128)(2,1)}, bf16[512,512]{1,0:T(8,128)(2,1)S(1)}, u32[]{:S(2)}) copy-start(bf16[512,512]{1,0:T(8,128)(2,1)S(1)} %collective-permute-done.28.got_sib) | copy-start | bytes 1572868
  (4 other events, 4.9 us)

commit v5 on v4

--- a/solution.py
+++ b/solution.py
@@ -362,8 +362,8 @@
     local_ids = all_ids - owner * vocab_rows
     inside = (local_ids >= 0) & (local_ids < vocab_rows)
     local_ids = jnp.clip(local_ids, 0, vocab_rows - 1)
+    local_ids, g_got = together(local_ids, g_got)
     mine[0], d_out = pack(0, (stay, ((0, 2),)), xl_arg, *after(g_out, w_gate, w_up, w_down))
-    local_ids, g_got, mine[0], d_out = together(local_ids, g_got, mine[0], d_out)
     u_got = swap(u_out, "xl")
     picked = embed_table.at[local_ids].get(mode="promise_in_bounds")
     picked = jnp.where(inside[:, None], picked, jnp.zeros((), BF)).reshape(2, -1, rows, width)
@@ -379,11 +379,10 @@
     mine[1], gu_out, last_out = pack(
         1, (stay, ((0, 0), (0, 1)), ((0, 2),)), xl_arg, *after(both, w_gate, w_up, w_down)
     )
-    pieces, mine_sib[0], mine[1], gu_out, last_out = together(
-        pieces, mine_sib[0], mine[1], gu_out, last_out
+    pieces, mine_sib[0], gu_sib, mine[1], gu_out, last_out = together(
+        pieces, mine_sib[0], gu_sib, mine[1], gu_out, last_out
     )
     x, sent = first(pieces)
-    sent, gu_sib = together(sent, gu_sib)
     others, others_sib = (gu_got,), (gu_sib,)
     mine_sib[1] = swap(after(x, mine[1]), "c")
 

time: 262 us -> 263 us (level)
    all_to_all x7, waiting for transfers between devices: 54.2 us -> 57.2 us  [exchange(): return lax.all_to_all(value, axes, 0, 0, tiled=True)]
  transfers between devices with their start and end apart: 36 -> 36, of which waited for: 21 -> 20; matrix products, arithmetic and copies ran while one was open for 4% -> 4% of each run, Pallas kernels for 7% -> 7%
where the time goes in v5:
time: 263 us; the launch traced here: 261 us
  waiting for transfers between devices  119 us (45%)
  starting transfers between devices  78.2 us (30%)
  Pallas kernels  33.5 us (13%)
  blocking collectives  15.6 us (6%)
  local copies, waits for them, and re-layouts  10.4 us (4%)
  other arithmetic  3.97 us (2%)
    all_to_all x7, waiting for transfers between devices, exchange(): return lax.all_to_all(value, axes, 0, 0, tiled=True)  57.2 us
    all_to_all x7, starting transfers between devices, exchange(): return lax.all_to_all(value, axes, 0, 0, tiled=True)  34.7 us
    ppermute x15, waiting for transfers between devices, swap(): return lax.ppermute(value, axis, turn(2, 1))  29 us
    ppermute x6, starting transfers between devices, scatter_sum_z(): down = lax.ppermute(down, 'z', turn(Z, -1))  20.1 us
    all_to_all x1, blocking collectives, exchange(): return lax.all_to_all(value, axes, 0, 0, tiled=True)  15.6 us
    ppermute x6, waiting for transfers between devices, scatter_sum_z(): down = lax.ppermute(down, 'z', turn(Z, -1))  14 us
    ppermute x15, starting transfers between devices, swap(): return lax.ppermute(value, axis, turn(2, 1))  13.2 us
    ppermute x6, waiting for transfers between devices, scatter_sum_z(): up = lax.ppermute(up, 'z', turn(Z, 1))  12.1 us
  transfers between devices with their start and end apart: 36, of which 20 were waited for; matrix products, arithmetic and copies ran while one was open for 4% of the time, Pallas kernels for 7%

profile of v5, /device:TPU:2, one launch (start us, length us, event | category | flops | bytes accessed | tf_op | source)
XLA Modules:
  0.0 261.5 jit_solution(1542304348348837741)
XLA Ops:
  0.0 2.1 collective-permute-start
  4.3 2.1 shard_map.91
  8.2 4.3 %all-to-all-start = ((s32[8,2,48]{2,1,0:T(2,128)}), s32[8,2,48]{2,1,0:T(2,128)S(1)}, u32[]{:S(2)}, u32[]{:S(2)}) async-start(s32[8,2,48]{2,1,0:T(2,128)} %broadcast_in_dim.22), calls=%async_computation | async-start | bytes 16384 | tf_op jit(solution)/shard_map/all_to_all | solution.py:308
  13.7 4.1 %all-to-all-done = s32[8,2,48]{2,1,0:T(2,128)S(1)} async-done(((s32[8,2,48]{2,1,0:T(2,128)}), s32[8,2,48]{2,1,0:T(2,128)S(1)}, u32[]{:S(2)}, u32[]{:S(2)}) %all-to-all-start) | async-done | bytes 3104 | tf_op jit(solution)/shard_map/all_to_all | solution.py:308
  18.0 3.7 %collective-permute-done.2.a = bf16[512,512]{1,0:T(8,128)(2,1)S(1)} collective-permute-done((bf16[512,512]{1,0:T(8,128)(2,1)}, bf16[512,512]{1,0:T(8,128)(2,1)S(1)}, u32[]{:S(2)}, u32[]{:S(2)}) %collective-permute-start.2) | collective-permute-done | bytes 524320 | tf_op jit(solution)/shard_map/ppermute | solution.py:30
  21.7 5.9 %gather_fusion = bf16[768,512]{1,0:T(8,128)(2,1)S(1)} fusion(bf16[4752,512]{1,0:T(8,128)(2,1)} %param.10, s32[1024]{0:T(1024)S(1)} %pad_clamp_fusion), kind=kCustom, calls=%fused_computation | custom fusion | bytes 1575936 | tf_op jit(solution)/shard_map/gather | solution.py:368
  27.8 3.4 %collective-permute-done.3.b = bf16[512,512]{1,0:T(8,128)(2,1)S(1)} collective-permute-done((bf16[512,512]{1,0:T(8,128)(2,1)}, bf16[512,512]{1,0:T(8,128)(2,1)S(1)}, u32[]{:S(2)}, u32[]{:S(2)}) %collective-permute-start.3) | collective-permute-done | bytes 524320 | tf_op jit(solution)/shard_map/ppermute | solution.py:30
  31.3 2.5 shard_map.92
  35.1 2.2 shard_map.93.refs_1_
  37.5 4.5 %all-to-all-start.1 = ((bf16[8,48,512]{2,1,0:T(8,128)(2,1)}), bf16[8,48,512]{2,1,0:T(8,128)(2,1)S(1)}, u32[]{:S(2)}, u32[]{:S(2)}) async-start(bf16[8,48,512]{2,1,0:T(8,128)(2,1)} %fusion), calls=%async_computation.1 | async-start | bytes 786432 | tf_op jit(solution)/shard_map/all_to_all | solution.py:308
  42.0 2.9 %shard_map.94 = (bf16[512,1536]{1,0:T(8,128)(2,1)}, bf16[512,1024]{1,0:T(8,128)(2,1)}, bf16[512,512]{1,0:T(8,128)(2,1)}) custom-call(s32[1]{0:T(128)} %bitcast.xl_ref, bf16[2,512,1024]{2,1,0:T(8,128)(2,1)} %gate.3, bf16[2,512,1024]{2,1,0:T(8,128)(2,1)} %up.3, bf16[2,1024,512]{2,1,0:T(8,128)(2,1)} %down.3), custom_call_target="tpu_custom_call" | custom-call | bytes 6291456 | tf_op jit(solution)/shard_map/pallas_call | solution.py:74
  44.8 7.4 %all-to-all-done.1.pieces = bf16[8,48,512]{2,1,0:T(8,128)(2,1)S(1)} async-done(((bf16[8,48,512]{2,1,0:T(8,128)(2,1)}), bf16[8,48,512]{2,1,0:T(8,128)(2,1)S(1)}, u32[]{:S(2)}, u32[]{:S(2)}) %all-to-all-start.1) | async-done | bytes 393248 | tf_op jit(solution)/shard_map/all_to_all | solution.py:308
  53.0 2.0 shard_map.95
  55.0 6.1 %all-to-all-start.2 = ((bf16[16,48,512]{2,1,0:T(8,128)(2,1)}), bf16[16,48,512]{2,1,0:T(8,128)(2,1)}, u32[]{:S(2)}, u32[]{:S(2)}) async-start(bf16[16,48,512]{2,1,0:T(8,128)(2,1)} %get-tuple-element.78), calls=%async_computation.2 | async-start | bytes 1572864 | tf_op jit(solution)/shard_map/all_to_all | solution.py:308
  61.1 11.9 %all-to-all-done.2 = bf16[16,48,512]{2,1,0:T(8,128)(2,1)} async-done(((bf16[16,48,512]{2,1,0:T(8,128)(2,1)}), bf16[16,48,512]{2,1,0:T(8,128)(2,1)}, u32[]{:S(2)}, u32[]{:S(2)}) %all-to-all-start.2) | async-done | bytes 786464 | tf_op jit(solution)/shard_map/all_to_all | solution.py:308
  74.3 4.0 %shard_map.96 = (bf16[8,48,2176]{2,1,0:T(8,128)(2,1)S(1)}, bf16[48,2176]{1,0:T(8,128)(2,1)S(1)}) custom-call(s32[2]{0:T(128)S(1)} %pad_add_fusion.1.at_ref, bf16[2,8,48,512]{3,2,1,0:T(8,128)(2,1)} %bitcast.12.x, f32[2,2,512]{2,1,0:T(2,128)S(1)} %pad_maximum_fusion.1.gains, bf16[512,1536]{1,0:T(8,128)(2,1)S(1)} %copy-done.1, bf16[512,1024]{1,0:T(8,128)(2,1)S(1)} %copy-done.4, ...), custom_call_target="tpu_custom_call" | custom-call | flops 1610612736 | bytes 6553600 | tf_op jit(solution)/shard_map/pallas_call | solution.py:175
  78.4 5.9 %collective-permute-start.7 = (bf16[48,2176]{1,0:T(8,128)(2,1)S(1)}, bf16[48,2176]{1,0:T(8,128)(2,1)S(1)}, u32[]{:S(2)}, u32[]{:S(2)}) collective-permute-start(bf16[48,2176]{1,0:T(8,128)(2,1)S(1)} %get-tuple-element.84), channel_id=1, source_target_pairs={{0,224},{32,0},{64,32},{96,64},{128,96},{160,128},{192,160},{224,1... | collective-permute-start | bytes 626696 | tf_op jit(solution)/shard_map/ppermute | solution.py:324
  84.5 3.2 %collective-permute-done.7 = bf16[48,2176]{1,0:T(8,128)(2,1)S(1)} collective-permute-done((bf16[48,2176]{1,0:T(8,128)(2,1)S(1)}, bf16[48,2176]{1,0:T(8,128)(2,1)S(1)}, u32[]{:S(2)}, u32[]{:S(2)}) %collective-permute-start.7) | collective-permute-done | bytes 208928 | tf_op jit(solution)/shard_map/ppermute | solution.py:324
  87.7 3.8 %collective-permute-start.8 = (bf16[48,2176]{1,0:T(8,128)(2,1)S(1)}, bf16[48,2176]{1,0:T(8,128)(2,1)S(1)}, u32[]{:S(2)}, u32[]{:S(2)}) collective-permute-start(bf16[48,2176]{1,0:T(8,128)(2,1)S(1)} %fusion.10), channel_id=1, source_target_pairs={{0,224},{32,0},{64,32},{96,64},{128,96},{160,128},{192,160},{224,1... | collective-permute-start | bytes 626696 | tf_op jit(solution)/shard_map/ppermute | solution.py:329
  91.5 3.3 %collective-permute-done.8 = bf16[48,2176]{1,0:T(8,128)(2,1)S(1)} collective-permute-done((bf16[48,2176]{1,0:T(8,128)(2,1)S(1)}, bf16[48,2176]{1,0:T(8,128)(2,1)S(1)}, u32[]{:S(2)}, u32[]{:S(2)}) %collective-permute-start.8) | collective-permute-done | bytes 208928 | tf_op jit(solution)/shard_map/ppermute | solution.py:329
  96.1 3.9 %collective-permute-start.9 = (bf16[48,2176]{1,0:T(8,128)(2,1)S(1)}, bf16[48,2176]{1,0:T(8,128)(2,1)S(1)}, u32[]{:S(2)}, u32[]{:S(2)}) collective-permute-start(bf16[48,2176]{1,0:T(8,128)(2,1)S(1)} %get-tuple-element.116), channel_id=1, source_target_pairs={{0,224},{32,0},{64,32},{96,64},{128,96},{160,128},{192,160},{224,1... | collective-permute-start | bytes 626696 | tf_op jit(solution)/shard_map/ppermute | solution.py:329
  104.7 3.6 %collective-permute-start.10 = (bf16[48,2176]{1,0:T(8,128)(2,1)S(1)}, bf16[48,2176]{1,0:T(8,128)(2,1)S(1)}, u32[]{:S(2)}, u32[]{:S(2)}) collective-permute-start(bf16[48,2176]{1,0:T(8,128)(2,1)S(1)} %get-tuple-element.114), channel_id=1, source_target_pairs={{0,224},{32,0},{64,32},{96,64},{128,96},{160,128},{192,160},{224,1... | collective-permute-start | bytes 626696 | tf_op jit(solution)/shard_map/ppermute | solution.py:329
  108.4 3.2 %collective-permute-done.10.a = bf16[48,2176]{1,0:T(8,128)(2,1)S(1)} collective-permute-done((bf16[48,2176]{1,0:T(8,128)(2,1)S(1)}, bf16[48,2176]{1,0:T(8,128)(2,1)S(1)}, u32[]{:S(2)}, u32[]{:S(2)}) %collective-permute-start.10) | collective-permute-done | bytes 208928 | tf_op jit(solution)/shard_map/ppermute | solution.py:329
  111.6 3.7 %collective-permute-done.13.b = bf16[48,2176]{1,0:T(8,128)(2,1)S(1)} collective-permute-done((bf16[48,2176]{1,0:T(8,128)(2,1)S(1)}, bf16[48,2176]{1,0:T(8,128)(2,1)S(1)}, u32[]{:S(2)}, u32[]{:S(2)}) %collective-permute-start.13) | collective-permute-done | bytes 208928 | tf_op jit(solution)/shard_map/ppermute | solution.py:330
  116.4 4.2 %all-to-all-start.3 = ((bf16[8,48,1024]{2,1,0:T(8,128)(2,1)}), bf16[8,48,1024]{2,1,0:T(8,128)(2,1)}, u32[]{:S(2)}, u32[]{:S(2)}) async-start(bf16[8,48,1024]{2,1,0:T(8,128)(2,1)} %shard_map.97), calls=%async_computation.3 | async-start | bytes 1572864 | tf_op jit(solution)/shard_map/all_to_all | solution.py:308
  120.6 2.9 %collective-permute-start.16 = (bf16[512,1024]{1,0:T(8,128)(2,1)}, bf16[512,1024]{1,0:T(8,128)(2,1)}, u32[]{:S(2)}, u32[]{:S(2)}) collective-permute-start(bf16[512,1024]{1,0:T(8,128)(2,1)} %get-tuple-element.89), channel_id=1, source_target_pairs={{0,16},{16,0},{1,17},{17,1},{2,18},{18,2},{3,19},{19,3},{4,20},{20... | collective-permute-start | bytes 3145736 | tf_op jit(solution)/shard_map/ppermute | solution.py:30
  124.0 19.9 %collective-permute-done.16.refs_1_ = bf16[512,1024]{1,0:T(8,128)(2,1)} collective-permute-done((bf16[512,1024]{1,0:T(8,128)(2,1)}, bf16[512,1024]{1,0:T(8,128)(2,1)}, u32[]{:S(2)}, u32[]{:S(2)}) %collective-permute-start.16) | collective-permute-done | bytes 1048608 | tf_op jit(solution)/shard_map/ppermute | solution.py:30
  144.0 3.4 %shard_map.98 = bf16[2,8,48,512]{3,2,1,0:T(8,128)(2,1)} custom-call(s32[1]{0:T(128)} %bitcast.xl_ref, bf16[8,48,1024]{2,1,0:T(8,128)(2,1)} %all-to-all-done.3.act, bf16[512,1536]{1,0:T(8,128)(2,1)} %get-tuple-element.68.refs_0_.mine, bf16[512,512]{1,0:T(8,128)(2,1)} %collective-permute-done.15.got, bf16[512,1536]{1,0:T(8,128)(2,1)} %copy-done.2, ...), custom_call_target="tpu_custom_call" | custom-call | flops 805306368 | bytes 3670016 | tf_op jit(solution)/shard_map/pallas_call | solution.py:253
  147.4 5.6 %all-to-all-start.4 = ((bf16[16,48,512]{2,1,0:T(8,128)(2,1)}), bf16[16,48,512]{2,1,0:T(8,128)(2,1)}, u32[]{:S(2)}, u32[]{:S(2)}) async-start(bf16[16,48,512]{2,1,0:T(8,128)(2,1)} %bitcast.64), calls=%async_computation.4 | async-start | bytes 1572864 | tf_op jit(solution)/shard_map/all_to_all | solution.py:308
  153.0 9.8 %all-to-all-done.4.pieces = bf16[16,48,512]{2,1,0:T(8,128)(2,1)} async-done(((bf16[16,48,512]{2,1,0:T(8,128)(2,1)}), bf16[16,48,512]{2,1,0:T(8,128)(2,1)}, u32[]{:S(2)}, u32[]{:S(2)}) %all-to-all-start.4) | async-done | bytes 786464 | tf_op jit(solution)/shard_map/all_to_all | solution.py:308
  162.8 2.2 shard_map.99
  165.1 5.5 %all-to-all-start.5 = ((bf16[16,48,512]{2,1,0:T(8,128)(2,1)}), bf16[16,48,512]{2,1,0:T(8,128)(2,1)}, u32[]{:S(2)}, u32[]{:S(2)}) async-start(bf16[16,48,512]{2,1,0:T(8,128)(2,1)} %get-tuple-element.93), calls=%async_computation.5 | async-start | bytes 1572864 | tf_op jit(solution)/shard_map/all_to_all | solution.py:308
  170.6 9.8 %all-to-all-done.5 = bf16[16,48,512]{2,1,0:T(8,128)(2,1)} async-done(((bf16[16,48,512]{2,1,0:T(8,128)(2,1)}), bf16[16,48,512]{2,1,0:T(8,128)(2,1)}, u32[]{:S(2)}, u32[]{:S(2)}) %all-to-all-start.5) | async-done | bytes 786464 | tf_op jit(solution)/shard_map/all_to_all | solution.py:308
  180.3 4.6 %shard_map.100 = (bf16[8,48,2176]{2,1,0:T(8,128)(2,1)S(1)}, bf16[48,2176]{1,0:T(8,128)(2,1)S(1)}) custom-call(s32[2]{0:T(128)S(1)} %pad_add_fusion.1.at_ref, bf16[2,8,48,512]{3,2,1,0:T(8,128)(2,1)} %bitcast.23.x, f32[2,2,512]{2,1,0:T(2,128)S(1)} %pad_maximum_fusion.1.gains, bf16[512,1536]{1,0:T(8,128)(2,1)S(1)} %copy-done, ...), custom_call_target="tpu_custom_call" | custom-call | flops 1610612736 | bytes 6553600 | tf_op jit(solution)/shard_map/pallas_call | solution.py:175
  185.0 3.0 %collective-permute-start.20 = (bf16[48,2176]{1,0:T(8,128)(2,1)S(1)}, bf16[48,2176]{1,0:T(8,128)(2,1)S(1)}, u32[]{:S(2)}, u32[]{:S(2)}) collective-permute-start(bf16[48,2176]{1,0:T(8,128)(2,1)S(1)} %get-tuple-element.99), channel_id=1, source_target_pairs={{0,224},{32,0},{64,32},{96,64},{128,96},{160,128},{192,160},{224,1... | collective-permute-start | bytes 626696 | tf_op jit(solution)/shard_map/ppermute | solution.py:324
  188.1 4.1 %collective-permute-done.20 = bf16[48,2176]{1,0:T(8,128)(2,1)S(1)} collective-permute-done((bf16[48,2176]{1,0:T(8,128)(2,1)S(1)}, bf16[48,2176]{1,0:T(8,128)(2,1)S(1)}, u32[]{:S(2)}, u32[]{:S(2)}) %collective-permute-start.20) | collective-permute-done | bytes 208928 | tf_op jit(solution)/shard_map/ppermute | solution.py:324
  192.2 3.8 %collective-permute-start.21 = (bf16[48,2176]{1,0:T(8,128)(2,1)S(1)}, bf16[48,2176]{1,0:T(8,128)(2,1)S(1)}, u32[]{:S(2)}, u32[]{:S(2)}) collective-permute-start(bf16[48,2176]{1,0:T(8,128)(2,1)S(1)} %fusion.5), channel_id=1, source_target_pairs={{0,224},{32,0},{64,32},{96,64},{128,96},{160,128},{192,160},{224,1... | collective-permute-start | bytes 626696 | tf_op jit(solution)/shard_map/ppermute | solution.py:329
  196.0 3.6 %collective-permute-done.21 = bf16[48,2176]{1,0:T(8,128)(2,1)S(1)} collective-permute-done((bf16[48,2176]{1,0:T(8,128)(2,1)S(1)}, bf16[48,2176]{1,0:T(8,128)(2,1)S(1)}, u32[]{:S(2)}, u32[]{:S(2)}) %collective-permute-start.21) | collective-permute-done | bytes 208928 | tf_op jit(solution)/shard_map/ppermute | solution.py:329
  200.3 3.5 %collective-permute-start.22 = (bf16[48,2176]{1,0:T(8,128)(2,1)S(1)}, bf16[48,2176]{1,0:T(8,128)(2,1)S(1)}, u32[]{:S(2)}, u32[]{:S(2)}) collective-permute-start(bf16[48,2176]{1,0:T(8,128)(2,1)S(1)} %get-tuple-element.110), channel_id=1, source_target_pairs={{0,224},{32,0},{64,32},{96,64},{128,96},{160,128},{192,160},{224,1... | collective-permute-start | bytes 626696 | tf_op jit(solution)/shard_map/ppermute | solution.py:329
  205.2 4.2 %collective-permute-done.25 = bf16[48,2176]{1,0:T(8,128)(2,1)S(1)} collective-permute-done((bf16[48,2176]{1,0:T(8,128)(2,1)S(1)}, bf16[48,2176]{1,0:T(8,128)(2,1)S(1)}, u32[]{:S(2)}, u32[]{:S(2)}) %collective-permute-start.25) | collective-permute-done | bytes 208928 | tf_op jit(solution)/shard_map/ppermute | solution.py:330
  211.6 3.8 %collective-permute-done.23.a = bf16[48,2176]{1,0:T(8,128)(2,1)S(1)} collective-permute-done((bf16[48,2176]{1,0:T(8,128)(2,1)S(1)}, bf16[48,2176]{1,0:T(8,128)(2,1)S(1)}, u32[]{:S(2)}, u32[]{:S(2)}) %collective-permute-start.23) | collective-permute-done | bytes 208928 | tf_op jit(solution)/shard_map/ppermute | solution.py:329
  215.4 2.6 %collective-permute-done.26.b = bf16[48,2176]{1,0:T(8,128)(2,1)S(1)} collective-permute-done((bf16[48,2176]{1,0:T(8,128)(2,1)S(1)}, bf16[48,2176]{1,0:T(8,128)(2,1)S(1)}, u32[]{:S(2)}, u32[]{:S(2)}) %collective-permute-start.26) | collective-permute-done | bytes 208928 | tf_op jit(solution)/shard_map/ppermute | solution.py:330
  219.1 4.5 %all-to-all-start.6 = ((bf16[8,48,1024]{2,1,0:T(8,128)(2,1)}), bf16[8,48,1024]{2,1,0:T(8,128)(2,1)S(1)}, u32[]{:S(2)}, u32[]{:S(2)}) async-start(bf16[8,48,1024]{2,1,0:T(8,128)(2,1)} %shard_map.101), calls=%async_computation.6 | async-start | bytes 1572864 | tf_op jit(solution)/shard_map/all_to_all | solution.py:308
  223.6 1.9 collective-permute-done.28.got_sib
  225.5 14.2 %all-to-all-done.6.act = bf16[8,48,1024]{2,1,0:T(8,128)(2,1)S(1)} async-done(((bf16[8,48,1024]{2,1,0:T(8,128)(2,1)}), bf16[8,48,1024]{2,1,0:T(8,128)(2,1)S(1)}, u32[]{:S(2)}, u32[]{:S(2)}) %all-to-all-start.6) | async-done | bytes 786464 | tf_op jit(solution)/shard_map/all_to_all | solution.py:308
  240.6 3.4 %shard_map.102 = bf16[2,8,48,512]{3,2,1,0:T(8,128)(2,1)} custom-call(s32[1]{0:T(128)} %bitcast.xl_ref, bf16[8,48,1024]{2,1,0:T(8,128)(2,1)} %copy-done.6, bf16[512,1536]{1,0:T(8,128)(2,1)} %get-tuple-element.96.refs_0_.mine, bf16[512,512]{1,0:T(8,128)(2,1)} %copy-done.8, bf16[512,1536]{1,0:T(8,128)(2,1)} %copy-done.3, bf16[512,512]{1,0:T(8,128)(2,1)} %copy-done.9), custom_call_target="tpu_custom_call" | custom-call | flops 805306368 | bytes 3670016 | tf_op jit(solution)/shard_map/pallas_call | solution.py:253
  244.0 15.6 %all_to_all.40.pieces = bf16[16,48,512]{2,1,0:T(8,128)(2,1)} all-to-all(bf16[16,48,512]{2,1,0:T(8,128)(2,1)} %bitcast.65), channel_id=1, replica_groups=mesh['z'=8,'xl'=2,'c'=2,'xh'=2,'y'=4] {'xl','xh','y'}, dimensions={0} | all-to-all | bytes 1572864 | tf_op jit(solution)/shard_map/all_to_all | solution.py:308
  259.6 1.9 shard_map.103
  (104 shorter events, 23.3 us)
Async XLA Ops:
  0.0 6.4 %collective-permute-start = (s32[48]{0:T(128)}, s32[48]{0:T(128)S(1)}, u32[]{:S(2)}, u32[]{:S(2)}) collective-permute-start(s32[48]{0:T(128)} %param.9), channel_id=1, source_target_pairs={{0,4},{4,0},{1,5},{5,1},{2,6},{6,2},{3,7},{7,3},{8,12},{12,8},{9,1... | collective-permute-start | bytes 584 | tf_op jit(solution)/shard_map/ppermute | solution.py:30
  2.1 4.3 %collective-permute-start.1 = (f32[2,512]{1,0:T(2,128)}, f32[2,512]{1,0:T(2,128)S(1)}, u32[]{:S(2)}, u32[]{:S(2)}) collective-permute-start(f32[2,512]{1,0:T(2,128)} %param.11), channel_id=1, source_target_pairs={{0,16},{16,0},{1,17},{17,1},{2,18},{18,2},{3,19},{19,3},{4,20},{20... | collective-permute-start | bytes 12296 | tf_op jit(solution)/shard_map/ppermute | solution.py:30
  6.5 15.2 %collective-permute-start.2 = (bf16[512,512]{1,0:T(8,128)(2,1)}, bf16[512,512]{1,0:T(8,128)(2,1)S(1)}, u32[]{:S(2)}, u32[]{:S(2)}) collective-permute-start(bf16[512,512]{1,0:T(8,128)(2,1)} %get-tuple-element.57), channel_id=1, source_target_pairs={{0,16},{16,0},{1,17},{17,1},{2,18},{18,2},{3,19},{19,3},{4,20},{20... | collective-permute-start | bytes 1572872 | tf_op jit(solution)/shard_map/ppermute | solution.py:30
  8.2 9.6 %all-to-all-start = ((s32[8,2,48]{2,1,0:T(2,128)}), s32[8,2,48]{2,1,0:T(2,128)S(1)}, u32[]{:S(2)}, u32[]{:S(2)}) async-start(s32[8,2,48]{2,1,0:T(2,128)} %broadcast_in_dim.22), calls=%async_computation | async-start | bytes 16384 | tf_op jit(solution)/shard_map/all_to_all | solution.py:308
  12.6 18.6 %collective-permute-start.3 = (bf16[512,512]{1,0:T(8,128)(2,1)}, bf16[512,512]{1,0:T(8,128)(2,1)S(1)}, u32[]{:S(2)}, u32[]{:S(2)}) collective-permute-start(bf16[512,512]{1,0:T(8,128)(2,1)} %get-tuple-element.59), channel_id=1, source_target_pairs={{0,16},{16,0},{1,17},{17,1},{2,18},{18,2},{3,19},{19,3},{4,20},{20... | collective-permute-start | bytes 1572872 | tf_op jit(solution)/shard_map/ppermute | solution.py:30
  21.7 5.9 %copy-start.10 = (bf16[512,512]{1,0:T(8,128)(2,1)}, bf16[512,512]{1,0:T(8,128)(2,1)S(1)}, u32[]{:S(2)}) copy-start(bf16[512,512]{1,0:T(8,128)(2,1)S(1)} %collective-permute-done.2.a) | copy-start | bytes 1572868
  31.2 2.7 %collective-permute-start.4 = (bf16[8,48,512]{2,1,0:T(8,128)(2,1)S(1)}, bf16[8,48,512]{2,1,0:T(8,128)(2,1)S(1)}, u32[]{:S(2)}, u32[]{:S(2)}) collective-permute-start(bf16[8,48,512]{2,1,0:T(8,128)(2,1)S(1)} %dynamic-slice_bitcast_fusion), channel_id=1, source_target_pairs={{0,8},{8,0},{1,9},{9,1},{2,10},{10,2},{3,11},{11,3},{4,12},{12,4},... | collective-permute-start | bytes 1179656 | tf_op jit(solution)/shard_map/ppermute | solution.py:30
  34.7 17.5 %collective-permute-start.5 = (bf16[512,1536]{1,0:T(8,128)(2,1)}, bf16[512,1536]{1,0:T(8,128)(2,1)S(1)}, u32[]{:S(2)}, u32[]{:S(2)}) collective-permute-start(bf16[512,1536]{1,0:T(8,128)(2,1)} %get-tuple-element.68.refs_0_.mine), channel_id=1, source_target_pairs={{0,8},{8,0},{1,9},{9,1},{2,10},{10,2},{3,11},{11,3},{4,12},{12,4},... | collective-permute-start | bytes 4718600 | tf_op jit(solution)/shard_map/ppermute | solution.py:30
  37.3 14.9 %collective-permute-start.6 = (bf16[512,1024]{1,0:T(8,128)(2,1)}, bf16[512,1024]{1,0:T(8,128)(2,1)}, u32[]{:S(2)}, u32[]{:S(2)}) collective-permute-start(bf16[512,1024]{1,0:T(8,128)(2,1)} %shard_map.93.refs_1_), channel_id=1, source_target_pairs={{0,8},{8,0},{1,9},{9,1},{2,10},{10,2},{3,11},{11,3},{4,12},{12,4},... | collective-permute-start | bytes 3145736 | tf_op jit(solution)/shard_map/ppermute | solution.py:30
  37.5 14.7 %all-to-all-start.1 = ((bf16[8,48,512]{2,1,0:T(8,128)(2,1)}), bf16[8,48,512]{2,1,0:T(8,128)(2,1)S(1)}, u32[]{:S(2)}, u32[]{:S(2)}) async-start(bf16[8,48,512]{2,1,0:T(8,128)(2,1)} %fusion), calls=%async_computation.1 | async-start | bytes 786432 | tf_op jit(solution)/shard_map/all_to_all | solution.py:308
  44.8 28.3 %copy-start.1 = (bf16[512,1536]{1,0:T(8,128)(2,1)S(1)}, bf16[512,1536]{1,0:T(8,128)(2,1)}, u32[]{:S(2)}) copy-start(bf16[512,1536]{1,0:T(8,128)(2,1)} %get-tuple-element.68.refs_0_.mine) | copy-start | bytes 4718596
  52.2 26.1 %copy-start.2 = (bf16[512,1536]{1,0:T(8,128)(2,1)}, bf16[512,1536]{1,0:T(8,128)(2,1)S(1)}, u32[]{:S(2)}) copy-start(bf16[512,1536]{1,0:T(8,128)(2,1)S(1)} %collective-permute-done.5.refs_2_.mine_sib) | copy-start | bytes 4718596
  55.0 18.1 %all-to-all-start.2 = ((bf16[16,48,512]{2,1,0:T(8,128)(2,1)}), bf16[16,48,512]{2,1,0:T(8,128)(2,1)}, u32[]{:S(2)}, u32[]{:S(2)}) async-start(bf16[16,48,512]{2,1,0:T(8,128)(2,1)} %get-tuple-element.78), calls=%async_computation.2 | async-start | bytes 1572864 | tf_op jit(solution)/shard_map/all_to_all | solution.py:308
  78.4 9.3 %copy-start.5 = (bf16[8,48,2176]{2,1,0:T(8,128)(2,1)}, bf16[8,48,2176]{2,1,0:T(8,128)(2,1)S(1)}, u32[]{:S(2)}) copy-start(bf16[8,48,2176]{2,1,0:T(8,128)(2,1)S(1)} %get-tuple-element.85) | copy-start | bytes 5013508
  78.4 21.6 %copy-start.12 = (f32[2,1024]{1,0:T(2,128)S(1)}, f32[2,1024]{1,0:T(2,128)}, u32[]{:S(2)}) copy-start(f32[2,1024]{1,0:T(2,128)} %param.14) | copy-start | bytes 24580
  78.4 21.6 %copy-start.13 = (f32[2,1024]{1,0:T(2,128)S(1)}, f32[2,1024]{1,0:T(2,128)}, u32[]{:S(2)}) copy-start(f32[2,1024]{1,0:T(2,128)} %param.15) | copy-start | bytes 24580
  78.4 21.8 %copy-start.16 = (bf16[512,512]{1,0:T(8,128)(2,1)S(1)}, bf16[512,512]{1,0:T(8,128)(2,1)}, u32[]{:S(2)}) copy-start(bf16[512,512]{1,0:T(8,128)(2,1)} %get-tuple-element.86) | copy-start | bytes 1572868
  78.4 9.3 %collective-permute-start.7 = (bf16[48,2176]{1,0:T(8,128)(2,1)S(1)}, bf16[48,2176]{1,0:T(8,128)(2,1)S(1)}, u32[]{:S(2)}, u32[]{:S(2)}) collective-permute-start(bf16[48,2176]{1,0:T(8,128)(2,1)S(1)} %get-tuple-element.84), channel_id=1, source_target_pairs={{0,224},{32,0},{64,32},{96,64},{128,96},{160,128},{192,160},{224,1... | collective-permute-start | bytes 626696 | tf_op jit(solution)/shard_map/ppermute | solution.py:324
  84.4 7.1 %collective-permute-start.11 = (bf16[48,2176]{1,0:T(8,128)(2,1)S(1)}, bf16[48,2176]{1,0:T(8,128)(2,1)S(1)}, u32[]{:S(2)}, u32[]{:S(2)}) collective-permute-start(bf16[48,2176]{1,0:T(8,128)(2,1)S(1)} %get-tuple-element.112), channel_id=1, source_target_pairs={{0,32},{32,64},{64,96},{96,128},{128,160},{160,192},{192,224},{224... | collective-permute-start | bytes 626696 | tf_op jit(solution)/shard_map/ppermute | solution.py:330
  87.7 7.1 %collective-permute-start.8 = (bf16[48,2176]{1,0:T(8,128)(2,1)S(1)}, bf16[48,2176]{1,0:T(8,128)(2,1)S(1)}, u32[]{:S(2)}, u32[]{:S(2)}) collective-permute-start(bf16[48,2176]{1,0:T(8,128)(2,1)S(1)} %fusion.10), channel_id=1, source_target_pairs={{0,224},{32,0},{64,32},{96,64},{128,96},{160,128},{192,160},{224,1... | collective-permute-start | bytes 626696 | tf_op jit(solution)/shard_map/ppermute | solution.py:329
  96.0 7.5 %collective-permute-start.12 = (bf16[48,2176]{1,0:T(8,128)(2,1)S(1)}, bf16[48,2176]{1,0:T(8,128)(2,1)S(1)}, u32[]{:S(2)}, u32[]{:S(2)}) collective-permute-start(bf16[48,2176]{1,0:T(8,128)(2,1)S(1)} %get-tuple-element.115), channel_id=1, source_target_pairs={{0,32},{32,64},{64,96},{96,128},{128,160},{160,192},{192,224},{224... | collective-permute-start | bytes 626696 | tf_op jit(solution)/shard_map/ppermute | solution.py:330
  96.1 7.5 %collective-permute-start.9 = (bf16[48,2176]{1,0:T(8,128)(2,1)S(1)}, bf16[48,2176]{1,0:T(8,128)(2,1)S(1)}, u32[]{:S(2)}, u32[]{:S(2)}) collective-permute-start(bf16[48,2176]{1,0:T(8,128)(2,1)S(1)} %get-tuple-element.116), channel_id=1, source_target_pairs={{0,224},{32,0},{64,32},{96,64},{128,96},{160,128},{192,160},{224,1... | collective-permute-start | bytes 626696 | tf_op jit(solution)/shard_map/ppermute | solution.py:329
  100.1 8.2 %collective-permute-start.14 = (f32[2,2,512]{2,1,0:T(2,128)S(1)}, f32[2,2,512]{2,1,0:T(2,128)S(1)}, u32[]{:S(2)}, u32[]{:S(2)}) collective-permute-start(f32[2,2,512]{2,1,0:T(2,128)S(1)} %fusion.11), channel_id=1, source_target_pairs={{0,8},{8,0},{1,9},{9,1},{2,10},{10,2},{3,11},{11,3},{4,12},{12,4},... | collective-permute-start | bytes 24584 | tf_op jit(solution)/shard_map/ppermute | solution.py:30
  100.2 16.2 %collective-permute-start.15 = (bf16[512,512]{1,0:T(8,128)(2,1)S(1)}, bf16[512,512]{1,0:T(8,128)(2,1)}, u32[]{:S(2)}, u32[]{:S(2)}) collective-permute-start(bf16[512,512]{1,0:T(8,128)(2,1)S(1)} %copy-done.16), channel_id=1, source_target_pairs={{0,16},{16,0},{1,17},{17,1},{2,18},{18,2},{3,19},{19,3},{4,20},{20... | collective-permute-start | bytes 1572872 | tf_op jit(solution)/shard_map/ppermute | solution.py:30
  104.7 18.9 %copy-start = (bf16[512,1536]{1,0:T(8,128)(2,1)S(1)}, bf16[512,1536]{1,0:T(8,128)(2,1)}, u32[]{:S(2)}) copy-start(bf16[512,1536]{1,0:T(8,128)(2,1)} %get-tuple-element.96.refs_0_.mine) | copy-start | bytes 4718596
  104.7 6.9 %collective-permute-start.10 = (bf16[48,2176]{1,0:T(8,128)(2,1)S(1)}, bf16[48,2176]{1,0:T(8,128)(2,1)S(1)}, u32[]{:S(2)}, u32[]{:S(2)}) collective-permute-start(bf16[48,2176]{1,0:T(8,128)(2,1)S(1)} %get-tuple-element.114), channel_id=1, source_target_pairs={{0,224},{32,0},{64,32},{96,64},{128,96},{160,128},{192,160},{224,1... | collective-permute-start | bytes 626696 | tf_op jit(solution)/shard_map/ppermute | solution.py:329
  108.3 7.0 %collective-permute-start.13 = (bf16[48,2176]{1,0:T(8,128)(2,1)S(1)}, bf16[48,2176]{1,0:T(8,128)(2,1)S(1)}, u32[]{:S(2)}, u32[]{:S(2)}) collective-permute-start(bf16[48,2176]{1,0:T(8,128)(2,1)S(1)} %get-tuple-element.113), channel_id=1, source_target_pairs={{0,32},{32,64},{64,96},{96,128},{128,160},{160,192},{192,224},{224... | collective-permute-start | bytes 626696 | tf_op jit(solution)/shard_map/ppermute | solution.py:330
  116.4 27.6 %all-to-all-start.3 = ((bf16[8,48,1024]{2,1,0:T(8,128)(2,1)}), bf16[8,48,1024]{2,1,0:T(8,128)(2,1)}, u32[]{:S(2)}, u32[]{:S(2)}) async-start(bf16[8,48,1024]{2,1,0:T(8,128)(2,1)} %shard_map.97), calls=%async_computation.3 | async-start | bytes 1572864 | tf_op jit(solution)/shard_map/all_to_all | solution.py:308
  120.6 23.4 %collective-permute-start.16 = (bf16[512,1024]{1,0:T(8,128)(2,1)}, bf16[512,1024]{1,0:T(8,128)(2,1)}, u32[]{:S(2)}, u32[]{:S(2)}) collective-permute-start(bf16[512,1024]{1,0:T(8,128)(2,1)} %get-tuple-element.89), channel_id=1, source_target_pairs={{0,16},{16,0},{1,17},{17,1},{2,18},{18,2},{3,19},{19,3},{4,20},{20... | collective-permute-start | bytes 3145736 | tf_op jit(solution)/shard_map/ppermute | solution.py:30
  123.5 20.5 %collective-permute-start.17 = (bf16[512,512]{1,0:T(8,128)(2,1)}, bf16[512,512]{1,0:T(8,128)(2,1)}, u32[]{:S(2)}, u32[]{:S(2)}) collective-permute-start(bf16[512,512]{1,0:T(8,128)(2,1)} %collective-permute-done.15.got), channel_id=1, source_target_pairs={{0,8},{8,0},{1,9},{9,1},{2,10},{10,2},{3,11},{11,3},{4,12},{12,4},... | collective-permute-start | bytes 1572872 | tf_op jit(solution)/shard_map/ppermute | solution.py:30
  123.5 47.0 %collective-permute-start.18 = (bf16[512,1536]{1,0:T(8,128)(2,1)S(1)}, bf16[512,1536]{1,0:T(8,128)(2,1)S(1)}, u32[]{:S(2)}, u32[]{:S(2)}) collective-permute-start(bf16[512,1536]{1,0:T(8,128)(2,1)S(1)} %copy-done), channel_id=1, source_target_pairs={{0,8},{8,0},{1,9},{9,1},{2,10},{10,2},{3,11},{11,3},{4,12},{12,4},... | collective-permute-start | bytes 4718600 | tf_op jit(solution)/shard_map/ppermute | solution.py:30
  147.4 15.4 %all-to-all-start.4 = ((bf16[16,48,512]{2,1,0:T(8,128)(2,1)}), bf16[16,48,512]{2,1,0:T(8,128)(2,1)}, u32[]{:S(2)}, u32[]{:S(2)}) async-start(bf16[16,48,512]{2,1,0:T(8,128)(2,1)} %bitcast.64), calls=%async_computation.4 | async-start | bytes 1572864 | tf_op jit(solution)/shard_map/all_to_all | solution.py:308
  153.0 17.5 %collective-permute-start.19 = (bf16[512,1024]{1,0:T(8,128)(2,1)}, bf16[512,1024]{1,0:T(8,128)(2,1)}, u32[]{:S(2)}, u32[]{:S(2)}) collective-permute-start(bf16[512,1024]{1,0:T(8,128)(2,1)} %collective-permute-done.16.refs_1_), channel_id=1, source_target_pairs={{0,8},{8,0},{1,9},{9,1},{2,10},{10,2},{3,11},{11,3},{4,12},{12,4},... | collective-permute-start | bytes 3145736 | tf_op jit(solution)/shard_map/ppermute | solution.py:30
  165.1 15.3 %all-to-all-start.5 = ((bf16[16,48,512]{2,1,0:T(8,128)(2,1)}), bf16[16,48,512]{2,1,0:T(8,128)(2,1)}, u32[]{:S(2)}, u32[]{:S(2)}) async-start(bf16[16,48,512]{2,1,0:T(8,128)(2,1)} %get-tuple-element.93), calls=%async_computation.5 | async-start | bytes 1572864 | tf_op jit(solution)/shard_map/all_to_all | solution.py:308
  170.5 14.4 %copy-start.3 = (bf16[512,1536]{1,0:T(8,128)(2,1)}, bf16[512,1536]{1,0:T(8,128)(2,1)S(1)}, u32[]{:S(2)}) copy-start(bf16[512,1536]{1,0:T(8,128)(2,1)S(1)} %collective-permute-done.18.refs_2_.mine_sib) | copy-start | bytes 4718596
  185.0 18.8 %copy-start.15 = (bf16[512,512]{1,0:T(8,128)(2,1)S(1)}, bf16[512,512]{1,0:T(8,128)(2,1)}, u32[]{:S(2)}) copy-start(bf16[512,512]{1,0:T(8,128)(2,1)} %get-tuple-element.101) | copy-start | bytes 1572868
  185.0 7.2 %collective-permute-start.20 = (bf16[48,2176]{1,0:T(8,128)(2,1)S(1)}, bf16[48,2176]{1,0:T(8,128)(2,1)S(1)}, u32[]{:S(2)}, u32[]{:S(2)}) collective-permute-start(bf16[48,2176]{1,0:T(8,128)(2,1)S(1)} %get-tuple-element.99), channel_id=1, source_target_pairs={{0,224},{32,0},{64,32},{96,64},{128,96},{160,128},{192,160},{224,1... | collective-permute-start | bytes 626696 | tf_op jit(solution)/shard_map/ppermute | solution.py:324
  188.0 8.0 %collective-permute-start.24 = (bf16[48,2176]{1,0:T(8,128)(2,1)S(1)}, bf16[48,2176]{1,0:T(8,128)(2,1)S(1)}, u32[]{:S(2)}, u32[]{:S(2)}) collective-permute-start(bf16[48,2176]{1,0:T(8,128)(2,1)S(1)} %get-tuple-element.106), channel_id=1, source_target_pairs={{0,32},{32,64},{64,96},{96,128},{128,160},{160,192},{192,224},{224... | collective-permute-start | bytes 626696 | tf_op jit(solution)/shard_map/ppermute | solution.py:330
  192.2 7.4 %collective-permute-start.21 = (bf16[48,2176]{1,0:T(8,128)(2,1)S(1)}, bf16[48,2176]{1,0:T(8,128)(2,1)S(1)}, u32[]{:S(2)}, u32[]{:S(2)}) collective-permute-start(bf16[48,2176]{1,0:T(8,128)(2,1)S(1)} %fusion.5), channel_id=1, source_target_pairs={{0,224},{32,0},{64,32},{96,64},{128,96},{160,128},{192,160},{224,1... | collective-permute-start | bytes 626696 | tf_op jit(solution)/shard_map/ppermute | solution.py:329
  199.7 9.7 %collective-permute-start.25 = (bf16[48,2176]{1,0:T(8,128)(2,1)S(1)}, bf16[48,2176]{1,0:T(8,128)(2,1)S(1)}, u32[]{:S(2)}, u32[]{:S(2)}) collective-permute-start(bf16[48,2176]{1,0:T(8,128)(2,1)S(1)} %get-tuple-element.109), channel_id=1, source_target_pairs={{0,32},{32,64},{64,96},{96,128},{128,160},{160,192},{192,224},{224... | collective-permute-start | bytes 626696 | tf_op jit(solution)/shard_map/ppermute | solution.py:330
  200.3 9.1 %collective-permute-start.22 = (bf16[48,2176]{1,0:T(8,128)(2,1)S(1)}, bf16[48,2176]{1,0:T(8,128)(2,1)S(1)}, u32[]{:S(2)}, u32[]{:S(2)}) collective-permute-start(bf16[48,2176]{1,0:T(8,128)(2,1)S(1)} %get-tuple-element.110), channel_id=1, source_target_pairs={{0,224},{32,0},{64,32},{96,64},{128,96},{160,128},{192,160},{224,1... | collective-permute-start | bytes 626696 | tf_op jit(solution)/shard_map/ppermute | solution.py:329
  203.8 15.4 %collective-permute-start.27 = (bf16[512,512]{1,0:T(8,128)(2,1)S(1)}, bf16[512,512]{1,0:T(8,128)(2,1)S(1)}, u32[]{:S(2)}, u32[]{:S(2)}) collective-permute-start(bf16[512,512]{1,0:T(8,128)(2,1)S(1)} %copy-done.15), channel_id=1, source_target_pairs={{0,16},{16,0},{1,17},{17,1},{2,18},{18,2},{3,19},{19,3},{4,20},{20... | collective-permute-start | bytes 1572872 | tf_op jit(solution)/shard_map/ppermute | solution.py:30
  209.5 5.9 %collective-permute-start.23 = (bf16[48,2176]{1,0:T(8,128)(2,1)S(1)}, bf16[48,2176]{1,0:T(8,128)(2,1)S(1)}, u32[]{:S(2)}, u32[]{:S(2)}) collective-permute-start(bf16[48,2176]{1,0:T(8,128)(2,1)S(1)} %get-tuple-element.108), channel_id=1, source_target_pairs={{0,224},{32,0},{64,32},{96,64},{128,96},{160,128},{192,160},{224,1... | collective-permute-start | bytes 626696 | tf_op jit(solution)/shard_map/ppermute | solution.py:329
  211.0 7.0 %collective-permute-start.26 = (bf16[48,2176]{1,0:T(8,128)(2,1)S(1)}, bf16[48,2176]{1,0:T(8,128)(2,1)S(1)}, u32[]{:S(2)}, u32[]{:S(2)}) collective-permute-start(bf16[48,2176]{1,0:T(8,128)(2,1)S(1)} %get-tuple-element.107), channel_id=1, source_target_pairs={{0,32},{32,64},{64,96},{96,128},{128,160},{160,192},{192,224},{224... | collective-permute-start | bytes 626696 | tf_op jit(solution)/shard_map/ppermute | solution.py:330
  219.1 20.6 %copy-start.8 = (bf16[512,512]{1,0:T(8,128)(2,1)}, bf16[512,512]{1,0:T(8,128)(2,1)S(1)}, u32[]{:S(2)}) copy-start(bf16[512,512]{1,0:T(8,128)(2,1)S(1)} %collective-permute-done.27.got) | copy-start | bytes 1572868
  219.1 20.6 %all-to-all-start.6 = ((bf16[8,48,1024]{2,1,0:T(8,128)(2,1)}), bf16[8,48,1024]{2,1,0:T(8,128)(2,1)S(1)}, u32[]{:S(2)}, u32[]{:S(2)}) async-start(bf16[8,48,1024]{2,1,0:T(8,128)(2,1)} %shard_map.101), calls=%async_computation.6 | async-start | bytes 1572864 | tf_op jit(solution)/shard_map/all_to_all | solution.py:308
  223.6 1.9 collective-permute-start.28
  225.5 14.2 %copy-start.9 = (bf16[512,512]{1,0:T(8,128)(2,1)}, bf16[512,512]{1,0:T(8,128)(2,1)S(1)}, u32[]{:S(2)}) copy-start(bf16[512,512]{1,0:T(8,128)(2,1)S(1)} %collective-permute-done.28.got_sib) | copy-start | bytes 1572868
  (5 other events, 7.6 us)
